TPU v7x, 32 devices: a whole 2x2x4 slice. The times are simulated.
32 devices in a mesh: clip: 4 (over z), seq: 8 (over y, x, core).
Axes of the slice: x: 2, y: 2, z: 4, core: 2. Of those that a mesh axis runs over, the one named last changes fastest.
Arguments:
- query_in: bfloat16 [4096, 4096], P(('clip', 'seq')), parts along dimension 0, may hold values from -12 to 12
- key_in: bfloat16 [4096, 4096], P(('clip', 'seq')), parts along dimension 0, may hold values from -12 to 12
- value_in: bfloat16 [4096, 4096], P(('clip', 'seq')), parts along dimension 0, may hold values from -6 to 6
- grad_out: bfloat16 [4096, 4096], P(('clip', 'seq')), parts along dimension 0, may hold values from -6 to 6
- positions: int32 [3, 4096], P(None, 'clip'), parts along dimension 1, may hold values from 0 to 15, as said below
- block_flags: int32 [32, 8], P('clip'), parts along dimension 0, may hold values from 0 to 1, as said below
- band_ids: int32 [32, 8], P('clip'), parts along dimension 0, may hold values from 0 to 3, as said below
Outputs:
- attn_out: bfloat16 [4096, 4096], P(('clip', 'seq')), parts along dimension 0
- grad_query: bfloat16 [4096, 4096], P(('clip', 'seq')), parts along dimension 0
- grad_key: bfloat16 [4096, 4096], P(('clip', 'seq')), parts along dimension 0
- grad_value: bfloat16 [4096, 4096], P(('clip', 'seq')), parts along dimension 0
There are 4 independent parts, one for each index of `clip`. A program takes and returns all parts, laid end to end along the dimension named above; each array names one. Nothing has to cross between parts.
Inputs may be any that keep to these rules, and one draw needn't show every extreme that they name: positions[0] is the latent frame of a token: tokens come in frames of 256, frame numbers rise strictly from frame to frame and may skip, and the last frame's number is 7; positions[1] and positions[2] are row and column in a square crop, row-major. `block_flags`: diagonal block pairs are always 1. `band_ids`: diagonal block pairs are 0.
All inputs are finite; a program needn't handle non-finite values.
Results may differ from a plain program's by a relative error of at most 0.015.
Values may be sent and summed in bfloat16 or wider, within the bound.
No kernel may reach another device: no remote copies, remote signals or barrier semaphores. Data moves between devices by JAX's collectives and lax.ppermute only.
A program may use at most 128 MiB of HBM per device.

v0:
```python
import functools
import math

import jax
import jax.numpy as jnp
from jax import lax
from jax.experimental import pallas as pl
from jax.experimental.pallas import tpu as pltpu
from jax.sharding import PartitionSpec as P

H = 32
DH = 128
BLK = 128
NTK = 2.0
CHUNKS = 2

F32 = jnp.float32
BF16 = jnp.bfloat16
NEG_INF = float("-inf")


def rope_tables(positions):
    third = 2 * (DH // 6)
    part_dims = (DH - 2 * third, third, third)
    pieces = []
    for axis_num, dim in enumerate(part_dims):
        base = 10000.0 * NTK ** (dim / (dim - 2.0))
        pair = (jnp.arange(dim, dtype=jnp.int32) // 2).astype(F32)
        inverse = jnp.exp(pair * (-2.0 * math.log(base) / dim))
        pieces.append(positions[axis_num].astype(F32)[:, None] * inverse[None, :])
    angle = jnp.concatenate(pieces, 1)
    sign = jnp.where(jnp.arange(DH, dtype=jnp.int32) % 2 == 0, -1.0, 1.0).astype(F32)
    return jnp.cos(angle), jnp.sin(angle) * sign[None, :]


def pack_kernel(groups, heads, first, count, me_ref, q_ref, k_ref, v_ref, g_ref, *rest):
    outs, sems = rest[:groups], rest[groups]
    me = me_ref[0]
    copies = []
    for d in range(groups):
        start = pl.multiple_of(((me ^ d) * heads + first) * DH, DH)
        for a, ref in enumerate((q_ref, k_ref, v_ref, g_ref)):
            copies.append(
                pltpu.make_async_copy(
                    ref.at[:, pl.ds(start, count * DH)], outs[d].at[a], sems.at[d, a]
                )
            )
    for copy in copies:
        copy.start()
    for copy in copies:
        copy.wait()


def unpack_kernel(groups, heads, first, count, kept, me_ref, *rest):
    pieces = rest[:groups]
    outs = rest[groups + kept : groups + kept + 4]
    sems = rest[groups + kept + 4]
    me = me_ref[0]
    copies = []
    for d in range(groups):
        start = pl.multiple_of(((me ^ d) * heads + first) * DH, DH)
        for a in range(4):
            copies.append(
                pltpu.make_async_copy(
                    pieces[d].at[a], outs[a].at[:, pl.ds(start, count * DH)], sems.at[d, a]
                )
            )
    for copy in copies:
        copy.start()
    for copy in copies:
        copy.wait()


def dot(x, y):
    return jnp.dot(x, y, preferred_element_type=F32)


def dot_t(x, y):
    return lax.dot_general(x, y, (((1,), (1,)), ((), ())), preferred_element_type=F32)


def attention_kernel(groups, rows, count, width, me_ref, flags_ref, bands_ref, cos_ref, sin_ref, *rest):
    ins, outs = rest[:groups], rest[groups : 2 * groups]
    qr, kr, vs, gs, kt, vt, gt, scores, low, ds, dk, dv, os, dqs = rest[2 * groups :]
    total = groups * rows
    per_piece = rows // BLK
    blocks = total // BLK
    scale = 1.0 / math.sqrt(DH)
    score_factor = scale / math.log(2.0)
    me = me_ref[0]

    even = lax.broadcasted_iota(jnp.int32, (rows, DH), 1) % 2 == 0
    apart = jnp.abs(
        lax.broadcasted_iota(jnp.int32, (BLK, BLK), 0) - lax.broadcasted_iota(jnp.int32, (BLK, BLK), 1)
    )

    def turn(x, cos, sin):
        partner = jnp.where(even, pltpu.roll(x, DH - 1, 1), pltpu.roll(x, 1, 1))
        return x * cos + partner * sin

    def table_rows(d):
        return pl.ds(pl.multiple_of((me ^ d) * rows, rows), rows)

    def block_of(b):
        return (me ^ (b // per_piece)) * per_piece + b % per_piece

    def one_head(h, carry):
        cols = pl.ds(pl.multiple_of(h * DH, DH), DH)
        for d in range(groups):
            at = slice(d * rows, (d + 1) * rows)
            cos, sin = cos_ref[table_rows(d), :], sin_ref[table_rows(d), :]
            qr[at, :] = turn(ins[d][0, :, cols].astype(F32), cos, sin).astype(BF16)
            key = turn(ins[d][1, :, cols].astype(F32), cos, sin).astype(BF16)
            kr[at, :] = key
            kt[:, at] = key.T
            value = ins[d][2, :, cols]
            vs[at, :] = value
            vt[:, at] = value.T
            grad = ins[d][3, :, cols]
            gs[at, :] = grad
            gt[:, at] = grad.T
        dk[...] = jnp.zeros_like(dk)
        dv[...] = jnp.zeros_like(dv)

        def one_step(i, carry):
            mine = pl.ds(pl.multiple_of(i * width, width), width)
            query, grad = qr[mine, :], gs[mine, :]
            top = jnp.full((8, width), NEG_INF, F32)
            for j in range(blocks):
                at = slice(j * BLK, (j + 1) * BLK)
                raw = dot_t(kr[at, :], query) * score_factor
                parts = []
                for w in range(width // BLK):
                    row, col = block_of(i * (width // BLK) + w), block_of(j)
                    reach = jnp.where(
                        flags_ref[row, col] == 1, jnp.right_shift(BLK, bands_ref[row, col]), 0
                    )
                    parts.append(jnp.where(apart < reach, raw[:, w * BLK : (w + 1) * BLK], NEG_INF))
                part = jnp.concatenate(parts, 1)
                scores[at, :] = part
                top = jnp.maximum(top, jnp.max(part.reshape(BLK // 8, 8, width), axis=0))
            largest = jnp.max(top, axis=0, keepdims=True)
            norm = jnp.zeros((8, width), F32)
            for j in range(blocks):
                at = slice(j * BLK, (j + 1) * BLK)
                weights = jnp.exp2(scores[at, :] - largest)
                scores[at, :] = weights
                norm = norm + jnp.sum(weights.reshape(BLK // 8, 8, width), axis=0)
            inverse = 1.0 / jnp.sum(norm, axis=0, keepdims=True)
            for j in range(blocks):
                at = slice(j * BLK, (j + 1) * BLK)
                probs = scores[at, :] * inverse
                scores[at, :] = probs
                low[at, :] = probs.astype(BF16)
            out_t = dot(vt[...], low[...]).astype(BF16).astype(F32)
            delta = jnp.sum(out_t * gt[:, mine].astype(F32), axis=0, keepdims=True)
            os[mine, :] = out_t.T.astype(BF16)
            for j in range(blocks):
                at = slice(j * BLK, (j + 1) * BLK)
                grad_probs = dot_t(vs[at, :], grad)
                ds[at, :] = (scores[at, :] * (grad_probs - delta)).astype(BF16)
            dqs[mine, :] = dot(kt[...], ds[...]).T
            dv[...] += dot(low[...], grad)
            dk[...] += dot(ds[...], query)
            return carry

        lax.fori_loop(0, total // width, one_step, 0)
        for d in range(groups):
            at = slice(d * rows, (d + 1) * rows)
            cos, sin = cos_ref[table_rows(d), :] * scale, sin_ref[table_rows(d), :] * -scale
            outs[d][0, :, cols] = os[at, :]
            outs[d][1, :, cols] = turn(dqs[at, :], cos, sin).astype(BF16)
            outs[d][2, :, cols] = turn(dk[at, :], cos, sin).astype(BF16)
            outs[d][3, :, cols] = dv[at, :].astype(BF16)
        return carry

    lax.fori_loop(0, count, one_head, 0)


SMEM = pl.BlockSpec(memory_space=pltpu.SMEM)
VMEM = pl.BlockSpec(memory_space=pltpu.VMEM)
ANY = pl.BlockSpec(memory_space=pl.ANY)


def body(query_in, key_in, value_in, grad_out, positions, block_flags, band_ids):
    groups = lax.axis_size("seq")
    rows, channels = query_in.shape
    heads = channels // DH // groups
    total = groups * rows
    chunks = math.gcd(CHUNKS, heads)
    count = heads // chunks
    width = 2 * BLK if total % (2 * BLK) == 0 else BLK
    me = lax.axis_index("seq").astype(jnp.int32).reshape(1)
    arrays = (query_in, key_in, value_in, grad_out)
    piece = jax.ShapeDtypeStruct((4, rows, count * DH), BF16)
    pairs = [[(i, i ^ d) for i in range(groups)] for d in range(groups)]
    limit = 40 * 1024 * 1024

    def exchange(pieces):
        return [pieces[0]] + [
            lax.ppermute(pieces[d], "seq", pairs[d]) for d in range(1, groups)
        ]

    def pack(c):
        return pl.pallas_call(
            functools.partial(pack_kernel, groups, heads, c * count, count),
            out_shape=[piece] * groups,
            in_specs=[SMEM] + [ANY] * 4,
            out_specs=[VMEM] * groups,
            scratch_shapes=[pltpu.SemaphoreType.DMA((groups, 4))],
            name=f"pack_{c}",
        )(me, *arrays)

    def attention(pieces, cos, sin):
        area = total * total
        return pl.pallas_call(
            functools.partial(attention_kernel, groups, rows, count, width),
            out_shape=[piece] * groups,
            in_specs=[SMEM] * 3 + [VMEM] * (2 + groups),
            out_specs=[VMEM] * groups,
            scratch_shapes=[pltpu.VMEM((total, DH), BF16)] * 4
            + [pltpu.VMEM((DH, total), BF16)] * 3
            + [pltpu.VMEM((total, width), F32)]
            + [pltpu.VMEM((total, width), BF16)] * 2
            + [pltpu.VMEM((total, DH), F32)] * 2
            + [pltpu.VMEM((total, DH), BF16), pltpu.VMEM((total, DH), F32)],
            compiler_params=pltpu.CompilerParams(vmem_limit_bytes=limit),
            cost_estimate=pl.CostEstimate(
                flops=10 * count * area * DH,
                bytes_accessed=16 * total * count * DH,
                transcendentals=count * area,
            ),
            name="attention",
        )(me, block_flags, band_ids, cos, sin, *pieces)

    def unpack(c, pieces, before):
        kept = len(before)
        return pl.pallas_call(
            functools.partial(unpack_kernel, groups, heads, c * count, count, kept),
            out_shape=[jax.ShapeDtypeStruct((rows, channels), BF16)] * 4,
            in_specs=[SMEM] + [VMEM] * groups + [ANY] * kept,
            out_specs=[ANY] * 4,
            input_output_aliases={1 + groups + a: a for a in range(kept)},
            scratch_shapes=[pltpu.SemaphoreType.DMA((groups, 4))],
            name=f"unpack_{c}",
        )(me, *pieces, *before)

    cos, sin = rope_tables(positions)
    arrived = [exchange(pack(c)) for c in range(chunks)]
    results = ()
    for c in range(chunks):
        results = unpack(c, exchange(attention(arrived[c], cos, sin)), results)
    return tuple(results)


def solution(mesh):
    tokens = P(("clip", "seq"), None)
    return jax.shard_map(
        body,
        mesh=mesh,
        in_specs=(tokens, tokens, tokens, tokens, P(None, "clip"), P("clip", None), P("clip", None)),
        out_specs=(tokens, tokens, tokens, tokens),
        check_vma=False,
    )
```

profile of v0, /device:TPU:0, one launch (start us, length us, event | category | flops | bytes accessed | tf_op | source)
XLA Modules:
  0.0 117.0 jit_solution(1183527023305317558)
XLA Ops:
  0.6 3.2 %pack_0.1 = (bf16[4,128,256]{2,1,0:T(8,128)(2,1)}, bf16[4,128,256]{2,1,0:T(8,128)(2,1)}, bf16[4,128,256]{2,1,0:T(8,128)(2,1)}, bf16[4,128,256]{2,1,0:T(8,128)(2,...) custom-call(s32[1]{0:T(128)} %bitcast.me_ref, ...), custom_call_target="tpu_custom_call" | custom-call | tf_op jit(solution)/shard_map/pack_0/pallas_call | solution.py:205
  3.8 0.5 collective-permute-start.14
  4.3 2.6 %collective-permute-start.15 = (bf16[4,128,256]{2,1,0:T(8,128)(2,1)}, bf16[4,128,256]{2,1,0:T(8,128)(2,1)S(1)}, u32[]{:S(2)}, u32[]{:S(2)}) collective-permute-start(bf16[4,128,256]{2,1,0:T(8,128)(2,1)} %get-tuple-element.58), channel_id=1, source_target_pairs={{0,2},{1,3},{2,0},{3,1},{4,6},{5,7},{6,4},{7,5},{8,10},{9,11},{10,... | collective-permute-start | bytes 786440 | tf_op jit(solution)/shard_map/ppermute | solution.py:201
  6.9 0.1 collective-permute-start.16
  7.0 1.8 %collective-permute-start.17 = (bf16[4,128,256]{2,1,0:T(8,128)(2,1)}, bf16[4,128,256]{2,1,0:T(8,128)(2,1)S(1)}, u32[]{:S(2)}, u32[]{:S(2)}) collective-permute-start(bf16[4,128,256]{2,1,0:T(8,128)(2,1)} %get-tuple-element.60), channel_id=1, source_target_pairs={{0,4},{1,5},{2,6},{3,7},{4,0},{5,1},{6,2},{7,3},{8,12},{9,13},{10,... | collective-permute-start | bytes 786440 | tf_op jit(solution)/shard_map/ppermute | solution.py:201
  8.7 0.0 collective-permute-start.18
  8.8 0.3 broadcast_multiply_fusion.1
  9.2 3.3 %pack_1.1 = (bf16[4,128,256]{2,1,0:T(8,128)(2,1)}, bf16[4,128,256]{2,1,0:T(8,128)(2,1)}, bf16[4,128,256]{2,1,0:T(8,128)(2,1)}, bf16[4,128,256]{2,1,0:T(8,128)(2,...) custom-call(s32[1]{0:T(128)} %bitcast.me_ref, ...), custom_call_target="tpu_custom_call" | custom-call | tf_op jit(solution)/shard_map/pack_1/pallas_call | solution.py:205
  12.4 0.0 collective-permute-done.14.rest_1_
  12.4 2.7 %collective-permute-start.19 = (bf16[4,128,256]{2,1,0:T(8,128)(2,1)S(1)}, bf16[4,128,256]{2,1,0:T(8,128)(2,1)S(1)}, u32[]{:S(2)}, u32[]{:S(2)}) collective-permute-start(bf16[4,128,256]{2,1,0:T(8,128)(2,1)S(1)} %copy-done.21), channel_id=1, source_target_pairs={{0,6},{1,7},{2,4},{3,5},{4,2},{5,3},{6,0},{7,1},{8,14},{9,15},{10,... | collective-permute-start | bytes 786440 | tf_op jit(solution)/shard_map/ppermute | solution.py:201
  15.1 0.0 collective-permute-done.15.rest_2_
  15.1 0.9 collective-permute-start.20
  16.0 3.5 %collective-permute-done.16.rest_3_ = bf16[4,128,256]{2,1,0:T(8,128)(2,1)S(1)} collective-permute-done((bf16[4,128,256]{2,1,0:T(8,128)(2,1)}, bf16[4,128,256]{2,1,0:T(8,128)(2,1)S(1)}, u32[]{:S(2)}, u32[]{:S(2)}) %collective-permute-start.16) | collective-permute-done | bytes 262176 | tf_op jit(solution)/shard_map/ppermute | solution.py:201
  19.5 0.5 collective-permute-start
  20.0 0.2 broadcast_multiply_fusion.2
  20.2 0.0 collective-permute-done.17.rest_4_
  20.2 2.0 %collective-permute-start.1 = (bf16[4,128,256]{2,1,0:T(8,128)(2,1)}, bf16[4,128,256]{2,1,0:T(8,128)(2,1)S(1)}, u32[]{:S(2)}, u32[]{:S(2)}) collective-permute-start(bf16[4,128,256]{2,1,0:T(8,128)(2,1)} %get-tuple-element.42), channel_id=1, source_target_pairs={{0,2},{1,3},{2,0},{3,1},{4,6},{5,7},{6,4},{7,5},{8,10},{9,11},{10,... | collective-permute-start | bytes 786440 | tf_op jit(solution)/shard_map/ppermute | solution.py:201
  22.2 9.7 %collective-permute-done.18.rest_5_ = bf16[4,128,256]{2,1,0:T(8,128)(2,1)S(1)} collective-permute-done((bf16[4,128,256]{2,1,0:T(8,128)(2,1)}, bf16[4,128,256]{2,1,0:T(8,128)(2,1)S(1)}, u32[]{:S(2)}, u32[]{:S(2)}) %collective-permute-start.18) | collective-permute-done | bytes 262176 | tf_op jit(solution)/shard_map/ppermute | solution.py:201
  32.0 2.1 %collective-permute-start.2 = (bf16[4,128,256]{2,1,0:T(8,128)(2,1)}, bf16[4,128,256]{2,1,0:T(8,128)(2,1)S(1)}, u32[]{:S(2)}, u32[]{:S(2)}) collective-permute-start(bf16[4,128,256]{2,1,0:T(8,128)(2,1)} %get-tuple-element.43), channel_id=1, source_target_pairs={{0,3},{1,2},{2,1},{3,0},{4,7},{5,6},{6,5},{7,4},{8,11},{9,10},{10,... | collective-permute-start | bytes 786440 | tf_op jit(solution)/shard_map/ppermute | solution.py:201
  34.0 0.0 collective-permute-done.19.rest_6_
  34.0 1.5 %collective-permute-start.3 = (bf16[4,128,256]{2,1,0:T(8,128)(2,1)}, bf16[4,128,256]{2,1,0:T(8,128)(2,1)S(1)}, u32[]{:S(2)}, u32[]{:S(2)}) collective-permute-start(bf16[4,128,256]{2,1,0:T(8,128)(2,1)} %get-tuple-element.44), channel_id=1, source_target_pairs={{0,4},{1,5},{2,6},{3,7},{4,0},{5,1},{6,2},{7,3},{8,12},{9,13},{10,... | collective-permute-start | bytes 786440 | tf_op jit(solution)/shard_map/ppermute | solution.py:201
  35.6 0.0 collective-permute-done.20.rest_7_
  35.6 0.0 collective-permute-start.4
  35.6 0.0 collective-permute-done.rest_1_
  35.6 1.2 collective-permute-start.5
  36.8 2.3 %sine_multiply_fusion = (f32[1024,128]{1,0:T(8,128)S(1)}, f32[1024,128]{1,0:T(8,128)S(1)}) fusion(f32[128]{0:T(128)S(1)} %compare_select_fusion, f32[1024,42]{1,0:T(8,128)S(1)} %get-tuple-element.82, f32[1024,42]{1,0:T(8,128)S(1)} %get-tuple-element.81, f32[1024,44]{1,0:T(8,128)S(1)} %broadcast_multiply_fusion.2), kind=kLoop, calls=%fused_computation.1 | loop fusion | flops 393216 | bytes 1573376 | tf_op jit(solution)/shard_map/mul | solution.py:33
  39.1 0.0 copy-start.4
  39.1 0.0 collective-permute-done.1.rest_2_
  39.1 1.8 %collective-permute-start.6 = (bf16[4,128,256]{2,1,0:T(8,128)(2,1)S(1)}, bf16[4,128,256]{2,1,0:T(8,128)(2,1)S(1)}, u32[]{:S(2)}, u32[]{:S(2)}) collective-permute-start(bf16[4,128,256]{2,1,0:T(8,128)(2,1)S(1)} %copy-done.17), channel_id=1, source_target_pairs={{0,7},{1,6},{2,5},{3,4},{4,3},{5,2},{6,1},{7,0},{8,15},{9,14},{10,... | collective-permute-start | bytes 786440 | tf_op jit(solution)/shard_map/ppermute | solution.py:201
  40.9 14.9 %attention.3 = (bf16[4,128,256]{2,1,0:T(8,128)(2,1)S(1)}, bf16[4,128,256]{2,1,0:T(8,128)(2,1)S(1)}, bf16[4,128,256]{2,1,0:T(8,128)(2,1)S(1)}, bf16[4,128,256]{2,...) custom-call(s32[1]{0:T(128)} %bitcast.me_ref, ...), custom_call_target="tpu_custom_call" | custom-call | flops 2684354560 | bytes 4194304 | tf_op jit(solution)/shard_map/attention/pallas_call | solution.py:216
  55.8 0.7 copy-done
  56.5 0.0 collective-permute-done.2.rest_3_
  56.5 0.2 collective-permute-start.21
  56.7 0.0 collective-permute-done.3.rest_4_
  56.7 0.8 collective-permute-start.22
  57.5 0.7 collective-permute-done.4.rest_5_
  58.2 1.0 collective-permute-start.23
  59.1 0.0 collective-permute-done.5.rest_6_
  59.1 1.5 %collective-permute-start.24 = (bf16[4,128,256]{2,1,0:T(8,128)(2,1)S(1)}, bf16[4,128,256]{2,1,0:T(8,128)(2,1)S(1)}, u32[]{:S(2)}, u32[]{:S(2)}) collective-permute-start(bf16[4,128,256]{2,1,0:T(8,128)(2,1)S(1)} %get-tuple-element.68), channel_id=1, source_target_pairs={{0,4},{1,5},{2,6},{3,7},{4,0},{5,1},{6,2},{7,3},{8,12},{9,13},{10,... | collective-permute-start | bytes 786440 | tf_op jit(solution)/shard_map/ppermute | solution.py:201
  60.7 14.8 %attention.2 = (bf16[4,128,256]{2,1,0:T(8,128)(2,1)S(1)}, bf16[4,128,256]{2,1,0:T(8,128)(2,1)S(1)}, bf16[4,128,256]{2,1,0:T(8,128)(2,1)S(1)}, bf16[4,128,256]{2,...) custom-call(s32[1]{0:T(128)} %bitcast.me_ref, ...), custom_call_target="tpu_custom_call" | custom-call | flops 2684354560 | bytes 4194304 | tf_op jit(solution)/shard_map/attention/pallas_call | solution.py:216
  75.5 0.7 copy-done.1
  76.2 0.0 collective-permute-done.21.rest_1_
  76.2 1.7 %collective-permute-start.26 = (bf16[4,128,256]{2,1,0:T(8,128)(2,1)S(1)}, bf16[4,128,256]{2,1,0:T(8,128)(2,1)S(1)}, u32[]{:S(2)}, u32[]{:S(2)}) collective-permute-start(bf16[4,128,256]{2,1,0:T(8,128)(2,1)S(1)} %get-tuple-element.70), channel_id=1, source_target_pairs={{0,6},{1,7},{2,4},{3,5},{4,2},{5,3},{6,0},{7,1},{8,14},{9,15},{10,... | collective-permute-start | bytes 786440 | tf_op jit(solution)/shard_map/ppermute | solution.py:201
  78.0 1.1 collective-permute-start.27
  79.1 0.0 collective-permute-done.23.rest_3_
  79.1 0.2 collective-permute-start.7
  79.3 1.5 %collective-permute-start.8 = (bf16[4,128,256]{2,1,0:T(8,128)(2,1)S(1)}, bf16[4,128,256]{2,1,0:T(8,128)(2,1)S(1)}, u32[]{:S(2)}, u32[]{:S(2)}) collective-permute-start(bf16[4,128,256]{2,1,0:T(8,128)(2,1)S(1)} %get-tuple-element.50), channel_id=1, source_target_pairs={{0,2},{1,3},{2,0},{3,1},{4,6},{5,7},{6,4},{7,5},{8,10},{9,11},{10,... | collective-permute-start | bytes 786440 | tf_op jit(solution)/shard_map/ppermute | solution.py:201
  80.7 0.0 collective-permute-done.25.rest_5_
  80.8 0.2 collective-permute-start.9
  81.0 5.3 %collective-permute-done.26.rest_6_ = bf16[4,128,256]{2,1,0:T(8,128)(2,1)S(1)} collective-permute-done((bf16[4,128,256]{2,1,0:T(8,128)(2,1)S(1)}, bf16[4,128,256]{2,1,0:T(8,128)(2,1)S(1)}, u32[]{:S(2)}, u32[]{:S(2)}) %collective-permute-start.26) | collective-permute-done | bytes 262176 | tf_op jit(solution)/shard_map/ppermute | solution.py:201
  86.2 1.2 %collective-permute-start.10 = (bf16[4,128,256]{2,1,0:T(8,128)(2,1)S(1)}, bf16[4,128,256]{2,1,0:T(8,128)(2,1)}, u32[]{:S(2)}, u32[]{:S(2)}) collective-permute-start(bf16[4,128,256]{2,1,0:T(8,128)(2,1)S(1)} %get-tuple-element.52), channel_id=1, source_target_pairs={{0,4},{1,5},{2,6},{3,7},{4,0},{5,1},{6,2},{7,3},{8,12},{9,13},{10,... | collective-permute-start | bytes 786440 | tf_op jit(solution)/shard_map/ppermute | solution.py:201
  87.5 3.9 %collective-permute-done.27.rest_7_ = bf16[4,128,256]{2,1,0:T(8,128)(2,1)S(1)} collective-permute-done((bf16[4,128,256]{2,1,0:T(8,128)(2,1)S(1)}, bf16[4,128,256]{2,1,0:T(8,128)(2,1)S(1)}, u32[]{:S(2)}, u32[]{:S(2)}) %collective-permute-start.27) | collective-permute-done | bytes 262176 | tf_op jit(solution)/shard_map/ppermute | solution.py:201
  91.4 1.5 %collective-permute-start.11 = (bf16[4,128,256]{2,1,0:T(8,128)(2,1)S(1)}, bf16[4,128,256]{2,1,0:T(8,128)(2,1)}, u32[]{:S(2)}, u32[]{:S(2)}) collective-permute-start(bf16[4,128,256]{2,1,0:T(8,128)(2,1)S(1)} %get-tuple-element.53), channel_id=1, source_target_pairs={{0,5},{1,4},{2,7},{3,6},{4,1},{5,0},{6,3},{7,2},{8,13},{9,12},{10,... | collective-permute-start | bytes 786440 | tf_op jit(solution)/shard_map/ppermute | solution.py:201
  92.8 0.0 collective-permute-done.7.rest_1_
  92.8 1.4 %collective-permute-start.12 = (bf16[4,128,256]{2,1,0:T(8,128)(2,1)S(1)}, bf16[4,128,256]{2,1,0:T(8,128)(2,1)}, u32[]{:S(2)}, u32[]{:S(2)}) collective-permute-start(bf16[4,128,256]{2,1,0:T(8,128)(2,1)S(1)} %get-tuple-element.54), channel_id=1, source_target_pairs={{0,6},{1,7},{2,4},{3,5},{4,2},{5,3},{6,0},{7,1},{8,14},{9,15},{10,... | collective-permute-start | bytes 786440 | tf_op jit(solution)/shard_map/ppermute | solution.py:201
  94.3 3.0 %collective-permute-done.8.rest_2_ = bf16[4,128,256]{2,1,0:T(8,128)(2,1)S(1)} collective-permute-done((bf16[4,128,256]{2,1,0:T(8,128)(2,1)S(1)}, bf16[4,128,256]{2,1,0:T(8,128)(2,1)S(1)}, u32[]{:S(2)}, u32[]{:S(2)}) %collective-permute-start.8) | collective-permute-done | bytes 262176 | tf_op jit(solution)/shard_map/ppermute | solution.py:201
  97.3 0.4 collective-permute-start.13
  97.8 3.1 %unpack_0.1 = (bf16[128,4096]{1,0:T(8,128)(2,1)}, bf16[128,4096]{1,0:T(8,128)(2,1)}, bf16[128,4096]{1,0:T(8,128)(2,1)}, bf16[128,4096]{1,0:T(8,128)(2,1)}) custom-call(s32[1]{0:T(128)} %bitcast.me_ref, bf16[4,128,256]{2,1,0:T(8,128)(2,1)} %copy-done, bf16[4,128,256]{2,1,0:T(8,128)(2,1)} %copy-done.6, bf16[4,128,256]{2,1,0:T(8,128)(2,1)} %copy-done.7, ...), custom_call_target="tpu_custom_call" | custom-call | tf_op jit(solution)/shard_map/unpack_0/pallas_call | solution.py:238
  100.9 2.0 %collective-permute-done.9.rest_3_ = bf16[4,128,256]{2,1,0:T(8,128)(2,1)S(1)} collective-permute-done((bf16[4,128,256]{2,1,0:T(8,128)(2,1)S(1)}, bf16[4,128,256]{2,1,0:T(8,128)(2,1)S(1)}, u32[]{:S(2)}, u32[]{:S(2)}) %collective-permute-start.9) | collective-permute-done | bytes 262176 | tf_op jit(solution)/shard_map/ppermute | solution.py:201
  102.9 0.0 collective-permute-done.10.rest_4_
  102.9 0.0 collective-permute-done.11.rest_5_
  102.9 5.9 %collective-permute-done.12.rest_6_ = bf16[4,128,256]{2,1,0:T(8,128)(2,1)} collective-permute-done((bf16[4,128,256]{2,1,0:T(8,128)(2,1)S(1)}, bf16[4,128,256]{2,1,0:T(8,128)(2,1)}, u32[]{:S(2)}, u32[]{:S(2)}) %collective-permute-start.12) | collective-permute-done | bytes 262176 | tf_op jit(solution)/shard_map/ppermute | solution.py:201
  108.8 5.0 %collective-permute-done.13.rest_7_ = bf16[4,128,256]{2,1,0:T(8,128)(2,1)} collective-permute-done((bf16[4,128,256]{2,1,0:T(8,128)(2,1)S(1)}, bf16[4,128,256]{2,1,0:T(8,128)(2,1)}, u32[]{:S(2)}, u32[]{:S(2)}) %collective-permute-start.13) | collective-permute-done | bytes 262176 | tf_op jit(solution)/shard_map/ppermute | solution.py:201
  113.9 3.1 %unpack_1.1 = (bf16[128,4096]{1,0:T(8,128)(2,1)}, bf16[128,4096]{1,0:T(8,128)(2,1)}, bf16[128,4096]{1,0:T(8,128)(2,1)}, bf16[128,4096]{1,0:T(8,128)(2,1)}) custom-call(s32[1]{0:T(128)} %bitcast.me_ref, bf16[4,128,256]{2,1,0:T(8,128)(2,1)} %copy-done.1, ...), custom_call_target="tpu_custom_call", output_to_operand_aliasing={{0}: (9, {}), {1}: (10, {}), {2}: (11, {}), {3}: (12, {})} | custom-call | tf_op jit(solution)/shard_map/unpack_1/pallas_call | solution.py:238
  (49 shorter events, 0.1 us)
Async XLA Ops:
  0.6 8.1 %copy-start.16 = (s32[3,1024]{1,0:T(4,128)S(1)}, s32[3,1024]{1,0:T(4,128)}, u32[]{:S(2)}) copy-start(s32[3,1024]{1,0:T(4,128)} %param.11) | copy-start | bytes 36868
  3.8 8.6 %collective-permute-start.14 = (bf16[4,128,256]{2,1,0:T(8,128)(2,1)}, bf16[4,128,256]{2,1,0:T(8,128)(2,1)S(1)}, u32[]{:S(2)}, u32[]{:S(2)}) collective-permute-start(bf16[4,128,256]{2,1,0:T(8,128)(2,1)} %get-tuple-element.57), channel_id=1, source_target_pairs={{0,1},{1,0},{2,3},{3,2},{4,5},{5,4},{6,7},{7,6},{8,9},{9,8},{10,11... | collective-permute-start | bytes 786440 | tf_op jit(solution)/shard_map/ppermute | solution.py:201
  4.3 10.8 %collective-permute-start.15 = (bf16[4,128,256]{2,1,0:T(8,128)(2,1)}, bf16[4,128,256]{2,1,0:T(8,128)(2,1)S(1)}, u32[]{:S(2)}, u32[]{:S(2)}) collective-permute-start(bf16[4,128,256]{2,1,0:T(8,128)(2,1)} %get-tuple-element.58), channel_id=1, source_target_pairs={{0,2},{1,3},{2,0},{3,1},{4,6},{5,7},{6,4},{7,5},{8,10},{9,11},{10,... | collective-permute-start | bytes 786440 | tf_op jit(solution)/shard_map/ppermute | solution.py:201
  6.9 12.6 %collective-permute-start.16 = (bf16[4,128,256]{2,1,0:T(8,128)(2,1)}, bf16[4,128,256]{2,1,0:T(8,128)(2,1)S(1)}, u32[]{:S(2)}, u32[]{:S(2)}) collective-permute-start(bf16[4,128,256]{2,1,0:T(8,128)(2,1)} %get-tuple-element.59), channel_id=1, source_target_pairs={{0,3},{1,2},{2,1},{3,0},{4,7},{5,6},{6,5},{7,4},{8,11},{9,10},{10,... | collective-permute-start | bytes 786440 | tf_op jit(solution)/shard_map/ppermute | solution.py:201
  7.0 13.2 %collective-permute-start.17 = (bf16[4,128,256]{2,1,0:T(8,128)(2,1)}, bf16[4,128,256]{2,1,0:T(8,128)(2,1)S(1)}, u32[]{:S(2)}, u32[]{:S(2)}) collective-permute-start(bf16[4,128,256]{2,1,0:T(8,128)(2,1)} %get-tuple-element.60), channel_id=1, source_target_pairs={{0,4},{1,5},{2,6},{3,7},{4,0},{5,1},{6,2},{7,3},{8,12},{9,13},{10,... | collective-permute-start | bytes 786440 | tf_op jit(solution)/shard_map/ppermute | solution.py:201
  8.7 23.2 %collective-permute-start.18 = (bf16[4,128,256]{2,1,0:T(8,128)(2,1)}, bf16[4,128,256]{2,1,0:T(8,128)(2,1)S(1)}, u32[]{:S(2)}, u32[]{:S(2)}) collective-permute-start(bf16[4,128,256]{2,1,0:T(8,128)(2,1)} %get-tuple-element.61), channel_id=1, source_target_pairs={{0,5},{1,4},{2,7},{3,6},{4,1},{5,0},{6,3},{7,2},{8,13},{9,12},{10,... | collective-permute-start | bytes 786440 | tf_op jit(solution)/shard_map/ppermute | solution.py:201
  9.1 3.3 %copy-start.21 = (bf16[4,128,256]{2,1,0:T(8,128)(2,1)S(1)}, bf16[4,128,256]{2,1,0:T(8,128)(2,1)}, u32[]{:S(2)}) copy-start(bf16[4,128,256]{2,1,0:T(8,128)(2,1)} %get-tuple-element.62) | copy-start | bytes 786436
  9.1 6.0 %copy-start.20 = (bf16[4,128,256]{2,1,0:T(8,128)(2,1)S(1)}, bf16[4,128,256]{2,1,0:T(8,128)(2,1)}, u32[]{:S(2)}) copy-start(bf16[4,128,256]{2,1,0:T(8,128)(2,1)} %get-tuple-element.63) | copy-start | bytes 786436
  12.4 21.6 %collective-permute-start.19 = (bf16[4,128,256]{2,1,0:T(8,128)(2,1)S(1)}, bf16[4,128,256]{2,1,0:T(8,128)(2,1)S(1)}, u32[]{:S(2)}, u32[]{:S(2)}) collective-permute-start(bf16[4,128,256]{2,1,0:T(8,128)(2,1)S(1)} %copy-done.21), channel_id=1, source_target_pairs={{0,6},{1,7},{2,4},{3,5},{4,2},{5,3},{6,0},{7,1},{8,14},{9,15},{10,... | collective-permute-start | bytes 786440 | tf_op jit(solution)/shard_map/ppermute | solution.py:201
  15.1 20.5 %collective-permute-start.20 = (bf16[4,128,256]{2,1,0:T(8,128)(2,1)S(1)}, bf16[4,128,256]{2,1,0:T(8,128)(2,1)S(1)}, u32[]{:S(2)}, u32[]{:S(2)}) collective-permute-start(bf16[4,128,256]{2,1,0:T(8,128)(2,1)S(1)} %copy-done.20), channel_id=1, source_target_pairs={{0,7},{1,6},{2,5},{3,4},{4,3},{5,2},{6,1},{7,0},{8,15},{9,14},{10,... | collective-permute-start | bytes 786440 | tf_op jit(solution)/shard_map/ppermute | solution.py:201
  19.5 16.1 %collective-permute-start = (bf16[4,128,256]{2,1,0:T(8,128)(2,1)}, bf16[4,128,256]{2,1,0:T(8,128)(2,1)S(1)}, u32[]{:S(2)}, u32[]{:S(2)}) collective-permute-start(bf16[4,128,256]{2,1,0:T(8,128)(2,1)} %get-tuple-element.41), channel_id=1, source_target_pairs={{0,1},{1,0},{2,3},{3,2},{4,5},{5,4},{6,7},{7,6},{8,9},{9,8},{10,11... | collective-permute-start | bytes 786440 | tf_op jit(solution)/shard_map/ppermute | solution.py:201
  20.0 15.6 %copy-start.19 = (bf16[4,128,256]{2,1,0:T(8,128)(2,1)S(1)}, bf16[4,128,256]{2,1,0:T(8,128)(2,1)}, u32[]{:S(2)}) copy-start(bf16[4,128,256]{2,1,0:T(8,128)(2,1)} %get-tuple-element.45) | copy-start | bytes 786436
  20.0 15.6 %copy-start.18 = (bf16[4,128,256]{2,1,0:T(8,128)(2,1)S(1)}, bf16[4,128,256]{2,1,0:T(8,128)(2,1)}, u32[]{:S(2)}) copy-start(bf16[4,128,256]{2,1,0:T(8,128)(2,1)} %get-tuple-element.46) | copy-start | bytes 786436
  20.2 18.9 %collective-permute-start.1 = (bf16[4,128,256]{2,1,0:T(8,128)(2,1)}, bf16[4,128,256]{2,1,0:T(8,128)(2,1)S(1)}, u32[]{:S(2)}, u32[]{:S(2)}) collective-permute-start(bf16[4,128,256]{2,1,0:T(8,128)(2,1)} %get-tuple-element.42), channel_id=1, source_target_pairs={{0,2},{1,3},{2,0},{3,1},{4,6},{5,7},{6,4},{7,5},{8,10},{9,11},{10,... | collective-permute-start | bytes 786440 | tf_op jit(solution)/shard_map/ppermute | solution.py:201
  32.0 24.5 %collective-permute-start.2 = (bf16[4,128,256]{2,1,0:T(8,128)(2,1)}, bf16[4,128,256]{2,1,0:T(8,128)(2,1)S(1)}, u32[]{:S(2)}, u32[]{:S(2)}) collective-permute-start(bf16[4,128,256]{2,1,0:T(8,128)(2,1)} %get-tuple-element.43), channel_id=1, source_target_pairs={{0,3},{1,2},{2,1},{3,0},{4,7},{5,6},{6,5},{7,4},{8,11},{9,10},{10,... | collective-permute-start | bytes 786440 | tf_op jit(solution)/shard_map/ppermute | solution.py:201
  34.0 22.7 %collective-permute-start.3 = (bf16[4,128,256]{2,1,0:T(8,128)(2,1)}, bf16[4,128,256]{2,1,0:T(8,128)(2,1)S(1)}, u32[]{:S(2)}, u32[]{:S(2)}) collective-permute-start(bf16[4,128,256]{2,1,0:T(8,128)(2,1)} %get-tuple-element.44), channel_id=1, source_target_pairs={{0,4},{1,5},{2,6},{3,7},{4,0},{5,1},{6,2},{7,3},{8,12},{9,13},{10,... | collective-permute-start | bytes 786440 | tf_op jit(solution)/shard_map/ppermute | solution.py:201
  35.6 22.6 %collective-permute-start.4 = (bf16[4,128,256]{2,1,0:T(8,128)(2,1)S(1)}, bf16[4,128,256]{2,1,0:T(8,128)(2,1)S(1)}, u32[]{:S(2)}, u32[]{:S(2)}) collective-permute-start(bf16[4,128,256]{2,1,0:T(8,128)(2,1)S(1)} %copy-done.19), channel_id=1, source_target_pairs={{0,5},{1,4},{2,7},{3,6},{4,1},{5,0},{6,3},{7,2},{8,13},{9,12},{10,... | collective-permute-start | bytes 786440 | tf_op jit(solution)/shard_map/ppermute | solution.py:201
  35.6 23.6 %collective-permute-start.5 = (bf16[4,128,256]{2,1,0:T(8,128)(2,1)S(1)}, bf16[4,128,256]{2,1,0:T(8,128)(2,1)S(1)}, u32[]{:S(2)}, u32[]{:S(2)}) collective-permute-start(bf16[4,128,256]{2,1,0:T(8,128)(2,1)S(1)} %copy-done.18), channel_id=1, source_target_pairs={{0,6},{1,7},{2,4},{3,5},{4,2},{5,3},{6,0},{7,1},{8,14},{9,15},{10,... | collective-permute-start | bytes 786440 | tf_op jit(solution)/shard_map/ppermute | solution.py:201
  36.8 2.4 %copy-start.17 = (bf16[4,128,256]{2,1,0:T(8,128)(2,1)S(1)}, bf16[4,128,256]{2,1,0:T(8,128)(2,1)}, u32[]{:S(2)}) copy-start(bf16[4,128,256]{2,1,0:T(8,128)(2,1)} %get-tuple-element.47) | copy-start | bytes 786436
  36.8 4.1 %copy-start.3 = (bf16[4,128,256]{2,1,0:T(8,128)(2,1)S(1)}, bf16[4,128,256]{2,1,0:T(8,128)(2,1)}, u32[]{:S(2)}) copy-start(bf16[4,128,256]{2,1,0:T(8,128)(2,1)} %get-tuple-element.56.rest_0_) | copy-start | bytes 786436
  36.8 4.1 %copy-start.5 = (s32[8,8]{1,0:T(8,128)S(1)}, s32[8,8]{1,0:T(8,128)}, u32[]{:S(2)}) copy-start(s32[8,8]{1,0:T(8,128)} %bands_ref.3) | copy-start | bytes 772
  39.1 1.8 %copy-start.4 = (s32[8,8]{1,0:T(8,128)S(1)}, s32[8,8]{1,0:T(8,128)}, u32[]{:S(2)}) copy-start(s32[8,8]{1,0:T(8,128)} %flags_ref.3) | copy-start | bytes 772
  39.1 21.5 %collective-permute-start.6 = (bf16[4,128,256]{2,1,0:T(8,128)(2,1)S(1)}, bf16[4,128,256]{2,1,0:T(8,128)(2,1)S(1)}, u32[]{:S(2)}, u32[]{:S(2)}) collective-permute-start(bf16[4,128,256]{2,1,0:T(8,128)(2,1)S(1)} %copy-done.17), channel_id=1, source_target_pairs={{0,7},{1,6},{2,5},{3,4},{4,3},{5,2},{6,1},{7,0},{8,15},{9,14},{10,... | collective-permute-start | bytes 786440 | tf_op jit(solution)/shard_map/ppermute | solution.py:201
  40.9 19.8 %copy-start.2 = (bf16[4,128,256]{2,1,0:T(8,128)(2,1)S(1)}, bf16[4,128,256]{2,1,0:T(8,128)(2,1)}, u32[]{:S(2)}) copy-start(bf16[4,128,256]{2,1,0:T(8,128)(2,1)} %get-tuple-element.40.rest_0_) | copy-start | bytes 786436
  55.8 0.7 copy-start
  56.5 19.7 %collective-permute-start.21 = (bf16[4,128,256]{2,1,0:T(8,128)(2,1)S(1)}, bf16[4,128,256]{2,1,0:T(8,128)(2,1)S(1)}, u32[]{:S(2)}, u32[]{:S(2)}) collective-permute-start(bf16[4,128,256]{2,1,0:T(8,128)(2,1)S(1)} %get-tuple-element.65), channel_id=1, source_target_pairs={{0,1},{1,0},{2,3},{3,2},{4,5},{5,4},{6,7},{7,6},{8,9},{9,8},{10,11... | collective-permute-start | bytes 786440 | tf_op jit(solution)/shard_map/ppermute | solution.py:201
  56.7 21.2 %collective-permute-start.22 = (bf16[4,128,256]{2,1,0:T(8,128)(2,1)S(1)}, bf16[4,128,256]{2,1,0:T(8,128)(2,1)S(1)}, u32[]{:S(2)}, u32[]{:S(2)}) collective-permute-start(bf16[4,128,256]{2,1,0:T(8,128)(2,1)S(1)} %get-tuple-element.66), channel_id=1, source_target_pairs={{0,2},{1,3},{2,0},{3,1},{4,6},{5,7},{6,4},{7,5},{8,10},{9,11},{10,... | collective-permute-start | bytes 786440 | tf_op jit(solution)/shard_map/ppermute | solution.py:201
  58.2 20.9 %collective-permute-start.23 = (bf16[4,128,256]{2,1,0:T(8,128)(2,1)S(1)}, bf16[4,128,256]{2,1,0:T(8,128)(2,1)S(1)}, u32[]{:S(2)}, u32[]{:S(2)}) collective-permute-start(bf16[4,128,256]{2,1,0:T(8,128)(2,1)S(1)} %get-tuple-element.67), channel_id=1, source_target_pairs={{0,3},{1,2},{2,1},{3,0},{4,7},{5,6},{6,5},{7,4},{8,11},{9,10},{10,... | collective-permute-start | bytes 786440 | tf_op jit(solution)/shard_map/ppermute | solution.py:201
  59.1 20.1 %collective-permute-start.24 = (bf16[4,128,256]{2,1,0:T(8,128)(2,1)S(1)}, bf16[4,128,256]{2,1,0:T(8,128)(2,1)S(1)}, u32[]{:S(2)}, u32[]{:S(2)}) collective-permute-start(bf16[4,128,256]{2,1,0:T(8,128)(2,1)S(1)} %get-tuple-element.68), channel_id=1, source_target_pairs={{0,4},{1,5},{2,6},{3,7},{4,0},{5,1},{6,2},{7,3},{8,12},{9,13},{10,... | collective-permute-start | bytes 786440 | tf_op jit(solution)/shard_map/ppermute | solution.py:201
  60.7 20.1 %collective-permute-start.25 = (bf16[4,128,256]{2,1,0:T(8,128)(2,1)S(1)}, bf16[4,128,256]{2,1,0:T(8,128)(2,1)S(1)}, u32[]{:S(2)}, u32[]{:S(2)}) collective-permute-start(bf16[4,128,256]{2,1,0:T(8,128)(2,1)S(1)} %get-tuple-element.69), channel_id=1, source_target_pairs={{0,5},{1,4},{2,7},{3,6},{4,1},{5,0},{6,3},{7,2},{8,13},{9,12},{10,... | collective-permute-start | bytes 786440 | tf_op jit(solution)/shard_map/ppermute | solution.py:201
  75.5 0.7 copy-start.1
  76.2 21.5 %copy-start.6 = (bf16[4,128,256]{2,1,0:T(8,128)(2,1)}, bf16[4,128,256]{2,1,0:T(8,128)(2,1)S(1)}, u32[]{:S(2)}) copy-start(bf16[4,128,256]{2,1,0:T(8,128)(2,1)S(1)} %collective-permute-done.21.rest_1_) | copy-start | bytes 786436
  76.2 10.0 %collective-permute-start.26 = (bf16[4,128,256]{2,1,0:T(8,128)(2,1)S(1)}, bf16[4,128,256]{2,1,0:T(8,128)(2,1)S(1)}, u32[]{:S(2)}, u32[]{:S(2)}) collective-permute-start(bf16[4,128,256]{2,1,0:T(8,128)(2,1)S(1)} %get-tuple-element.70), channel_id=1, source_target_pairs={{0,6},{1,7},{2,4},{3,5},{4,2},{5,3},{6,0},{7,1},{8,14},{9,15},{10,... | collective-permute-start | bytes 786440 | tf_op jit(solution)/shard_map/ppermute | solution.py:201
  78.0 19.8 %copy-start.7 = (bf16[4,128,256]{2,1,0:T(8,128)(2,1)}, bf16[4,128,256]{2,1,0:T(8,128)(2,1)S(1)}, u32[]{:S(2)}) copy-start(bf16[4,128,256]{2,1,0:T(8,128)(2,1)S(1)} %collective-permute-done.22.rest_2_) | copy-start | bytes 786436
  78.0 13.4 %collective-permute-start.27 = (bf16[4,128,256]{2,1,0:T(8,128)(2,1)S(1)}, bf16[4,128,256]{2,1,0:T(8,128)(2,1)S(1)}, u32[]{:S(2)}, u32[]{:S(2)}) collective-permute-start(bf16[4,128,256]{2,1,0:T(8,128)(2,1)S(1)} %get-tuple-element.71), channel_id=1, source_target_pairs={{0,7},{1,6},{2,5},{3,4},{4,3},{5,2},{6,1},{7,0},{8,15},{9,14},{10,... | collective-permute-start | bytes 786440 | tf_op jit(solution)/shard_map/ppermute | solution.py:201
  79.1 18.6 %copy-start.8 = (bf16[4,128,256]{2,1,0:T(8,128)(2,1)}, bf16[4,128,256]{2,1,0:T(8,128)(2,1)S(1)}, u32[]{:S(2)}) copy-start(bf16[4,128,256]{2,1,0:T(8,128)(2,1)S(1)} %collective-permute-done.23.rest_3_) | copy-start | bytes 786436
  79.1 13.7 %collective-permute-start.7 = (bf16[4,128,256]{2,1,0:T(8,128)(2,1)S(1)}, bf16[4,128,256]{2,1,0:T(8,128)(2,1)S(1)}, u32[]{:S(2)}, u32[]{:S(2)}) collective-permute-start(bf16[4,128,256]{2,1,0:T(8,128)(2,1)S(1)} %get-tuple-element.49), channel_id=1, source_target_pairs={{0,1},{1,0},{2,3},{3,2},{4,5},{5,4},{6,7},{7,6},{8,9},{9,8},{10,11... | collective-permute-start | bytes 786440 | tf_op jit(solution)/shard_map/ppermute | solution.py:201
  79.3 18.5 %copy-start.9 = (bf16[4,128,256]{2,1,0:T(8,128)(2,1)}, bf16[4,128,256]{2,1,0:T(8,128)(2,1)S(1)}, u32[]{:S(2)}) copy-start(bf16[4,128,256]{2,1,0:T(8,128)(2,1)S(1)} %collective-permute-done.24.rest_4_) | copy-start | bytes 786436
  79.3 18.0 %collective-permute-start.8 = (bf16[4,128,256]{2,1,0:T(8,128)(2,1)S(1)}, bf16[4,128,256]{2,1,0:T(8,128)(2,1)S(1)}, u32[]{:S(2)}, u32[]{:S(2)}) collective-permute-start(bf16[4,128,256]{2,1,0:T(8,128)(2,1)S(1)} %get-tuple-element.50), channel_id=1, source_target_pairs={{0,2},{1,3},{2,0},{3,1},{4,6},{5,7},{6,4},{7,5},{8,10},{9,11},{10,... | collective-permute-start | bytes 786440 | tf_op jit(solution)/shard_map/ppermute | solution.py:201
  80.7 17.0 %copy-start.10 = (bf16[4,128,256]{2,1,0:T(8,128)(2,1)}, bf16[4,128,256]{2,1,0:T(8,128)(2,1)S(1)}, u32[]{:S(2)}) copy-start(bf16[4,128,256]{2,1,0:T(8,128)(2,1)S(1)} %collective-permute-done.25.rest_5_) | copy-start | bytes 786436
  80.8 22.1 %collective-permute-start.9 = (bf16[4,128,256]{2,1,0:T(8,128)(2,1)S(1)}, bf16[4,128,256]{2,1,0:T(8,128)(2,1)S(1)}, u32[]{:S(2)}, u32[]{:S(2)}) collective-permute-start(bf16[4,128,256]{2,1,0:T(8,128)(2,1)S(1)} %get-tuple-element.51), channel_id=1, source_target_pairs={{0,3},{1,2},{2,1},{3,0},{4,7},{5,6},{6,5},{7,4},{8,11},{9,10},{10,... | collective-permute-start | bytes 786440 | tf_op jit(solution)/shard_map/ppermute | solution.py:201
  86.2 11.5 %copy-start.14 = (bf16[4,128,256]{2,1,0:T(8,128)(2,1)}, bf16[4,128,256]{2,1,0:T(8,128)(2,1)S(1)}, u32[]{:S(2)}) copy-start(bf16[4,128,256]{2,1,0:T(8,128)(2,1)S(1)} %collective-permute-done.26.rest_6_) | copy-start | bytes 786436
  86.2 16.7 %collective-permute-start.10 = (bf16[4,128,256]{2,1,0:T(8,128)(2,1)S(1)}, bf16[4,128,256]{2,1,0:T(8,128)(2,1)}, u32[]{:S(2)}, u32[]{:S(2)}) collective-permute-start(bf16[4,128,256]{2,1,0:T(8,128)(2,1)S(1)} %get-tuple-element.52), channel_id=1, source_target_pairs={{0,4},{1,5},{2,6},{3,7},{4,0},{5,1},{6,2},{7,3},{8,12},{9,13},{10,... | collective-permute-start | bytes 786440 | tf_op jit(solution)/shard_map/ppermute | solution.py:201
  91.4 6.4 %copy-start.15 = (bf16[4,128,256]{2,1,0:T(8,128)(2,1)}, bf16[4,128,256]{2,1,0:T(8,128)(2,1)S(1)}, u32[]{:S(2)}) copy-start(bf16[4,128,256]{2,1,0:T(8,128)(2,1)S(1)} %collective-permute-done.27.rest_7_) | copy-start | bytes 786436
  91.4 11.6 %collective-permute-start.11 = (bf16[4,128,256]{2,1,0:T(8,128)(2,1)S(1)}, bf16[4,128,256]{2,1,0:T(8,128)(2,1)}, u32[]{:S(2)}, u32[]{:S(2)}) collective-permute-start(bf16[4,128,256]{2,1,0:T(8,128)(2,1)S(1)} %get-tuple-element.53), channel_id=1, source_target_pairs={{0,5},{1,4},{2,7},{3,6},{4,1},{5,0},{6,3},{7,2},{8,13},{9,12},{10,... | collective-permute-start | bytes 786440 | tf_op jit(solution)/shard_map/ppermute | solution.py:201
  92.8 8.0 %copy-start.11 = (bf16[4,128,256]{2,1,0:T(8,128)(2,1)}, bf16[4,128,256]{2,1,0:T(8,128)(2,1)S(1)}, u32[]{:S(2)}) copy-start(bf16[4,128,256]{2,1,0:T(8,128)(2,1)S(1)} %collective-permute-done.7.rest_1_) | copy-start | bytes 786436
  92.8 16.0 %collective-permute-start.12 = (bf16[4,128,256]{2,1,0:T(8,128)(2,1)S(1)}, bf16[4,128,256]{2,1,0:T(8,128)(2,1)}, u32[]{:S(2)}, u32[]{:S(2)}) collective-permute-start(bf16[4,128,256]{2,1,0:T(8,128)(2,1)S(1)} %get-tuple-element.54), channel_id=1, source_target_pairs={{0,6},{1,7},{2,4},{3,5},{4,2},{5,3},{6,0},{7,1},{8,14},{9,15},{10,... | collective-permute-start | bytes 786440 | tf_op jit(solution)/shard_map/ppermute | solution.py:201
  97.3 3.6 %copy-start.12 = (bf16[4,128,256]{2,1,0:T(8,128)(2,1)}, bf16[4,128,256]{2,1,0:T(8,128)(2,1)S(1)}, u32[]{:S(2)}) copy-start(bf16[4,128,256]{2,1,0:T(8,128)(2,1)S(1)} %collective-permute-done.8.rest_2_) | copy-start | bytes 786436
  97.3 16.6 %collective-permute-start.13 = (bf16[4,128,256]{2,1,0:T(8,128)(2,1)S(1)}, bf16[4,128,256]{2,1,0:T(8,128)(2,1)}, u32[]{:S(2)}, u32[]{:S(2)}) collective-permute-start(bf16[4,128,256]{2,1,0:T(8,128)(2,1)S(1)} %get-tuple-element.55), channel_id=1, source_target_pairs={{0,7},{1,6},{2,5},{3,4},{4,3},{5,2},{6,1},{7,0},{8,15},{9,14},{10,... | collective-permute-start | bytes 786440 | tf_op jit(solution)/shard_map/ppermute | solution.py:201
  102.9 11.0 %copy-start.13 = (bf16[4,128,256]{2,1,0:T(8,128)(2,1)}, bf16[4,128,256]{2,1,0:T(8,128)(2,1)S(1)}, u32[]{:S(2)}) copy-start(bf16[4,128,256]{2,1,0:T(8,128)(2,1)S(1)} %collective-permute-done.9.rest_3_) | copy-start | bytes 786436
where the time goes:
time: 117 us
  Pallas kernels  42.3 us (36%)
  waiting for transfers between devices  39.1 us (33%)
  starting transfers between devices  30.3 us (26%)
  other arithmetic  2.9 us (2%)
  local copies, waits for them, and re-layouts  1.46 us (1%)
    ppermute x28, waiting for transfers between devices, exchange(): lax.ppermute(pieces[d], 'seq', pairs[d])  39.1 us
    ppermute x28, starting transfers between devices, exchange(): lax.ppermute(pieces[d], 'seq', pairs[d])  30.3 us
    pallas_call x2, Pallas kernels, attention(): pl.pallas_call(functools.partial(attention_kernel, groups, rows, count, w...  29.7 us
    pallas_call x2, Pallas kernels, pack(): pl.pallas_call(functools.partial(pack_kernel, groups, heads, c * count, c...  6.42 us
    pallas_call x2, Pallas kernels, unpack(): pl.pallas_call(functools.partial(unpack_kernel, groups, heads, c * count,...  6.15 us
  transfers between devices with their start and end apart: 28, of which 9 were waited for; matrix products, arithmetic and copies ran while one was open for 2% of the time, Pallas kernels for 31%

commit v1 on v0

v1 whole, which is shorter than its diff:
```python
import functools
import math

import jax
import jax.numpy as jnp
from jax import lax
from jax.experimental import pallas as pl
from jax.experimental.pallas import tpu as pltpu
from jax.sharding import PartitionSpec as P

H = 32
DH = 128
BLK = 128
NTK = 2.0
CHUNKS = 2
LIMIT = 40 * 1024 * 1024

F32 = jnp.float32
BF16 = jnp.bfloat16
NEG_INF = float("-inf")


def rope_tables(positions):
    third = 2 * (DH // 6)
    part_dims = (DH - 2 * third, third, third)
    pieces = []
    for axis_num, dim in enumerate(part_dims):
        base = 10000.0 * NTK ** (dim / (dim - 2.0))
        pair = (jnp.arange(dim, dtype=jnp.int32) // 2).astype(F32)
        inverse = jnp.exp(pair * (-2.0 * math.log(base) / dim))
        pieces.append(positions[axis_num].astype(F32)[:, None] * inverse[None, :])
    angle = jnp.concatenate(pieces, 1)
    sign = jnp.where(jnp.arange(DH, dtype=jnp.int32) % 2 == 0, -1.0, 1.0).astype(F32)
    return jnp.cos(angle), jnp.sin(angle) * sign[None, :]


def pack_kernel(hops, heads, first, count, me_ref, q_ref, k_ref, v_ref, g_ref, *rest):
    groups = len(hops)
    outs, sems = rest[:groups], rest[groups]
    me = me_ref[0]
    copies = []
    for d in range(groups):
        start = pl.multiple_of(((me ^ hops[d]) * heads + first) * DH, DH)
        for a, ref in enumerate((q_ref, k_ref, v_ref, g_ref)):
            copies.append(
                pltpu.make_async_copy(
                    ref.at[:, pl.ds(start, count * DH)], outs[d].at[a], sems.at[d, a]
                )
            )
    for copy in copies:
        copy.start()
    for copy in copies:
        copy.wait()


def unpack_kernel(hops, heads, first, count, kept, me_ref, *rest):
    groups = len(hops)
    pieces = rest[:groups]
    outs = rest[groups + kept : groups + kept + 4]
    sems = rest[groups + kept + 4]
    me = me_ref[0]
    copies = []
    for d in range(groups):
        start = pl.multiple_of(((me ^ hops[d]) * heads + first) * DH, DH)
        for a in range(4):
            copies.append(
                pltpu.make_async_copy(
                    pieces[d].at[a], outs[a].at[:, pl.ds(start, count * DH)], sems.at[d, a]
                )
            )
    for copy in copies:
        copy.start()
    for copy in copies:
        copy.wait()


def dot(x, y):
    return jnp.dot(x, y, preferred_element_type=F32)


def dot_t(x, y):
    return lax.dot_general(x, y, (((1,), (1,)), ((), ())), preferred_element_type=F32)


def attention_kernel(hops, rows, count, width, me_ref, hops_ref, flags_ref, bands_ref, cos_ref, sin_ref, *rest):
    groups = len(hops)
    ins, outs = rest[:groups], rest[groups : 2 * groups]
    qr, kr, vs, gs, kt, vt, gt, scores, low, ds, dk, dv, os, dqs = rest[2 * groups :]
    total = groups * rows
    per_piece = rows // BLK
    blocks = total // BLK
    scale = 1.0 / math.sqrt(DH)
    score_factor = scale / math.log(2.0)
    me = me_ref[0]

    lane = lax.broadcasted_iota(jnp.int32, (DH, DH), 1)
    sublane = lax.broadcasted_iota(jnp.int32, (DH, DH), 0)
    swap = jnp.where((lane ^ 1) == sublane, 1.0, 0.0).astype(BF16)
    even = lax.broadcasted_iota(jnp.int32, (rows, DH), 1) % 2 == 0
    apart = jnp.abs(
        lax.broadcasted_iota(jnp.int32, (BLK, BLK), 0) - lax.broadcasted_iota(jnp.int32, (BLK, BLK), 1)
    )

    def turn_low(x, cos, sin):
        return (x.astype(F32) * cos + dot(x, swap) * sin).astype(BF16)

    def turn(x, cos, sin):
        partner = jnp.where(even, pltpu.roll(x, DH - 1, 1), pltpu.roll(x, 1, 1))
        return (x * cos + partner * sin).astype(BF16)

    def table_rows(d):
        return pl.ds(pl.multiple_of((me ^ hops[d]) * rows, rows), rows)

    def block_of(b):
        return (me ^ hops_ref[b // per_piece]) * per_piece + b % per_piece

    heads = range(count)
    for d in range(groups):
        at = slice(d * rows, (d + 1) * rows)
        cos, sin = cos_ref[table_rows(d), :], sin_ref[table_rows(d), :]
        for h in heads:
            cols = slice(h * DH, (h + 1) * DH)
            qr[h, at, :] = turn_low(ins[d][0, :, cols], cos, sin)
            key = turn_low(ins[d][1, :, cols], cos, sin)
            kr[h, at, :] = key
            kt[h, :, at] = key.T
            value = ins[d][2, :, cols]
            vs[h, at, :] = value
            vt[h, :, at] = value.T
            grad = ins[d][3, :, cols]
            gs[h, at, :] = grad
            gt[h, :, at] = grad.T
    dk[...] = jnp.zeros_like(dk)
    dv[...] = jnp.zeros_like(dv)

    def one_step(i, carry):
        mine = pl.ds(pl.multiple_of(i * width, width), width)
        largest, inverse, delta = {}, {}, {}
        for h in heads:
            query = qr[h, mine, :]
            top = jnp.full((8, width), NEG_INF, F32)
            for j in range(blocks):
                at = slice(j * BLK, (j + 1) * BLK)
                raw = dot_t(kr[h, at, :], query) * score_factor
                parts = []
                for w in range(width // BLK):
                    row, col = block_of(i * (width // BLK) + w), block_of(j)
                    reach = jnp.where(
                        flags_ref[row, col] == 1, jnp.right_shift(BLK, bands_ref[row, col]), 0
                    )
                    parts.append(jnp.where(apart < reach, raw[:, w * BLK : (w + 1) * BLK], NEG_INF))
                part = jnp.concatenate(parts, 1)
                scores[h, at, :] = part
                top = jnp.maximum(top, jnp.max(part.reshape(BLK // 8, 8, width), axis=0))
            largest[h] = jnp.max(top, axis=0, keepdims=True)
        for h in heads:
            norm = jnp.zeros((8, width), F32)
            for j in range(blocks):
                at = slice(j * BLK, (j + 1) * BLK)
                weights = jnp.exp2(scores[h, at, :] - largest[h])
                scores[h, at, :] = weights
                low[h, at, :] = weights.astype(BF16)
                norm = norm + jnp.sum(weights.reshape(BLK // 8, 8, width), axis=0)
            inverse[h] = 1.0 / jnp.sum(norm, axis=0, keepdims=True)
        for h in heads:
            out_t = (dot(vt[h], low[h]) * inverse[h]).astype(BF16).astype(F32)
            grad_t = gt[h, :, mine].astype(F32)
            delta[h] = jnp.sum(out_t * grad_t, axis=0, keepdims=True)
            os[h, mine, :] = out_t.T.astype(BF16)
            dv[h] += dot_t(low[h], (grad_t * inverse[h]).astype(BF16))
        for h in heads:
            grad = gs[h, mine, :]
            for j in range(blocks):
                at = slice(j * BLK, (j + 1) * BLK)
                grad_probs = dot_t(vs[h, at, :], grad)
                ds[h, at, :] = (scores[h, at, :] * ((grad_probs - delta[h]) * inverse[h])).astype(BF16)
        for h in heads:
            dqs[h, mine, :] = dot(kt[h], ds[h]).T
            dk[h] += dot(ds[h], qr[h, mine, :])
        return carry

    lax.fori_loop(0, total // width, one_step, 0, unroll=True)
    for d in range(groups):
        at = slice(d * rows, (d + 1) * rows)
        cos, sin = cos_ref[table_rows(d), :] * scale, sin_ref[table_rows(d), :] * -scale
        for h in heads:
            cols = slice(h * DH, (h + 1) * DH)
            outs[d][0, :, cols] = os[h, at, :]
            outs[d][1, :, cols] = turn(dqs[h, at, :], cos, sin)
            outs[d][2, :, cols] = turn(dk[h, at, :], cos, sin)
            outs[d][3, :, cols] = dv[h, at, :].astype(BF16)


SMEM = pl.BlockSpec(memory_space=pltpu.SMEM)
VMEM = pl.BlockSpec(memory_space=pltpu.VMEM)
ANY = pl.BlockSpec(memory_space=pl.ANY)


def attention_call(hops, count, me, block_flags, band_ids, tables, pieces):
    rows = pieces[0].shape[1]
    total = len(hops) * rows
    width = 2 * BLK if total % (2 * BLK) == 0 else BLK
    area = total * total
    return pl.pallas_call(
        functools.partial(attention_kernel, hops, rows, count, width),
        out_shape=[jax.ShapeDtypeStruct(pieces[0].shape, BF16)] * len(hops),
        in_specs=[SMEM] * 4 + [VMEM] * (len(tables) + len(hops)),
        out_specs=[VMEM] * len(hops),
        scratch_shapes=[pltpu.VMEM((count, total, DH), BF16)] * 4
        + [pltpu.VMEM((count, DH, total), BF16)] * 3
        + [pltpu.VMEM((count, total, width), F32)]
        + [pltpu.VMEM((count, total, width), BF16)] * 2
        + [pltpu.VMEM((count, total, DH), F32)] * 2
        + [pltpu.VMEM((count, total, DH), BF16), pltpu.VMEM((count, total, DH), F32)],
        compiler_params=pltpu.CompilerParams(vmem_limit_bytes=LIMIT),
        cost_estimate=pl.CostEstimate(
            flops=10 * count * area * DH,
            bytes_accessed=16 * total * count * DH,
            transcendentals=count * area,
        ),
        name="attention",
    )(me, jnp.array(hops, jnp.int32), block_flags, band_ids, *tables, *pieces)


def body(query_in, key_in, value_in, grad_out, positions, block_flags, band_ids):
    groups = lax.axis_size("seq")
    rows, channels = query_in.shape
    heads = channels // DH // groups
    chunks = math.gcd(CHUNKS, heads)
    count = heads // chunks
    me = lax.axis_index("seq").astype(jnp.int32).reshape(1)
    arrays = (query_in, key_in, value_in, grad_out)
    piece = jax.ShapeDtypeStruct((4, rows, count * DH), BF16)
    hops = tuple(sorted(range(groups), key=lambda d: (d > 0, -(d >> 1).bit_count(), d & 1, d)))

    def exchange(pieces):
        return [pieces[0]] + [
            lax.ppermute(piece, "seq", [(i, i ^ d) for i in range(groups)])
            for piece, d in zip(pieces[1:], hops[1:])
        ]

    def pack(c):
        return pl.pallas_call(
            functools.partial(pack_kernel, hops, heads, c * count, count),
            out_shape=[piece] * groups,
            in_specs=[SMEM] + [ANY] * 4,
            out_specs=[VMEM] * groups,
            scratch_shapes=[pltpu.SemaphoreType.DMA((groups, 4))],
            name=f"pack_{c}",
        )(me, *arrays)

    def unpack(c, pieces, before):
        kept = len(before)
        return pl.pallas_call(
            functools.partial(unpack_kernel, hops, heads, c * count, count, kept),
            out_shape=[jax.ShapeDtypeStruct((rows, channels), BF16)] * 4,
            in_specs=[SMEM] + [VMEM] * groups + [ANY] * kept,
            out_specs=[ANY] * 4,
            input_output_aliases={1 + groups + a: a for a in range(kept)},
            scratch_shapes=[pltpu.SemaphoreType.DMA((groups, 4))],
            name=f"unpack_{c}",
        )(me, *pieces, *before)

    tables = rope_tables(positions)
    arrived = [exchange(pack(c)) for c in range(chunks)]
    results = ()
    for c in range(chunks):
        turned = exchange(
            attention_call(hops, count, me, block_flags, band_ids, tables, arrived[c])
        )
        results = unpack(c, turned, results)
    return tuple(results)


def solution(mesh):
    tokens = P(("clip", "seq"), None)
    return jax.shard_map(
        body,
        mesh=mesh,
        in_specs=(tokens, tokens, tokens, tokens, P(None, "clip"), P("clip", None), P("clip", None)),
        out_specs=(tokens, tokens, tokens, tokens),
        check_vma=False,
    )
```

time: 117 us -> 106 us (0.906)
  Pallas kernels: 42.3 us -> 31.1 us
  starting transfers between devices: 30.3 us -> 23.9 us
  waiting for transfers between devices: 39.1 us -> 44.6 us
    pallas_call x6, Pallas kernels: 42.3 us -> 31.1 us  [the longest x2 18.5 us: attention_call(): pl.pallas_call(functools.partial(attention_kernel, hops, rows, count, wid...]
    ppermute x28, starting transfers between devices: 30.3 us -> 23.9 us  [exchange(): lax.ppermute(piece, 'seq', [(i, i ^ d) for i in range(groups)])]
    ppermute x28, waiting for transfers between devices: 39.1 us -> 44.6 us  [exchange(): lax.ppermute(piece, 'seq', [(i, i ^ d) for i in range(groups)])]
  transfers between devices with their start and end apart: 28 -> 28, of which waited for: 9 -> 13; matrix products, arithmetic and copies ran while one was open for 2% -> 3% of each run, Pallas kernels for 31% -> 23%
where the time goes in v1:
time: 106 us
  waiting for transfers between devices  44.6 us (42%)
  Pallas kernels  31.1 us (29%)
  starting transfers between devices  23.9 us (23%)
  other arithmetic  3.09 us (3%)
  local copies, waits for them, and re-layouts  2.1 us (2%)
  between operations  1.07 us (1%)
    ppermute x28, waiting for transfers between devices, exchange(): lax.ppermute(piece, 'seq', [(i, i ^ d) for i in range(groups)])  44.6 us
    ppermute x28, starting transfers between devices, exchange(): lax.ppermute(piece, 'seq', [(i, i ^ d) for i in range(groups)])  23.9 us
    pallas_call x2, Pallas kernels, attention_call(): pl.pallas_call(functools.partial(attention_kernel, hops, rows, count, wid...  18.5 us
    pallas_call x2, Pallas kernels, pack(): pl.pallas_call(functools.partial(pack_kernel, hops, heads, c * count, cou...  6.43 us
    pallas_call x2, Pallas kernels, unpack(): pl.pallas_call(functools.partial(unpack_kernel, hops, heads, c * count, c...  6.15 us
    mul x1, other arithmetic, rope_tables(): return (jnp.cos(angle), jnp.sin(angle) * sign[None, :])  2.54 us
  transfers between devices with their start and end apart: 28, of which 13 were waited for; matrix products, arithmetic and copies ran while one was open for 3% of the time, Pallas kernels for 23%

profile of v1, /device:TPU:0, one launch (start us, length us, event | category | flops | bytes accessed | tf_op | source)
XLA Modules:
  0.0 105.8 jit_solution(5137981299562467967)
XLA Ops:
  0.6 3.2 %pack_0.1 = (bf16[4,128,256]{2,1,0:T(8,128)(2,1)}, bf16[4,128,256]{2,1,0:T(8,128)(2,1)}, bf16[4,128,256]{2,1,0:T(8,128)(2,1)}, bf16[4,128,256]{2,1,0:T(8,128)(2,...) custom-call(s32[1]{0:T(128)} %bitcast.me_ref, ...), custom_call_target="tpu_custom_call" | custom-call | tf_op jit(solution)/shard_map/pack_0/pallas_call | solution.py:243
  3.8 4.0 %collective-permute-start.14 = (bf16[4,128,256]{2,1,0:T(8,128)(2,1)}, bf16[4,128,256]{2,1,0:T(8,128)(2,1)S(1)}, u32[]{:S(2)}, u32[]{:S(2)}) collective-permute-start(bf16[4,128,256]{2,1,0:T(8,128)(2,1)} %get-tuple-element.57), channel_id=1, source_target_pairs={{0,6},{1,7},{2,4},{3,5},{4,2},{5,3},{6,0},{7,1},{8,14},{9,15},{10,... | collective-permute-start | bytes 786440 | tf_op jit(solution)/shard_map/ppermute | solution.py:238
  7.8 0.0 collective-permute-start.15
  7.8 1.1 %collective-permute-start.16 = (bf16[4,128,256]{2,1,0:T(8,128)(2,1)}, bf16[4,128,256]{2,1,0:T(8,128)(2,1)S(1)}, u32[]{:S(2)}, u32[]{:S(2)}) collective-permute-start(bf16[4,128,256]{2,1,0:T(8,128)(2,1)} %get-tuple-element.59), channel_id=1, source_target_pairs={{0,2},{1,3},{2,0},{3,1},{4,6},{5,7},{6,4},{7,5},{8,10},{9,11},{10,... | collective-permute-start | bytes 786440 | tf_op jit(solution)/shard_map/ppermute | solution.py:238
  8.9 1.5 %collective-permute-start.17 = (bf16[4,128,256]{2,1,0:T(8,128)(2,1)}, bf16[4,128,256]{2,1,0:T(8,128)(2,1)S(1)}, u32[]{:S(2)}, u32[]{:S(2)}) collective-permute-start(bf16[4,128,256]{2,1,0:T(8,128)(2,1)} %get-tuple-element.60), channel_id=1, source_target_pairs={{0,4},{1,5},{2,6},{3,7},{4,0},{5,1},{6,2},{7,3},{8,12},{9,13},{10,... | collective-permute-start | bytes 786440 | tf_op jit(solution)/shard_map/ppermute | solution.py:238
  10.4 0.6 collective-permute-start.18
  11.0 0.3 broadcast_multiply_fusion.1
  11.4 3.3 %pack_1.1 = (bf16[4,128,256]{2,1,0:T(8,128)(2,1)}, bf16[4,128,256]{2,1,0:T(8,128)(2,1)}, bf16[4,128,256]{2,1,0:T(8,128)(2,1)}, bf16[4,128,256]{2,1,0:T(8,128)(2,...) custom-call(s32[1]{0:T(128)} %bitcast.me_ref, ...), custom_call_target="tpu_custom_call" | custom-call | tf_op jit(solution)/shard_map/pack_1/pallas_call | solution.py:243
  14.7 0.5 collective-permute-done.14.rest_1_
  15.2 0.1 collective-permute-start.19
  15.3 5.1 %collective-permute-done.15.rest_2_ = bf16[4,128,256]{2,1,0:T(8,128)(2,1)S(1)} collective-permute-done((bf16[4,128,256]{2,1,0:T(8,128)(2,1)}, bf16[4,128,256]{2,1,0:T(8,128)(2,1)S(1)}, u32[]{:S(2)}, u32[]{:S(2)}) %collective-permute-start.15) | collective-permute-done | bytes 262176 | tf_op jit(solution)/shard_map/ppermute | solution.py:238
  20.5 0.1 collective-permute-start.20
  20.6 6.4 %collective-permute-done.16.rest_3_ = bf16[4,128,256]{2,1,0:T(8,128)(2,1)S(1)} collective-permute-done((bf16[4,128,256]{2,1,0:T(8,128)(2,1)}, bf16[4,128,256]{2,1,0:T(8,128)(2,1)S(1)}, u32[]{:S(2)}, u32[]{:S(2)}) %collective-permute-start.16) | collective-permute-done | bytes 262176 | tf_op jit(solution)/shard_map/ppermute | solution.py:238
  27.0 1.4 %collective-permute-start = (bf16[4,128,256]{2,1,0:T(8,128)(2,1)}, bf16[4,128,256]{2,1,0:T(8,128)(2,1)S(1)}, u32[]{:S(2)}, u32[]{:S(2)}) collective-permute-start(bf16[4,128,256]{2,1,0:T(8,128)(2,1)} %get-tuple-element.41), channel_id=1, source_target_pairs={{0,6},{1,7},{2,4},{3,5},{4,2},{5,3},{6,0},{7,1},{8,14},{9,15},{10,... | collective-permute-start | bytes 786440 | tf_op jit(solution)/shard_map/ppermute | solution.py:238
  28.4 0.2 broadcast_multiply_fusion.2
  28.6 0.0 collective-permute-done.17.rest_4_
  28.6 0.1 collective-permute-start.1
  28.7 3.0 %collective-permute-done.18.rest_5_ = bf16[4,128,256]{2,1,0:T(8,128)(2,1)S(1)} collective-permute-done((bf16[4,128,256]{2,1,0:T(8,128)(2,1)}, bf16[4,128,256]{2,1,0:T(8,128)(2,1)S(1)}, u32[]{:S(2)}, u32[]{:S(2)}) %collective-permute-start.18) | collective-permute-done | bytes 262176 | tf_op jit(solution)/shard_map/ppermute | solution.py:238
  31.7 0.5 collective-permute-start.2
  32.2 0.0 collective-permute-done.19.rest_6_
  32.2 1.7 %collective-permute-start.3 = (bf16[4,128,256]{2,1,0:T(8,128)(2,1)}, bf16[4,128,256]{2,1,0:T(8,128)(2,1)S(1)}, u32[]{:S(2)}, u32[]{:S(2)}) collective-permute-start(bf16[4,128,256]{2,1,0:T(8,128)(2,1)} %get-tuple-element.44), channel_id=1, source_target_pairs={{0,4},{1,5},{2,6},{3,7},{4,0},{5,1},{6,2},{7,3},{8,12},{9,13},{10,... | collective-permute-start | bytes 786440 | tf_op jit(solution)/shard_map/ppermute | solution.py:238
  33.9 0.0 collective-permute-done.20.rest_7_
  33.9 0.9 collective-permute-start.4
  34.8 2.9 %collective-permute-done.rest_1_ = bf16[4,128,256]{2,1,0:T(8,128)(2,1)S(1)} collective-permute-done((bf16[4,128,256]{2,1,0:T(8,128)(2,1)}, bf16[4,128,256]{2,1,0:T(8,128)(2,1)S(1)}, u32[]{:S(2)}, u32[]{:S(2)}) %collective-permute-start) | collective-permute-done | bytes 262176 | tf_op jit(solution)/shard_map/ppermute | solution.py:238
  37.7 0.0 collective-permute-start.5
  37.8 0.0 copy-start.5
  37.8 2.5 %sine_multiply_fusion = (f32[1024,128]{1,0:T(8,128)S(1)}, f32[1024,128]{1,0:T(8,128)S(1)}) fusion(f32[128]{0:T(128)S(1)} %compare_select_fusion, f32[1024,42]{1,0:T(8,128)S(1)} %get-tuple-element.82, f32[1024,42]{1,0:T(8,128)S(1)} %get-tuple-element.81, f32[1024,44]{1,0:T(8,128)S(1)} %broadcast_multiply_fusion.2), kind=kLoop, calls=%fused_computation.1 | loop fusion | flops 393216 | bytes 1573376 | tf_op jit(solution)/shard_map/mul | solution.py:34
  40.3 0.0 copy-start.4
  40.3 2.7 %collective-permute-done.1.rest_2_ = bf16[4,128,256]{2,1,0:T(8,128)(2,1)S(1)} collective-permute-done((bf16[4,128,256]{2,1,0:T(8,128)(2,1)}, bf16[4,128,256]{2,1,0:T(8,128)(2,1)S(1)}, u32[]{:S(2)}, u32[]{:S(2)}) %collective-permute-start.1) | collective-permute-done | bytes 262176 | tf_op jit(solution)/shard_map/ppermute | solution.py:238
  43.0 0.1 collective-permute-start.6
  43.1 0.6 copy-done.6
  43.8 9.1 %attention.3 = (bf16[4,128,256]{2,1,0:T(8,128)(2,1)S(1)}, bf16[4,128,256]{2,1,0:T(8,128)(2,1)S(1)}, bf16[4,128,256]{2,1,0:T(8,128)(2,1)S(1)}, bf16[4,128,256]{2,...) custom-call(s32[1]{0:T(128)} %bitcast.me_ref, ...), custom_call_target="tpu_custom_call" | custom-call | flops 2684354560 | bytes 4194304 | tf_op jit(solution)/shard_map/attention/pallas_call | solution.py:204
  52.9 0.7 copy-done
  53.6 0.0 collective-permute-done.2.rest_3_
  53.6 3.0 %collective-permute-start.21 = (bf16[4,128,256]{2,1,0:T(8,128)(2,1)S(1)}, bf16[4,128,256]{2,1,0:T(8,128)(2,1)S(1)}, u32[]{:S(2)}, u32[]{:S(2)}) collective-permute-start(bf16[4,128,256]{2,1,0:T(8,128)(2,1)S(1)} %get-tuple-element.65), channel_id=1, source_target_pairs={{0,6},{1,7},{2,4},{3,5},{4,2},{5,3},{6,0},{7,1},{8,14},{9,15},{10,... | collective-permute-start | bytes 786440 | tf_op jit(solution)/shard_map/ppermute | solution.py:238
  56.6 0.0 collective-permute-done.3.rest_4_
  56.6 0.0 collective-permute-start.22
  56.6 0.0 collective-permute-done.4.rest_5_
  56.6 1.3 %collective-permute-start.23 = (bf16[4,128,256]{2,1,0:T(8,128)(2,1)S(1)}, bf16[4,128,256]{2,1,0:T(8,128)(2,1)S(1)}, u32[]{:S(2)}, u32[]{:S(2)}) collective-permute-start(bf16[4,128,256]{2,1,0:T(8,128)(2,1)S(1)} %get-tuple-element.67), channel_id=1, source_target_pairs={{0,2},{1,3},{2,0},{3,1},{4,6},{5,7},{6,4},{7,5},{8,10},{9,11},{10,... | collective-permute-start | bytes 786440 | tf_op jit(solution)/shard_map/ppermute | solution.py:238
  57.9 0.0 collective-permute-done.5.rest_6_
  57.9 1.5 %collective-permute-start.24 = (bf16[4,128,256]{2,1,0:T(8,128)(2,1)S(1)}, bf16[4,128,256]{2,1,0:T(8,128)(2,1)S(1)}, u32[]{:S(2)}, u32[]{:S(2)}) collective-permute-start(bf16[4,128,256]{2,1,0:T(8,128)(2,1)S(1)} %get-tuple-element.68), channel_id=1, source_target_pairs={{0,4},{1,5},{2,6},{3,7},{4,0},{5,1},{6,2},{7,3},{8,12},{9,13},{10,... | collective-permute-start | bytes 786440 | tf_op jit(solution)/shard_map/ppermute | solution.py:238
  59.4 0.0 collective-permute-done.6.rest_7_
  59.4 0.4 collective-permute-start.25
  59.8 9.3 %attention.2 = (bf16[4,128,256]{2,1,0:T(8,128)(2,1)S(1)}, bf16[4,128,256]{2,1,0:T(8,128)(2,1)S(1)}, bf16[4,128,256]{2,1,0:T(8,128)(2,1)S(1)}, bf16[4,128,256]{2,...) custom-call(s32[1]{0:T(128)} %bitcast.me_ref, ...), custom_call_target="tpu_custom_call" | custom-call | flops 2684354560 | bytes 4194304 | tf_op jit(solution)/shard_map/attention/pallas_call | solution.py:204
  69.1 0.7 copy-done.1
  69.8 0.0 collective-permute-done.21.rest_1_
  69.8 0.7 collective-permute-start.26
  70.5 0.0 collective-permute-start.27
  70.5 5.0 %collective-permute-done.23.rest_3_ = bf16[4,128,256]{2,1,0:T(8,128)(2,1)S(1)} collective-permute-done((bf16[4,128,256]{2,1,0:T(8,128)(2,1)S(1)}, bf16[4,128,256]{2,1,0:T(8,128)(2,1)S(1)}, u32[]{:S(2)}, u32[]{:S(2)}) %collective-permute-start.23) | collective-permute-done | bytes 262176 | tf_op jit(solution)/shard_map/ppermute | solution.py:238
  75.5 1.4 %collective-permute-start.7 = (bf16[4,128,256]{2,1,0:T(8,128)(2,1)S(1)}, bf16[4,128,256]{2,1,0:T(8,128)(2,1)S(1)}, u32[]{:S(2)}, u32[]{:S(2)}) collective-permute-start(bf16[4,128,256]{2,1,0:T(8,128)(2,1)S(1)} %get-tuple-element.49), channel_id=1, source_target_pairs={{0,6},{1,7},{2,4},{3,5},{4,2},{5,3},{6,0},{7,1},{8,14},{9,15},{10,... | collective-permute-start | bytes 786440 | tf_op jit(solution)/shard_map/ppermute | solution.py:238
  77.0 3.2 %collective-permute-done.25.rest_5_ = bf16[4,128,256]{2,1,0:T(8,128)(2,1)S(1)} collective-permute-done((bf16[4,128,256]{2,1,0:T(8,128)(2,1)S(1)}, bf16[4,128,256]{2,1,0:T(8,128)(2,1)S(1)}, u32[]{:S(2)}, u32[]{:S(2)}) %collective-permute-start.25) | collective-permute-done | bytes 262176 | tf_op jit(solution)/shard_map/ppermute | solution.py:238
  80.2 0.6 collective-permute-start.9
  80.7 1.7 %collective-permute-start.10 = (bf16[4,128,256]{2,1,0:T(8,128)(2,1)S(1)}, bf16[4,128,256]{2,1,0:T(8,128)(2,1)}, u32[]{:S(2)}, u32[]{:S(2)}) collective-permute-start(bf16[4,128,256]{2,1,0:T(8,128)(2,1)S(1)} %get-tuple-element.52), channel_id=1, source_target_pairs={{0,4},{1,5},{2,6},{3,7},{4,0},{5,1},{6,2},{7,3},{8,12},{9,13},{10,... | collective-permute-start | bytes 786440 | tf_op jit(solution)/shard_map/ppermute | solution.py:238
  82.4 0.0 collective-permute-done.27.rest_7_
  82.4 0.9 collective-permute-start.11
  83.4 2.9 %collective-permute-done.7.rest_1_ = bf16[4,128,256]{2,1,0:T(8,128)(2,1)S(1)} collective-permute-done((bf16[4,128,256]{2,1,0:T(8,128)(2,1)S(1)}, bf16[4,128,256]{2,1,0:T(8,128)(2,1)S(1)}, u32[]{:S(2)}, u32[]{:S(2)}) %collective-permute-start.7) | collective-permute-done | bytes 262176 | tf_op jit(solution)/shard_map/ppermute | solution.py:238
  86.3 0.0 collective-permute-start.12
  86.3 5.1 %collective-permute-done.8.rest_2_ = bf16[4,128,256]{2,1,0:T(8,128)(2,1)S(1)} collective-permute-done((bf16[4,128,256]{2,1,0:T(8,128)(2,1)S(1)}, bf16[4,128,256]{2,1,0:T(8,128)(2,1)S(1)}, u32[]{:S(2)}, u32[]{:S(2)}) %collective-permute-start.8) | collective-permute-done | bytes 262176 | tf_op jit(solution)/shard_map/ppermute | solution.py:238
  91.4 0.2 collective-permute-start.13
  91.7 3.1 %unpack_0.1 = (bf16[128,4096]{1,0:T(8,128)(2,1)}, bf16[128,4096]{1,0:T(8,128)(2,1)}, bf16[128,4096]{1,0:T(8,128)(2,1)}, bf16[128,4096]{1,0:T(8,128)(2,1)}) custom-call(s32[1]{0:T(128)} %bitcast.me_ref, bf16[4,128,256]{2,1,0:T(8,128)(2,1)} %copy-done, bf16[4,128,256]{2,1,0:T(8,128)(2,1)} %copy-done.7, bf16[4,128,256]{2,1,0:T(8,128)(2,1)} %copy-done.8, ...), custom_call_target="tpu_custom_call" | custom-call | tf_op jit(solution)/shard_map/unpack_0/pallas_call | solution.py:254
  94.8 3.2 %collective-permute-done.9.rest_3_ = bf16[4,128,256]{2,1,0:T(8,128)(2,1)S(1)} collective-permute-done((bf16[4,128,256]{2,1,0:T(8,128)(2,1)S(1)}, bf16[4,128,256]{2,1,0:T(8,128)(2,1)S(1)}, u32[]{:S(2)}, u32[]{:S(2)}) %collective-permute-start.9) | collective-permute-done | bytes 262176 | tf_op jit(solution)/shard_map/ppermute | solution.py:238
  98.1 3.8 %collective-permute-done.11.rest_5_ = bf16[4,128,256]{2,1,0:T(8,128)(2,1)} collective-permute-done((bf16[4,128,256]{2,1,0:T(8,128)(2,1)S(1)}, bf16[4,128,256]{2,1,0:T(8,128)(2,1)}, u32[]{:S(2)}, u32[]{:S(2)}) %collective-permute-start.11) | collective-permute-done | bytes 262176 | tf_op jit(solution)/shard_map/ppermute | solution.py:238
  101.9 0.7 collective-permute-done.12.rest_6_
  102.6 3.1 %unpack_1.1 = (bf16[128,4096]{1,0:T(8,128)(2,1)}, bf16[128,4096]{1,0:T(8,128)(2,1)}, bf16[128,4096]{1,0:T(8,128)(2,1)}, bf16[128,4096]{1,0:T(8,128)(2,1)}) custom-call(s32[1]{0:T(128)} %bitcast.me_ref, bf16[4,128,256]{2,1,0:T(8,128)(2,1)} %copy-done.1, ...), custom_call_target="tpu_custom_call", output_to_operand_aliasing={{0}: (9, {}), {1}: (10, {}), {2}: (11, {}), {3}: (12, {})} | custom-call | tf_op jit(solution)/shard_map/unpack_1/pallas_call | solution.py:254
  (51 shorter events, 0.1 us)
Async XLA Ops:
  0.6 10.4 %copy-start.17 = (s32[3,1024]{1,0:T(4,128)S(1)}, s32[3,1024]{1,0:T(4,128)}, u32[]{:S(2)}) copy-start(s32[3,1024]{1,0:T(4,128)} %param.13) | copy-start | bytes 36868
  3.8 11.4 %collective-permute-start.14 = (bf16[4,128,256]{2,1,0:T(8,128)(2,1)}, bf16[4,128,256]{2,1,0:T(8,128)(2,1)S(1)}, u32[]{:S(2)}, u32[]{:S(2)}) collective-permute-start(bf16[4,128,256]{2,1,0:T(8,128)(2,1)} %get-tuple-element.57), channel_id=1, source_target_pairs={{0,6},{1,7},{2,4},{3,5},{4,2},{5,3},{6,0},{7,1},{8,14},{9,15},{10,... | collective-permute-start | bytes 786440 | tf_op jit(solution)/shard_map/ppermute | solution.py:238
  7.8 12.7 %collective-permute-start.15 = (bf16[4,128,256]{2,1,0:T(8,128)(2,1)}, bf16[4,128,256]{2,1,0:T(8,128)(2,1)S(1)}, u32[]{:S(2)}, u32[]{:S(2)}) collective-permute-start(bf16[4,128,256]{2,1,0:T(8,128)(2,1)} %get-tuple-element.58), channel_id=1, source_target_pairs={{0,7},{1,6},{2,5},{3,4},{4,3},{5,2},{6,1},{7,0},{8,15},{9,14},{10,... | collective-permute-start | bytes 786440 | tf_op jit(solution)/shard_map/ppermute | solution.py:238
  7.8 19.2 %collective-permute-start.16 = (bf16[4,128,256]{2,1,0:T(8,128)(2,1)}, bf16[4,128,256]{2,1,0:T(8,128)(2,1)S(1)}, u32[]{:S(2)}, u32[]{:S(2)}) collective-permute-start(bf16[4,128,256]{2,1,0:T(8,128)(2,1)} %get-tuple-element.59), channel_id=1, source_target_pairs={{0,2},{1,3},{2,0},{3,1},{4,6},{5,7},{6,4},{7,5},{8,10},{9,11},{10,... | collective-permute-start | bytes 786440 | tf_op jit(solution)/shard_map/ppermute | solution.py:238
  8.9 19.7 %collective-permute-start.17 = (bf16[4,128,256]{2,1,0:T(8,128)(2,1)}, bf16[4,128,256]{2,1,0:T(8,128)(2,1)S(1)}, u32[]{:S(2)}, u32[]{:S(2)}) collective-permute-start(bf16[4,128,256]{2,1,0:T(8,128)(2,1)} %get-tuple-element.60), channel_id=1, source_target_pairs={{0,4},{1,5},{2,6},{3,7},{4,0},{5,1},{6,2},{7,3},{8,12},{9,13},{10,... | collective-permute-start | bytes 786440 | tf_op jit(solution)/shard_map/ppermute | solution.py:238
  10.4 21.3 %collective-permute-start.18 = (bf16[4,128,256]{2,1,0:T(8,128)(2,1)}, bf16[4,128,256]{2,1,0:T(8,128)(2,1)S(1)}, u32[]{:S(2)}, u32[]{:S(2)}) collective-permute-start(bf16[4,128,256]{2,1,0:T(8,128)(2,1)} %get-tuple-element.61), channel_id=1, source_target_pairs={{0,3},{1,2},{2,1},{3,0},{4,7},{5,6},{6,5},{7,4},{8,11},{9,10},{10,... | collective-permute-start | bytes 786440 | tf_op jit(solution)/shard_map/ppermute | solution.py:238
  11.4 3.8 %copy-start.22 = (bf16[4,128,256]{2,1,0:T(8,128)(2,1)S(1)}, bf16[4,128,256]{2,1,0:T(8,128)(2,1)}, u32[]{:S(2)}) copy-start(bf16[4,128,256]{2,1,0:T(8,128)(2,1)} %get-tuple-element.62) | copy-start | bytes 786436
  11.4 9.1 %copy-start.21 = (bf16[4,128,256]{2,1,0:T(8,128)(2,1)S(1)}, bf16[4,128,256]{2,1,0:T(8,128)(2,1)}, u32[]{:S(2)}) copy-start(bf16[4,128,256]{2,1,0:T(8,128)(2,1)} %get-tuple-element.63) | copy-start | bytes 786436
  15.2 17.0 %collective-permute-start.19 = (bf16[4,128,256]{2,1,0:T(8,128)(2,1)S(1)}, bf16[4,128,256]{2,1,0:T(8,128)(2,1)S(1)}, u32[]{:S(2)}, u32[]{:S(2)}) collective-permute-start(bf16[4,128,256]{2,1,0:T(8,128)(2,1)S(1)} %copy-done.22), channel_id=1, source_target_pairs={{0,5},{1,4},{2,7},{3,6},{4,1},{5,0},{6,3},{7,2},{8,13},{9,12},{10,... | collective-permute-start | bytes 786440 | tf_op jit(solution)/shard_map/ppermute | solution.py:238
  20.5 13.4 %collective-permute-start.20 = (bf16[4,128,256]{2,1,0:T(8,128)(2,1)S(1)}, bf16[4,128,256]{2,1,0:T(8,128)(2,1)S(1)}, u32[]{:S(2)}, u32[]{:S(2)}) collective-permute-start(bf16[4,128,256]{2,1,0:T(8,128)(2,1)S(1)} %copy-done.21), channel_id=1, source_target_pairs={{0,1},{1,0},{2,3},{3,2},{4,5},{5,4},{6,7},{7,6},{8,9},{9,8},{10,11... | collective-permute-start | bytes 786440 | tf_op jit(solution)/shard_map/ppermute | solution.py:238
  27.0 10.8 %collective-permute-start = (bf16[4,128,256]{2,1,0:T(8,128)(2,1)}, bf16[4,128,256]{2,1,0:T(8,128)(2,1)S(1)}, u32[]{:S(2)}, u32[]{:S(2)}) collective-permute-start(bf16[4,128,256]{2,1,0:T(8,128)(2,1)} %get-tuple-element.41), channel_id=1, source_target_pairs={{0,6},{1,7},{2,4},{3,5},{4,2},{5,3},{6,0},{7,1},{8,14},{9,15},{10,... | collective-permute-start | bytes 786440 | tf_op jit(solution)/shard_map/ppermute | solution.py:238
  28.4 5.5 %copy-start.20 = (bf16[4,128,256]{2,1,0:T(8,128)(2,1)S(1)}, bf16[4,128,256]{2,1,0:T(8,128)(2,1)}, u32[]{:S(2)}) copy-start(bf16[4,128,256]{2,1,0:T(8,128)(2,1)} %get-tuple-element.45) | copy-start | bytes 786436
  28.4 9.3 %copy-start.19 = (bf16[4,128,256]{2,1,0:T(8,128)(2,1)S(1)}, bf16[4,128,256]{2,1,0:T(8,128)(2,1)}, u32[]{:S(2)}) copy-start(bf16[4,128,256]{2,1,0:T(8,128)(2,1)} %get-tuple-element.46) | copy-start | bytes 786436
  28.6 14.4 %collective-permute-start.1 = (bf16[4,128,256]{2,1,0:T(8,128)(2,1)}, bf16[4,128,256]{2,1,0:T(8,128)(2,1)S(1)}, u32[]{:S(2)}, u32[]{:S(2)}) collective-permute-start(bf16[4,128,256]{2,1,0:T(8,128)(2,1)} %get-tuple-element.42), channel_id=1, source_target_pairs={{0,7},{1,6},{2,5},{3,4},{4,3},{5,2},{6,1},{7,0},{8,15},{9,14},{10,... | collective-permute-start | bytes 786440 | tf_op jit(solution)/shard_map/ppermute | solution.py:238
  31.7 21.9 %collective-permute-start.2 = (bf16[4,128,256]{2,1,0:T(8,128)(2,1)}, bf16[4,128,256]{2,1,0:T(8,128)(2,1)S(1)}, u32[]{:S(2)}, u32[]{:S(2)}) collective-permute-start(bf16[4,128,256]{2,1,0:T(8,128)(2,1)} %get-tuple-element.43), channel_id=1, source_target_pairs={{0,2},{1,3},{2,0},{3,1},{4,6},{5,7},{6,4},{7,5},{8,10},{9,11},{10,... | collective-permute-start | bytes 786440 | tf_op jit(solution)/shard_map/ppermute | solution.py:238
  32.2 24.3 %collective-permute-start.3 = (bf16[4,128,256]{2,1,0:T(8,128)(2,1)}, bf16[4,128,256]{2,1,0:T(8,128)(2,1)S(1)}, u32[]{:S(2)}, u32[]{:S(2)}) collective-permute-start(bf16[4,128,256]{2,1,0:T(8,128)(2,1)} %get-tuple-element.44), channel_id=1, source_target_pairs={{0,4},{1,5},{2,6},{3,7},{4,0},{5,1},{6,2},{7,3},{8,12},{9,13},{10,... | collective-permute-start | bytes 786440 | tf_op jit(solution)/shard_map/ppermute | solution.py:238
  33.9 22.7 %collective-permute-start.4 = (bf16[4,128,256]{2,1,0:T(8,128)(2,1)S(1)}, bf16[4,128,256]{2,1,0:T(8,128)(2,1)S(1)}, u32[]{:S(2)}, u32[]{:S(2)}) collective-permute-start(bf16[4,128,256]{2,1,0:T(8,128)(2,1)S(1)} %copy-done.20), channel_id=1, source_target_pairs={{0,3},{1,2},{2,1},{3,0},{4,7},{5,6},{6,5},{7,4},{8,11},{9,10},{10,... | collective-permute-start | bytes 786440 | tf_op jit(solution)/shard_map/ppermute | solution.py:238
  37.7 20.1 %collective-permute-start.5 = (bf16[4,128,256]{2,1,0:T(8,128)(2,1)S(1)}, bf16[4,128,256]{2,1,0:T(8,128)(2,1)S(1)}, u32[]{:S(2)}, u32[]{:S(2)}) collective-permute-start(bf16[4,128,256]{2,1,0:T(8,128)(2,1)S(1)} %copy-done.19), channel_id=1, source_target_pairs={{0,5},{1,4},{2,7},{3,6},{4,1},{5,0},{6,3},{7,2},{8,13},{9,12},{10,... | collective-permute-start | bytes 786440 | tf_op jit(solution)/shard_map/ppermute | solution.py:238
  37.7 5.2 %copy-start.18 = (bf16[4,128,256]{2,1,0:T(8,128)(2,1)S(1)}, bf16[4,128,256]{2,1,0:T(8,128)(2,1)}, u32[]{:S(2)}) copy-start(bf16[4,128,256]{2,1,0:T(8,128)(2,1)} %get-tuple-element.47) | copy-start | bytes 786436
  37.7 5.4 %copy-start.3 = (bf16[4,128,256]{2,1,0:T(8,128)(2,1)S(1)}, bf16[4,128,256]{2,1,0:T(8,128)(2,1)}, u32[]{:S(2)}) copy-start(bf16[4,128,256]{2,1,0:T(8,128)(2,1)} %get-tuple-element.56.rest_0_) | copy-start | bytes 786436
  37.8 5.4 %copy-start.5 = (s32[8,8]{1,0:T(8,128)S(1)}, s32[8,8]{1,0:T(8,128)}, u32[]{:S(2)}) copy-start(s32[8,8]{1,0:T(8,128)} %bands_ref.3) | copy-start | bytes 772
  40.3 2.8 %copy-start.4 = (s32[8,8]{1,0:T(8,128)S(1)}, s32[8,8]{1,0:T(8,128)}, u32[]{:S(2)}) copy-start(s32[8,8]{1,0:T(8,128)} %flags_ref.3) | copy-start | bytes 772
  43.0 16.4 %collective-permute-start.6 = (bf16[4,128,256]{2,1,0:T(8,128)(2,1)S(1)}, bf16[4,128,256]{2,1,0:T(8,128)(2,1)S(1)}, u32[]{:S(2)}, u32[]{:S(2)}) collective-permute-start(bf16[4,128,256]{2,1,0:T(8,128)(2,1)S(1)} %copy-done.18), channel_id=1, source_target_pairs={{0,1},{1,0},{2,3},{3,2},{4,5},{5,4},{6,7},{7,6},{8,9},{9,8},{10,11... | collective-permute-start | bytes 786440 | tf_op jit(solution)/shard_map/ppermute | solution.py:238
  43.1 0.7 copy-start.6
  43.8 16.0 %copy-start.2 = (bf16[4,128,256]{2,1,0:T(8,128)(2,1)S(1)}, bf16[4,128,256]{2,1,0:T(8,128)(2,1)}, u32[]{:S(2)}) copy-start(bf16[4,128,256]{2,1,0:T(8,128)(2,1)} %get-tuple-element.40.rest_0_) | copy-start | bytes 786436
  52.9 0.7 copy-start
  53.6 16.2 %collective-permute-start.21 = (bf16[4,128,256]{2,1,0:T(8,128)(2,1)S(1)}, bf16[4,128,256]{2,1,0:T(8,128)(2,1)S(1)}, u32[]{:S(2)}, u32[]{:S(2)}) collective-permute-start(bf16[4,128,256]{2,1,0:T(8,128)(2,1)S(1)} %get-tuple-element.65), channel_id=1, source_target_pairs={{0,6},{1,7},{2,4},{3,5},{4,2},{5,3},{6,0},{7,1},{8,14},{9,15},{10,... | collective-permute-start | bytes 786440 | tf_op jit(solution)/shard_map/ppermute | solution.py:238
  56.6 13.9 %collective-permute-start.22 = (bf16[4,128,256]{2,1,0:T(8,128)(2,1)S(1)}, bf16[4,128,256]{2,1,0:T(8,128)(2,1)S(1)}, u32[]{:S(2)}, u32[]{:S(2)}) collective-permute-start(bf16[4,128,256]{2,1,0:T(8,128)(2,1)S(1)} %get-tuple-element.66), channel_id=1, source_target_pairs={{0,7},{1,6},{2,5},{3,4},{4,3},{5,2},{6,1},{7,0},{8,15},{9,14},{10,... | collective-permute-start | bytes 786440 | tf_op jit(solution)/shard_map/ppermute | solution.py:238
  56.6 18.9 %collective-permute-start.23 = (bf16[4,128,256]{2,1,0:T(8,128)(2,1)S(1)}, bf16[4,128,256]{2,1,0:T(8,128)(2,1)S(1)}, u32[]{:S(2)}, u32[]{:S(2)}) collective-permute-start(bf16[4,128,256]{2,1,0:T(8,128)(2,1)S(1)} %get-tuple-element.67), channel_id=1, source_target_pairs={{0,2},{1,3},{2,0},{3,1},{4,6},{5,7},{6,4},{7,5},{8,10},{9,11},{10,... | collective-permute-start | bytes 786440 | tf_op jit(solution)/shard_map/ppermute | solution.py:238
  57.9 19.1 %collective-permute-start.24 = (bf16[4,128,256]{2,1,0:T(8,128)(2,1)S(1)}, bf16[4,128,256]{2,1,0:T(8,128)(2,1)S(1)}, u32[]{:S(2)}, u32[]{:S(2)}) collective-permute-start(bf16[4,128,256]{2,1,0:T(8,128)(2,1)S(1)} %get-tuple-element.68), channel_id=1, source_target_pairs={{0,4},{1,5},{2,6},{3,7},{4,0},{5,1},{6,2},{7,3},{8,12},{9,13},{10,... | collective-permute-start | bytes 786440 | tf_op jit(solution)/shard_map/ppermute | solution.py:238
  59.4 20.8 %collective-permute-start.25 = (bf16[4,128,256]{2,1,0:T(8,128)(2,1)S(1)}, bf16[4,128,256]{2,1,0:T(8,128)(2,1)S(1)}, u32[]{:S(2)}, u32[]{:S(2)}) collective-permute-start(bf16[4,128,256]{2,1,0:T(8,128)(2,1)S(1)} %get-tuple-element.69), channel_id=1, source_target_pairs={{0,3},{1,2},{2,1},{3,0},{4,7},{5,6},{6,5},{7,4},{8,11},{9,10},{10,... | collective-permute-start | bytes 786440 | tf_op jit(solution)/shard_map/ppermute | solution.py:238
  69.1 0.7 copy-start.1
  69.8 21.9 %copy-start.7 = (bf16[4,128,256]{2,1,0:T(8,128)(2,1)}, bf16[4,128,256]{2,1,0:T(8,128)(2,1)S(1)}, u32[]{:S(2)}) copy-start(bf16[4,128,256]{2,1,0:T(8,128)(2,1)S(1)} %collective-permute-done.21.rest_1_) | copy-start | bytes 786436
  69.8 10.9 %collective-permute-start.26 = (bf16[4,128,256]{2,1,0:T(8,128)(2,1)S(1)}, bf16[4,128,256]{2,1,0:T(8,128)(2,1)S(1)}, u32[]{:S(2)}, u32[]{:S(2)}) collective-permute-start(bf16[4,128,256]{2,1,0:T(8,128)(2,1)S(1)} %get-tuple-element.70), channel_id=1, source_target_pairs={{0,5},{1,4},{2,7},{3,6},{4,1},{5,0},{6,3},{7,2},{8,13},{9,12},{10,... | collective-permute-start | bytes 786440 | tf_op jit(solution)/shard_map/ppermute | solution.py:238
  70.5 21.2 %copy-start.8 = (bf16[4,128,256]{2,1,0:T(8,128)(2,1)}, bf16[4,128,256]{2,1,0:T(8,128)(2,1)S(1)}, u32[]{:S(2)}) copy-start(bf16[4,128,256]{2,1,0:T(8,128)(2,1)S(1)} %collective-permute-done.22.rest_2_) | copy-start | bytes 786436
  70.5 12.0 %collective-permute-start.27 = (bf16[4,128,256]{2,1,0:T(8,128)(2,1)S(1)}, bf16[4,128,256]{2,1,0:T(8,128)(2,1)S(1)}, u32[]{:S(2)}, u32[]{:S(2)}) collective-permute-start(bf16[4,128,256]{2,1,0:T(8,128)(2,1)S(1)} %get-tuple-element.71), channel_id=1, source_target_pairs={{0,1},{1,0},{2,3},{3,2},{4,5},{5,4},{6,7},{7,6},{8,9},{9,8},{10,11... | collective-permute-start | bytes 786440 | tf_op jit(solution)/shard_map/ppermute | solution.py:238
  75.5 16.2 %copy-start.9 = (bf16[4,128,256]{2,1,0:T(8,128)(2,1)}, bf16[4,128,256]{2,1,0:T(8,128)(2,1)S(1)}, u32[]{:S(2)}) copy-start(bf16[4,128,256]{2,1,0:T(8,128)(2,1)S(1)} %collective-permute-done.23.rest_3_) | copy-start | bytes 786436
  75.5 10.8 %collective-permute-start.7 = (bf16[4,128,256]{2,1,0:T(8,128)(2,1)S(1)}, bf16[4,128,256]{2,1,0:T(8,128)(2,1)S(1)}, u32[]{:S(2)}, u32[]{:S(2)}) collective-permute-start(bf16[4,128,256]{2,1,0:T(8,128)(2,1)S(1)} %get-tuple-element.49), channel_id=1, source_target_pairs={{0,6},{1,7},{2,4},{3,5},{4,2},{5,3},{6,0},{7,1},{8,14},{9,15},{10,... | collective-permute-start | bytes 786440 | tf_op jit(solution)/shard_map/ppermute | solution.py:238
  77.0 14.7 %copy-start.10 = (bf16[4,128,256]{2,1,0:T(8,128)(2,1)}, bf16[4,128,256]{2,1,0:T(8,128)(2,1)S(1)}, u32[]{:S(2)}) copy-start(bf16[4,128,256]{2,1,0:T(8,128)(2,1)S(1)} %collective-permute-done.24.rest_4_) | copy-start | bytes 786436
  77.0 14.5 %collective-permute-start.8 = (bf16[4,128,256]{2,1,0:T(8,128)(2,1)S(1)}, bf16[4,128,256]{2,1,0:T(8,128)(2,1)S(1)}, u32[]{:S(2)}, u32[]{:S(2)}) collective-permute-start(bf16[4,128,256]{2,1,0:T(8,128)(2,1)S(1)} %get-tuple-element.50), channel_id=1, source_target_pairs={{0,7},{1,6},{2,5},{3,4},{4,3},{5,2},{6,1},{7,0},{8,15},{9,14},{10,... | collective-permute-start | bytes 786440 | tf_op jit(solution)/shard_map/ppermute | solution.py:238
  80.2 11.5 %copy-start.11 = (bf16[4,128,256]{2,1,0:T(8,128)(2,1)}, bf16[4,128,256]{2,1,0:T(8,128)(2,1)S(1)}, u32[]{:S(2)}) copy-start(bf16[4,128,256]{2,1,0:T(8,128)(2,1)S(1)} %collective-permute-done.25.rest_5_) | copy-start | bytes 786436
  80.2 17.9 %collective-permute-start.9 = (bf16[4,128,256]{2,1,0:T(8,128)(2,1)S(1)}, bf16[4,128,256]{2,1,0:T(8,128)(2,1)S(1)}, u32[]{:S(2)}, u32[]{:S(2)}) collective-permute-start(bf16[4,128,256]{2,1,0:T(8,128)(2,1)S(1)} %get-tuple-element.51), channel_id=1, source_target_pairs={{0,2},{1,3},{2,0},{3,1},{4,6},{5,7},{6,4},{7,5},{8,10},{9,11},{10,... | collective-permute-start | bytes 786440 | tf_op jit(solution)/shard_map/ppermute | solution.py:238
  80.7 10.9 %copy-start.15 = (bf16[4,128,256]{2,1,0:T(8,128)(2,1)}, bf16[4,128,256]{2,1,0:T(8,128)(2,1)S(1)}, u32[]{:S(2)}) copy-start(bf16[4,128,256]{2,1,0:T(8,128)(2,1)S(1)} %collective-permute-done.26.rest_6_) | copy-start | bytes 786436
  80.7 17.3 %collective-permute-start.10 = (bf16[4,128,256]{2,1,0:T(8,128)(2,1)S(1)}, bf16[4,128,256]{2,1,0:T(8,128)(2,1)}, u32[]{:S(2)}, u32[]{:S(2)}) collective-permute-start(bf16[4,128,256]{2,1,0:T(8,128)(2,1)S(1)} %get-tuple-element.52), channel_id=1, source_target_pairs={{0,4},{1,5},{2,6},{3,7},{4,0},{5,1},{6,2},{7,3},{8,12},{9,13},{10,... | collective-permute-start | bytes 786440 | tf_op jit(solution)/shard_map/ppermute | solution.py:238
  82.4 9.2 %copy-start.16 = (bf16[4,128,256]{2,1,0:T(8,128)(2,1)}, bf16[4,128,256]{2,1,0:T(8,128)(2,1)S(1)}, u32[]{:S(2)}) copy-start(bf16[4,128,256]{2,1,0:T(8,128)(2,1)S(1)} %collective-permute-done.27.rest_7_) | copy-start | bytes 786436
  82.4 19.4 %collective-permute-start.11 = (bf16[4,128,256]{2,1,0:T(8,128)(2,1)S(1)}, bf16[4,128,256]{2,1,0:T(8,128)(2,1)}, u32[]{:S(2)}, u32[]{:S(2)}) collective-permute-start(bf16[4,128,256]{2,1,0:T(8,128)(2,1)S(1)} %get-tuple-element.53), channel_id=1, source_target_pairs={{0,3},{1,2},{2,1},{3,0},{4,7},{5,6},{6,5},{7,4},{8,11},{9,10},{10,... | collective-permute-start | bytes 786440 | tf_op jit(solution)/shard_map/ppermute | solution.py:238
  86.3 8.5 %copy-start.12 = (bf16[4,128,256]{2,1,0:T(8,128)(2,1)}, bf16[4,128,256]{2,1,0:T(8,128)(2,1)S(1)}, u32[]{:S(2)}) copy-start(bf16[4,128,256]{2,1,0:T(8,128)(2,1)S(1)} %collective-permute-done.7.rest_1_) | copy-start | bytes 786436
  86.3 16.3 %collective-permute-start.12 = (bf16[4,128,256]{2,1,0:T(8,128)(2,1)S(1)}, bf16[4,128,256]{2,1,0:T(8,128)(2,1)}, u32[]{:S(2)}, u32[]{:S(2)}) collective-permute-start(bf16[4,128,256]{2,1,0:T(8,128)(2,1)S(1)} %get-tuple-element.54), channel_id=1, source_target_pairs={{0,5},{1,4},{2,7},{3,6},{4,1},{5,0},{6,3},{7,2},{8,13},{9,12},{10,... | collective-permute-start | bytes 786440 | tf_op jit(solution)/shard_map/ppermute | solution.py:238
  91.4 3.4 %copy-start.13 = (bf16[4,128,256]{2,1,0:T(8,128)(2,1)}, bf16[4,128,256]{2,1,0:T(8,128)(2,1)S(1)}, u32[]{:S(2)}) copy-start(bf16[4,128,256]{2,1,0:T(8,128)(2,1)S(1)} %collective-permute-done.8.rest_2_) | copy-start | bytes 786436
  91.4 11.1 %collective-permute-start.13 = (bf16[4,128,256]{2,1,0:T(8,128)(2,1)S(1)}, bf16[4,128,256]{2,1,0:T(8,128)(2,1)}, u32[]{:S(2)}, u32[]{:S(2)}) collective-permute-start(bf16[4,128,256]{2,1,0:T(8,128)(2,1)S(1)} %get-tuple-element.55), channel_id=1, source_target_pairs={{0,1},{1,0},{2,3},{3,2},{4,5},{5,4},{6,7},{7,6},{8,9},{9,8},{10,11... | collective-permute-start | bytes 786440 | tf_op jit(solution)/shard_map/ppermute | solution.py:238
  98.0 4.5 %copy-start.14 = (bf16[4,128,256]{2,1,0:T(8,128)(2,1)}, bf16[4,128,256]{2,1,0:T(8,128)(2,1)S(1)}, u32[]{:S(2)}) copy-start(bf16[4,128,256]{2,1,0:T(8,128)(2,1)S(1)} %collective-permute-done.9.rest_3_) | copy-start | bytes 786436

commit v2 on v1

--- a/solution.py
+++ b/solution.py
@@ -13,6 +13,10 @@
 BLK = 128
 NTK = 2.0
 CHUNKS = 2
+AHEAD = 5
+SMALL = 8 * 1024 * 1024
+FIRST_CUTS = (0,)
+LAST_CUTS = (0,)
 LIMIT = 40 * 1024 * 1024
 
 F32 = jnp.float32
@@ -233,42 +237,70 @@
     piece = jax.ShapeDtypeStruct((4, rows, count * DH), BF16)
     hops = tuple(sorted(range(groups), key=lambda d: (d > 0, -(d >> 1).bit_count(), d & 1, d)))
 
-    def exchange(pieces):
-        return [pieces[0]] + [
-            lax.ppermute(piece, "seq", [(i, i ^ d) for i in range(groups)])
-            for piece, d in zip(pieces[1:], hops[1:])
+    def exchange(pieces, start=0):
+        return [
+            lax.ppermute(piece, "seq", [(i, i ^ d) for i in range(groups)]) if d else piece
+            for piece, d in zip(pieces, hops[start:])
         ]
 
-    def pack(c):
+    def pack(c, slots):
         return pl.pallas_call(
-            functools.partial(pack_kernel, hops, heads, c * count, count),
-            out_shape=[piece] * groups,
+            functools.partial(pack_kernel, hops[slots], heads, c * count, count),
+            out_shape=[piece] * len(hops[slots]),
             in_specs=[SMEM] + [ANY] * 4,
-            out_specs=[VMEM] * groups,
-            scratch_shapes=[pltpu.SemaphoreType.DMA((groups, 4))],
-            name=f"pack_{c}",
+            out_specs=[VMEM] * len(hops[slots]),
+            scratch_shapes=[pltpu.SemaphoreType.DMA((len(hops[slots]), 4))],
+            name=f"pack_{c}_{slots.start}",
         )(me, *arrays)
 
-    def unpack(c, pieces, before):
-        kept = len(before)
+    def unpack(c, slots, pieces, before):
+        kept, own = len(before), len(hops[slots])
         return pl.pallas_call(
-            functools.partial(unpack_kernel, hops, heads, c * count, count, kept),
+            functools.partial(unpack_kernel, hops[slots], heads, c * count, count, kept),
             out_shape=[jax.ShapeDtypeStruct((rows, channels), BF16)] * 4,
-            in_specs=[SMEM] + [VMEM] * groups + [ANY] * kept,
+            in_specs=[SMEM] + [VMEM] * own + [ANY] * kept,
             out_specs=[ANY] * 4,
-            input_output_aliases={1 + groups + a: a for a in range(kept)},
-            scratch_shapes=[pltpu.SemaphoreType.DMA((groups, 4))],
-            name=f"unpack_{c}",
-        )(me, *pieces, *before)
+            input_output_aliases={1 + own + a: a for a in range(kept)},
+            scratch_shapes=[pltpu.SemaphoreType.DMA((own, 4))],
+            compiler_params=pltpu.CompilerParams(vmem_limit_bytes=SMALL),
+            name=f"unpack_{c}_{slots.start}",
+        )(me, *pieces[slots], *before)
+
+    def after(pieces, others):
+        both = lax.optimization_barrier((*pieces, *others))
+        return list(both[: len(pieces)]), list(both[len(pieces) :])
 
     tables = rope_tables(positions)
-    arrived = [exchange(pack(c)) for c in range(chunks)]
+    packed = [
+        [p for lo, hi in zip(cuts, cuts[1:]) for p in pack(c, slice(lo, hi))]
+        for c, cuts in enumerate([FIRST_CUTS + (groups,)] + [(0, groups)] * (chunks - 1))
+    ]
+    near = AHEAD + 1
+    if chunks > 1:
+        packed[1], tables = after(packed[1], tables)
+    arrived = [exchange(packed[0])]
+    turned = []
+    for c in range(chunks):
+        pending = packed[c + 1] if c + 1 < chunks else turned[-1] if turned else []
+        head = exchange(pending[:near])
+        new = attention_call(hops, count, me, block_flags, band_ids, tables, arrived[c])
+        tail, new = pending[near:], list(new)
+        if c + 1 < chunks:
+            tail, new = after(tail, new)
+        moved = head + exchange(tail, near)
+        if c + 1 < chunks:
+            arrived.append(moved)
+            if c:
+                turned[-1] = exchange(turned[-1])
+        elif turned:
+            turned[-1] = moved
+        turned.append(new)
+    turned[-1] = exchange(turned[-1])
     results = ()
     for c in range(chunks):
-        turned = exchange(
-            attention_call(hops, count, me, block_flags, band_ids, tables, arrived[c])
-        )
-        results = unpack(c, turned, results)
+        cuts = LAST_CUTS if c + 1 == chunks else (0,)
+        for lo, hi in zip(cuts, cuts[1:] + (groups,)):
+            results = unpack(c, slice(lo, hi), turned[c], results)
     return tuple(results)
 
 

time: 106 us -> 101 us (0.953)
  Pallas kernels: 31.1 us -> 28 us
  local copies, waits for them, and re-layouts: 2.1 us -> 0.07 us
    pallas_call x4, Pallas kernels: 12.6 us -> 9.53 us  [the longest x2 6.39 us: pack(): pl.pallas_call(functools.partial(pack_kernel, hops[slots], heads, c * cou...]
    unnamed x46 -> x26, local copies, waits for them, and re-layouts: 2.1 us -> 0.07 us
where the time goes in v2:
time: 101 us; the launch traced here: 100 us
  waiting for transfers between devices  43.6 us (43%)
  Pallas kernels  28 us (28%)
  starting transfers between devices  24.8 us (25%)
  other arithmetic  2.92 us (3%)
  between operations  1.03 us (1%)
    ppermute x28, waiting for transfers between devices, exchange(): lax.ppermute(piece, 'seq', [(i, i ^ d) for i in range(groups)])  43.6 us
    ppermute x28, starting transfers between devices, exchange(): lax.ppermute(piece, 'seq', [(i, i ^ d) for i in range(groups)])  24.8 us
    pallas_call x2, Pallas kernels, attention_call(): pl.pallas_call(functools.partial(attention_kernel, hops, rows, count, wid...  18.5 us
    pallas_call x2, Pallas kernels, pack(): pl.pallas_call(functools.partial(pack_kernel, hops[slots], heads, c * cou...  6.39 us
    pallas_call x2, Pallas kernels, unpack(): pl.pallas_call(functools.partial(unpack_kernel, hops[slots], heads, c * c...  3.13 us
    mul x1, other arithmetic, rope_tables(): return (jnp.cos(angle), jnp.sin(angle) * sign[None, :])  2.35 us
  transfers between devices with their start and end apart: 28, of which 13 were waited for; matrix products, arithmetic and copies ran while one was open for 3% of the time, Pallas kernels for 23%

profile of v2, /device:TPU:0, one launch (start us, length us, event | category | flops | bytes accessed | tf_op | source)
XLA Modules:
  0.0 100.4 jit_solution(17364713942374812349)
XLA Ops:
  0.6 3.2 %pack_0_0.1 = (bf16[4,128,256]{2,1,0:T(8,128)(2,1)}, bf16[4,128,256]{2,1,0:T(8,128)(2,1)}, bf16[4,128,256]{2,1,0:T(8,128)(2,1)}, bf16[4,128,256]{2,1,0:T(8,128)(...) custom-call(s32[1]{0:T(128)} %bitcast.me_ref, ...), custom_call_target="tpu_custom_call" | custom-call | tf_op jit(solution)/shard_map/pack_0_0/pallas_call | solution.py:247
  3.8 4.0 %collective-permute-start.5 = (bf16[4,128,256]{2,1,0:T(8,128)(2,1)}, bf16[4,128,256]{2,1,0:T(8,128)(2,1)S(1)}, u32[]{:S(2)}, u32[]{:S(2)}) collective-permute-start(bf16[4,128,256]{2,1,0:T(8,128)(2,1)} %get-tuple-element.79), channel_id=1, source_target_pairs={{0,6},{1,7},{2,4},{3,5},{4,2},{5,3},{6,0},{7,1},{8,14},{9,15},{10,... | collective-permute-start | bytes 786440 | tf_op jit(solution)/shard_map/ppermute | solution.py:242
  7.8 0.0 collective-permute-start.6
  7.8 1.1 %collective-permute-start.7 = (bf16[4,128,256]{2,1,0:T(8,128)(2,1)}, bf16[4,128,256]{2,1,0:T(8,128)(2,1)S(1)}, u32[]{:S(2)}, u32[]{:S(2)}) collective-permute-start(bf16[4,128,256]{2,1,0:T(8,128)(2,1)} %get-tuple-element.81), channel_id=1, source_target_pairs={{0,2},{1,3},{2,0},{3,1},{4,6},{5,7},{6,4},{7,5},{8,10},{9,11},{10,... | collective-permute-start | bytes 786440 | tf_op jit(solution)/shard_map/ppermute | solution.py:242
  8.9 1.5 %collective-permute-start.8 = (bf16[4,128,256]{2,1,0:T(8,128)(2,1)}, bf16[4,128,256]{2,1,0:T(8,128)(2,1)S(1)}, u32[]{:S(2)}, u32[]{:S(2)}) collective-permute-start(bf16[4,128,256]{2,1,0:T(8,128)(2,1)} %get-tuple-element.82), channel_id=1, source_target_pairs={{0,4},{1,5},{2,6},{3,7},{4,0},{5,1},{6,2},{7,3},{8,12},{9,13},{10,... | collective-permute-start | bytes 786440 | tf_op jit(solution)/shard_map/ppermute | solution.py:242
  10.5 0.6 collective-permute-start.9
  11.1 0.2 broadcast_multiply_fusion.2
  11.3 0.3 broadcast_multiply_fusion.1
  11.6 3.6 %collective-permute-done.5.rest_1_ = bf16[4,128,256]{2,1,0:T(8,128)(2,1)S(1)} collective-permute-done((bf16[4,128,256]{2,1,0:T(8,128)(2,1)}, bf16[4,128,256]{2,1,0:T(8,128)(2,1)S(1)}, u32[]{:S(2)}, u32[]{:S(2)}) %collective-permute-start.5) | collective-permute-done | bytes 262176 | tf_op jit(solution)/shard_map/ppermute | solution.py:242
  15.2 0.0 collective-permute-start.10
  15.3 5.2 %collective-permute-done.6.rest_2_ = bf16[4,128,256]{2,1,0:T(8,128)(2,1)S(1)} collective-permute-done((bf16[4,128,256]{2,1,0:T(8,128)(2,1)}, bf16[4,128,256]{2,1,0:T(8,128)(2,1)S(1)}, u32[]{:S(2)}, u32[]{:S(2)}) %collective-permute-start.6) | collective-permute-done | bytes 262176 | tf_op jit(solution)/shard_map/ppermute | solution.py:242
  20.5 0.1 collective-permute-start.11
  20.6 3.2 %pack_1_0.1 = (bf16[4,128,256]{2,1,0:T(8,128)(2,1)}, bf16[4,128,256]{2,1,0:T(8,128)(2,1)}, bf16[4,128,256]{2,1,0:T(8,128)(2,1)}, bf16[4,128,256]{2,1,0:T(8,128)(...) custom-call(s32[1]{0:T(128)} %bitcast.me_ref, ...), custom_call_target="tpu_custom_call" | custom-call | tf_op jit(solution)/shard_map/pack_1_0/pallas_call | solution.py:247
  23.8 0.0 copy-start.12
  23.9 0.0 copy-start.11
  23.9 0.0 copy-start.10
  23.9 2.4 %sine_multiply_fusion = (f32[1024,128]{1,0:T(8,128)S(1)}, f32[1024,128]{1,0:T(8,128)S(1)}) fusion(f32[128]{0:T(128)S(1)} %compare_select_fusion, f32[1024,42]{1,0:T(8,128)S(1)} %get-tuple-element.122, f32[1024,42]{1,0:T(8,128)S(1)} %get-tuple-element.121, f32[1024,44]{1,0:T(8,128)S(1)} %broadcast_multiply_fusion.2), kind=kLoop, calls=%fused_computation.1 | loop fusion | flops 393216 | bytes 1573376 | tf_op jit(solution)/shard_map/mul | solution.py:38
  26.3 0.0 copy-start.3
  26.3 0.0 copy-start.2
  26.3 0.0 copy-start.4
  26.3 0.7 collective-permute-done.7.rest_3_
  27.0 2.4 %collective-permute-start = (bf16[4,128,256]{2,1,0:T(8,128)(2,1)S(1)}, bf16[4,128,256]{2,1,0:T(8,128)(2,1)S(1)}, u32[]{:S(2)}, u32[]{:S(2)}) collective-permute-start(bf16[4,128,256]{2,1,0:T(8,128)(2,1)S(1)} %copy-done.12), channel_id=1, source_target_pairs={{0,6},{1,7},{2,4},{3,5},{4,2},{5,3},{6,0},{7,1},{8,14},{9,15},{10,... | collective-permute-start | bytes 786440 | tf_op jit(solution)/shard_map/ppermute | solution.py:242
  29.4 0.0 collective-permute-done.8.rest_4_
  29.4 0.0 collective-permute-start.1
  29.4 2.2 %collective-permute-done.9.rest_5_ = bf16[4,128,256]{2,1,0:T(8,128)(2,1)S(1)} collective-permute-done((bf16[4,128,256]{2,1,0:T(8,128)(2,1)}, bf16[4,128,256]{2,1,0:T(8,128)(2,1)S(1)}, u32[]{:S(2)}, u32[]{:S(2)}) %collective-permute-start.9) | collective-permute-done | bytes 262176 | tf_op jit(solution)/shard_map/ppermute | solution.py:242
  31.5 0.5 collective-permute-start.2
  32.1 0.0 collective-permute-done.10.rest_6_
  32.1 1.7 %collective-permute-start.3 = (bf16[4,128,256]{2,1,0:T(8,128)(2,1)S(1)}, bf16[4,128,256]{2,1,0:T(8,128)(2,1)S(1)}, u32[]{:S(2)}, u32[]{:S(2)}) collective-permute-start(bf16[4,128,256]{2,1,0:T(8,128)(2,1)S(1)} %copy-done.9), channel_id=1, source_target_pairs={{0,4},{1,5},{2,6},{3,7},{4,0},{5,1},{6,2},{7,3},{8,12},{9,13},{10,... | collective-permute-start | bytes 786440 | tf_op jit(solution)/shard_map/ppermute | solution.py:242
  33.7 0.0 collective-permute-done.11.rest_7_
  33.7 0.9 collective-permute-start.4
  34.7 0.0 copy-start
  34.7 9.1 %attention.2 = (bf16[4,128,256]{2,1,0:T(8,128)(2,1)S(1)}, bf16[4,128,256]{2,1,0:T(8,128)(2,1)S(1)}, bf16[4,128,256]{2,1,0:T(8,128)(2,1)S(1)}, bf16[4,128,256]{2,...) custom-call(s32[1]{0:T(128)} %bitcast.me_ref, ...), custom_call_target="tpu_custom_call" | custom-call | flops 2684354560 | bytes 4194304 | tf_op jit(solution)/shard_map/attention/pallas_call | solution.py:208
  43.9 0.0 collective-permute-done.rest_1_
  43.9 0.7 collective-permute-start.12
  44.6 0.0 collective-permute-done.1.rest_2_
  44.6 0.4 collective-permute-start.13
  45.1 4.2 %collective-permute-done.2.rest_3_ = bf16[4,128,256]{2,1,0:T(8,128)(2,1)S(1)} collective-permute-done((bf16[4,128,256]{2,1,0:T(8,128)(2,1)S(1)}, bf16[4,128,256]{2,1,0:T(8,128)(2,1)S(1)}, u32[]{:S(2)}, u32[]{:S(2)}) %collective-permute-start.2) | collective-permute-done | bytes 262176 | tf_op jit(solution)/shard_map/ppermute | solution.py:242
  49.3 1.4 %collective-permute-start.21 = (bf16[4,128,256]{2,1,0:T(8,128)(2,1)S(1)}, bf16[4,128,256]{2,1,0:T(8,128)(2,1)S(1)}, u32[]{:S(2)}, u32[]{:S(2)}) collective-permute-start(bf16[4,128,256]{2,1,0:T(8,128)(2,1)S(1)} %get-tuple-element.105), channel_id=1, source_target_pairs={{0,6},{1,7},{2,4},{3,5},{4,2},{5,3},{6,0},{7,1},{8,14},{9,15},{10,... | collective-permute-start | bytes 786440 | tf_op jit(solution)/shard_map/ppermute | solution.py:242
  50.7 0.0 collective-permute-done.3.rest_4_
  50.7 0.0 collective-permute-start.22
  50.7 3.2 %collective-permute-done.4.rest_5_ = bf16[4,128,256]{2,1,0:T(8,128)(2,1)S(1)} collective-permute-done((bf16[4,128,256]{2,1,0:T(8,128)(2,1)S(1)}, bf16[4,128,256]{2,1,0:T(8,128)(2,1)S(1)}, u32[]{:S(2)}, u32[]{:S(2)}) %collective-permute-start.4) | collective-permute-done | bytes 262176 | tf_op jit(solution)/shard_map/ppermute | solution.py:242
  53.9 0.6 collective-permute-start.23
  54.5 0.0 collective-permute-done.12.rest_6_
  54.5 1.7 %collective-permute-start.24 = (bf16[4,128,256]{2,1,0:T(8,128)(2,1)S(1)}, bf16[4,128,256]{2,1,0:T(8,128)(2,1)S(1)}, u32[]{:S(2)}, u32[]{:S(2)}) collective-permute-start(bf16[4,128,256]{2,1,0:T(8,128)(2,1)S(1)} %get-tuple-element.108), channel_id=1, source_target_pairs={{0,4},{1,5},{2,6},{3,7},{4,0},{5,1},{6,2},{7,3},{8,12},{9,13},{10,... | collective-permute-start | bytes 786440 | tf_op jit(solution)/shard_map/ppermute | solution.py:242
  56.2 0.9 collective-permute-start.25
  57.1 9.3 %attention.3 = (bf16[4,128,256]{2,1,0:T(8,128)(2,1)S(1)}, bf16[4,128,256]{2,1,0:T(8,128)(2,1)S(1)}, bf16[4,128,256]{2,1,0:T(8,128)(2,1)S(1)}, bf16[4,128,256]{2,...) custom-call(s32[1]{0:T(128)} %bitcast.me_ref, ...), custom_call_target="tpu_custom_call" | custom-call | flops 2684354560 | bytes 4194304 | tf_op jit(solution)/shard_map/attention/pallas_call | solution.py:208
  66.4 1.0 collective-permute-start.26
  67.4 0.3 collective-permute-start.27
  67.7 4.2 %collective-permute-done.23.rest_3_ = bf16[4,128,256]{2,1,0:T(8,128)(2,1)S(1)} collective-permute-done((bf16[4,128,256]{2,1,0:T(8,128)(2,1)S(1)}, bf16[4,128,256]{2,1,0:T(8,128)(2,1)S(1)}, u32[]{:S(2)}, u32[]{:S(2)}) %collective-permute-start.23) | collective-permute-done | bytes 262176 | tf_op jit(solution)/shard_map/ppermute | solution.py:242
  71.8 1.4 %collective-permute-start.14 = (bf16[4,128,256]{2,1,0:T(8,128)(2,1)S(1)}, bf16[4,128,256]{2,1,0:T(8,128)(2,1)S(1)}, u32[]{:S(2)}, u32[]{:S(2)}) collective-permute-start(bf16[4,128,256]{2,1,0:T(8,128)(2,1)S(1)} %get-tuple-element.97), channel_id=1, source_target_pairs={{0,6},{1,7},{2,4},{3,5},{4,2},{5,3},{6,0},{7,1},{8,14},{9,15},{10,... | collective-permute-start | bytes 786440 | tf_op jit(solution)/shard_map/ppermute | solution.py:242
  73.3 3.2 %collective-permute-done.25.rest_5_ = bf16[4,128,256]{2,1,0:T(8,128)(2,1)S(1)} collective-permute-done((bf16[4,128,256]{2,1,0:T(8,128)(2,1)S(1)}, bf16[4,128,256]{2,1,0:T(8,128)(2,1)S(1)}, u32[]{:S(2)}, u32[]{:S(2)}) %collective-permute-start.25) | collective-permute-done | bytes 262176 | tf_op jit(solution)/shard_map/ppermute | solution.py:242
  76.4 0.6 collective-permute-start.16
  77.0 1.7 %collective-permute-start.17 = (bf16[4,128,256]{2,1,0:T(8,128)(2,1)S(1)}, bf16[4,128,256]{2,1,0:T(8,128)(2,1)S(1)}, u32[]{:S(2)}, u32[]{:S(2)}) collective-permute-start(bf16[4,128,256]{2,1,0:T(8,128)(2,1)S(1)} %get-tuple-element.100), channel_id=1, source_target_pairs={{0,4},{1,5},{2,6},{3,7},{4,0},{5,1},{6,2},{7,3},{8,12},{9,13},{10,... | collective-permute-start | bytes 786440 | tf_op jit(solution)/shard_map/ppermute | solution.py:242
  78.7 0.0 collective-permute-done.27.rest_7_
  78.7 0.8 collective-permute-start.18
  79.6 3.2 %collective-permute-done.14.rest_1_ = bf16[4,128,256]{2,1,0:T(8,128)(2,1)S(1)} collective-permute-done((bf16[4,128,256]{2,1,0:T(8,128)(2,1)S(1)}, bf16[4,128,256]{2,1,0:T(8,128)(2,1)S(1)}, u32[]{:S(2)}, u32[]{:S(2)}) %collective-permute-start.14) | collective-permute-done | bytes 262176 | tf_op jit(solution)/shard_map/ppermute | solution.py:242
  82.8 0.0 collective-permute-start.19
  82.8 4.9 %collective-permute-done.15.rest_2_ = bf16[4,128,256]{2,1,0:T(8,128)(2,1)S(1)} collective-permute-done((bf16[4,128,256]{2,1,0:T(8,128)(2,1)S(1)}, bf16[4,128,256]{2,1,0:T(8,128)(2,1)S(1)}, u32[]{:S(2)}, u32[]{:S(2)}) %collective-permute-start.15) | collective-permute-done | bytes 262176 | tf_op jit(solution)/shard_map/ppermute | solution.py:242
  87.7 0.5 collective-permute-start.20
  88.2 1.6 %unpack_0_0.1 = (bf16[128,4096]{1,0:T(8,128)(2,1)}, bf16[128,4096]{1,0:T(8,128)(2,1)}, bf16[128,4096]{1,0:T(8,128)(2,1)}, bf16[128,4096]{1,0:T(8,128)(2,1)}) custom-call(s32[1]{0:T(128)} %bitcast.me_ref, bf16[4,128,256]{2,1,0:T(8,128)(2,1)S(1)} %get-tuple-element.104.rest_0_, bf16[4,128,256]{2,1,0:T(8,128)(2,1)S(1)} %collective-permute-done.21.rest_1_, ...), custom_call_target="tpu_custom_call" | custom-call | tf_op jit(solution)/shard_map/unpack_0_0/pallas_call | solution.py:258
  89.7 4.6 %collective-permute-done.16.rest_3_ = bf16[4,128,256]{2,1,0:T(8,128)(2,1)S(1)} collective-permute-done((bf16[4,128,256]{2,1,0:T(8,128)(2,1)S(1)}, bf16[4,128,256]{2,1,0:T(8,128)(2,1)S(1)}, u32[]{:S(2)}, u32[]{:S(2)}) %collective-permute-start.16) | collective-permute-done | bytes 262176 | tf_op jit(solution)/shard_map/ppermute | solution.py:242
  94.3 3.7 %collective-permute-done.18.rest_5_ = bf16[4,128,256]{2,1,0:T(8,128)(2,1)S(1)} collective-permute-done((bf16[4,128,256]{2,1,0:T(8,128)(2,1)S(1)}, bf16[4,128,256]{2,1,0:T(8,128)(2,1)S(1)}, u32[]{:S(2)}, u32[]{:S(2)}) %collective-permute-start.18) | collective-permute-done | bytes 262176 | tf_op jit(solution)/shard_map/ppermute | solution.py:242
  98.1 0.7 collective-permute-done.19.rest_6_
  98.7 1.6 %unpack_1_0.1 = (bf16[128,4096]{1,0:T(8,128)(2,1)}, bf16[128,4096]{1,0:T(8,128)(2,1)}, bf16[128,4096]{1,0:T(8,128)(2,1)}, bf16[128,4096]{1,0:T(8,128)(2,1)}) custom-call(s32[1]{0:T(128)} %bitcast.me_ref, bf16[4,128,256]{2,1,0:T(8,128)(2,1)S(1)} %get-tuple-element.96.rest_0_, ...), custom_call_target="tpu_custom_call", output_to_operand_aliasing={{0}: (9, {}), {1}: (10, {}), {2}: (11, {}), {3}: (12, {})} | custom-call | tf_op jit(solution)/shard_map/unpack_1_0/pallas_call | solution.py:258
  (31 shorter events, 0.1 us)
Async XLA Ops:
  0.6 10.4 %copy-start.5 = (s32[3,1024]{1,0:T(4,128)S(1)}, s32[3,1024]{1,0:T(4,128)}, u32[]{:S(2)}) copy-start(s32[3,1024]{1,0:T(4,128)} %param.13) | copy-start | bytes 36868
  3.8 11.4 %collective-permute-start.5 = (bf16[4,128,256]{2,1,0:T(8,128)(2,1)}, bf16[4,128,256]{2,1,0:T(8,128)(2,1)S(1)}, u32[]{:S(2)}, u32[]{:S(2)}) collective-permute-start(bf16[4,128,256]{2,1,0:T(8,128)(2,1)} %get-tuple-element.79), channel_id=1, source_target_pairs={{0,6},{1,7},{2,4},{3,5},{4,2},{5,3},{6,0},{7,1},{8,14},{9,15},{10,... | collective-permute-start | bytes 786440 | tf_op jit(solution)/shard_map/ppermute | solution.py:242
  7.8 12.7 %collective-permute-start.6 = (bf16[4,128,256]{2,1,0:T(8,128)(2,1)}, bf16[4,128,256]{2,1,0:T(8,128)(2,1)S(1)}, u32[]{:S(2)}, u32[]{:S(2)}) collective-permute-start(bf16[4,128,256]{2,1,0:T(8,128)(2,1)} %get-tuple-element.80), channel_id=1, source_target_pairs={{0,7},{1,6},{2,5},{3,4},{4,3},{5,2},{6,1},{7,0},{8,15},{9,14},{10,... | collective-permute-start | bytes 786440 | tf_op jit(solution)/shard_map/ppermute | solution.py:242
  7.8 19.2 %collective-permute-start.7 = (bf16[4,128,256]{2,1,0:T(8,128)(2,1)}, bf16[4,128,256]{2,1,0:T(8,128)(2,1)S(1)}, u32[]{:S(2)}, u32[]{:S(2)}) collective-permute-start(bf16[4,128,256]{2,1,0:T(8,128)(2,1)} %get-tuple-element.81), channel_id=1, source_target_pairs={{0,2},{1,3},{2,0},{3,1},{4,6},{5,7},{6,4},{7,5},{8,10},{9,11},{10,... | collective-permute-start | bytes 786440 | tf_op jit(solution)/shard_map/ppermute | solution.py:242
  8.9 20.4 %collective-permute-start.8 = (bf16[4,128,256]{2,1,0:T(8,128)(2,1)}, bf16[4,128,256]{2,1,0:T(8,128)(2,1)S(1)}, u32[]{:S(2)}, u32[]{:S(2)}) collective-permute-start(bf16[4,128,256]{2,1,0:T(8,128)(2,1)} %get-tuple-element.82), channel_id=1, source_target_pairs={{0,4},{1,5},{2,6},{3,7},{4,0},{5,1},{6,2},{7,3},{8,12},{9,13},{10,... | collective-permute-start | bytes 786440 | tf_op jit(solution)/shard_map/ppermute | solution.py:242
  10.5 21.1 %collective-permute-start.9 = (bf16[4,128,256]{2,1,0:T(8,128)(2,1)}, bf16[4,128,256]{2,1,0:T(8,128)(2,1)S(1)}, u32[]{:S(2)}, u32[]{:S(2)}) collective-permute-start(bf16[4,128,256]{2,1,0:T(8,128)(2,1)} %get-tuple-element.83), channel_id=1, source_target_pairs={{0,3},{1,2},{2,1},{3,0},{4,7},{5,6},{6,5},{7,4},{8,11},{9,10},{10,... | collective-permute-start | bytes 786440 | tf_op jit(solution)/shard_map/ppermute | solution.py:242
  15.2 16.8 %collective-permute-start.10 = (bf16[4,128,256]{2,1,0:T(8,128)(2,1)}, bf16[4,128,256]{2,1,0:T(8,128)(2,1)S(1)}, u32[]{:S(2)}, u32[]{:S(2)}) collective-permute-start(bf16[4,128,256]{2,1,0:T(8,128)(2,1)} %get-tuple-element.84), channel_id=1, source_target_pairs={{0,5},{1,4},{2,7},{3,6},{4,1},{5,0},{6,3},{7,2},{8,13},{9,12},{10,... | collective-permute-start | bytes 786440 | tf_op jit(solution)/shard_map/ppermute | solution.py:242
  20.5 13.2 %collective-permute-start.11 = (bf16[4,128,256]{2,1,0:T(8,128)(2,1)}, bf16[4,128,256]{2,1,0:T(8,128)(2,1)S(1)}, u32[]{:S(2)}, u32[]{:S(2)}) collective-permute-start(bf16[4,128,256]{2,1,0:T(8,128)(2,1)} %get-tuple-element.85), channel_id=1, source_target_pairs={{0,1},{1,0},{2,3},{3,2},{4,5},{5,4},{6,7},{7,6},{8,9},{9,8},{10,11... | collective-permute-start | bytes 786440 | tf_op jit(solution)/shard_map/ppermute | solution.py:242
  23.8 3.2 %copy-start.12 = (bf16[4,128,256]{2,1,0:T(8,128)(2,1)S(1)}, bf16[4,128,256]{2,1,0:T(8,128)(2,1)}, u32[]{:S(2)}) copy-start(bf16[4,128,256]{2,1,0:T(8,128)(2,1)} %get-tuple-element.71) | copy-start | bytes 786436
  23.9 5.5 %copy-start.11 = (bf16[4,128,256]{2,1,0:T(8,128)(2,1)S(1)}, bf16[4,128,256]{2,1,0:T(8,128)(2,1)}, u32[]{:S(2)}) copy-start(bf16[4,128,256]{2,1,0:T(8,128)(2,1)} %get-tuple-element.72) | copy-start | bytes 786436
  23.9 7.7 %copy-start.10 = (bf16[4,128,256]{2,1,0:T(8,128)(2,1)S(1)}, bf16[4,128,256]{2,1,0:T(8,128)(2,1)}, u32[]{:S(2)}) copy-start(bf16[4,128,256]{2,1,0:T(8,128)(2,1)} %get-tuple-element.73) | copy-start | bytes 786436
  23.9 8.2 %copy-start.9 = (bf16[4,128,256]{2,1,0:T(8,128)(2,1)S(1)}, bf16[4,128,256]{2,1,0:T(8,128)(2,1)}, u32[]{:S(2)}) copy-start(bf16[4,128,256]{2,1,0:T(8,128)(2,1)} %get-tuple-element.74) | copy-start | bytes 786436
  23.9 9.8 %copy-start.8 = (bf16[4,128,256]{2,1,0:T(8,128)(2,1)S(1)}, bf16[4,128,256]{2,1,0:T(8,128)(2,1)}, u32[]{:S(2)}) copy-start(bf16[4,128,256]{2,1,0:T(8,128)(2,1)} %get-tuple-element.75) | copy-start | bytes 786436
  23.9 10.8 %copy-start.1 = (bf16[4,128,256]{2,1,0:T(8,128)(2,1)S(1)}, bf16[4,128,256]{2,1,0:T(8,128)(2,1)}, u32[]{:S(2)}) copy-start(bf16[4,128,256]{2,1,0:T(8,128)(2,1)} %get-tuple-element.78.rest_0_) | copy-start | bytes 786436
  26.3 8.4 %copy-start.3 = (s32[8,8]{1,0:T(8,128)S(1)}, s32[8,8]{1,0:T(8,128)}, u32[]{:S(2)}) copy-start(s32[8,8]{1,0:T(8,128)} %bands_ref.3) | copy-start | bytes 772
  26.3 8.4 %copy-start.2 = (s32[8,8]{1,0:T(8,128)S(1)}, s32[8,8]{1,0:T(8,128)}, u32[]{:S(2)}) copy-start(s32[8,8]{1,0:T(8,128)} %flags_ref.3) | copy-start | bytes 772
  26.3 8.4 %copy-start.4 = (s32[8]{0:T(128)S(1)}, s32[8]{0:T(128)}, u32[]{:S(2)}) copy-start(s32[8]{0:T(128)} %constant.57.clone.hops_ref) | copy-start | bytes 100
  27.0 16.9 %collective-permute-start = (bf16[4,128,256]{2,1,0:T(8,128)(2,1)S(1)}, bf16[4,128,256]{2,1,0:T(8,128)(2,1)S(1)}, u32[]{:S(2)}, u32[]{:S(2)}) collective-permute-start(bf16[4,128,256]{2,1,0:T(8,128)(2,1)S(1)} %copy-done.12), channel_id=1, source_target_pairs={{0,6},{1,7},{2,4},{3,5},{4,2},{5,3},{6,0},{7,1},{8,14},{9,15},{10,... | collective-permute-start | bytes 786440 | tf_op jit(solution)/shard_map/ppermute | solution.py:242
  29.4 15.3 %collective-permute-start.1 = (bf16[4,128,256]{2,1,0:T(8,128)(2,1)S(1)}, bf16[4,128,256]{2,1,0:T(8,128)(2,1)S(1)}, u32[]{:S(2)}, u32[]{:S(2)}) collective-permute-start(bf16[4,128,256]{2,1,0:T(8,128)(2,1)S(1)} %copy-done.11), channel_id=1, source_target_pairs={{0,7},{1,6},{2,5},{3,4},{4,3},{5,2},{6,1},{7,0},{8,15},{9,14},{10,... | collective-permute-start | bytes 786440 | tf_op jit(solution)/shard_map/ppermute | solution.py:242
  31.5 17.8 %collective-permute-start.2 = (bf16[4,128,256]{2,1,0:T(8,128)(2,1)S(1)}, bf16[4,128,256]{2,1,0:T(8,128)(2,1)S(1)}, u32[]{:S(2)}, u32[]{:S(2)}) collective-permute-start(bf16[4,128,256]{2,1,0:T(8,128)(2,1)S(1)} %copy-done.10), channel_id=1, source_target_pairs={{0,2},{1,3},{2,0},{3,1},{4,6},{5,7},{6,4},{7,5},{8,10},{9,11},{10,... | collective-permute-start | bytes 786440 | tf_op jit(solution)/shard_map/ppermute | solution.py:242
  32.1 18.7 %collective-permute-start.3 = (bf16[4,128,256]{2,1,0:T(8,128)(2,1)S(1)}, bf16[4,128,256]{2,1,0:T(8,128)(2,1)S(1)}, u32[]{:S(2)}, u32[]{:S(2)}) collective-permute-start(bf16[4,128,256]{2,1,0:T(8,128)(2,1)S(1)} %copy-done.9), channel_id=1, source_target_pairs={{0,4},{1,5},{2,6},{3,7},{4,0},{5,1},{6,2},{7,3},{8,12},{9,13},{10,... | collective-permute-start | bytes 786440 | tf_op jit(solution)/shard_map/ppermute | solution.py:242
  33.7 20.2 %collective-permute-start.4 = (bf16[4,128,256]{2,1,0:T(8,128)(2,1)S(1)}, bf16[4,128,256]{2,1,0:T(8,128)(2,1)S(1)}, u32[]{:S(2)}, u32[]{:S(2)}) collective-permute-start(bf16[4,128,256]{2,1,0:T(8,128)(2,1)S(1)} %copy-done.8), channel_id=1, source_target_pairs={{0,3},{1,2},{2,1},{3,0},{4,7},{5,6},{6,5},{7,4},{8,11},{9,10},{10,... | collective-permute-start | bytes 786440 | tf_op jit(solution)/shard_map/ppermute | solution.py:242
  34.7 9.2 %copy-start.7 = (bf16[4,128,256]{2,1,0:T(8,128)(2,1)S(1)}, bf16[4,128,256]{2,1,0:T(8,128)(2,1)}, u32[]{:S(2)}) copy-start(bf16[4,128,256]{2,1,0:T(8,128)(2,1)} %get-tuple-element.94) | copy-start | bytes 786436
  34.7 9.9 %copy-start.6 = (bf16[4,128,256]{2,1,0:T(8,128)(2,1)S(1)}, bf16[4,128,256]{2,1,0:T(8,128)(2,1)}, u32[]{:S(2)}) copy-start(bf16[4,128,256]{2,1,0:T(8,128)(2,1)} %get-tuple-element.95) | copy-start | bytes 786436
  34.7 22.4 %copy-start = (bf16[4,128,256]{2,1,0:T(8,128)(2,1)S(1)}, bf16[4,128,256]{2,1,0:T(8,128)(2,1)}, u32[]{:S(2)}) copy-start(bf16[4,128,256]{2,1,0:T(8,128)(2,1)} %get-tuple-element.70.rest_0_) | copy-start | bytes 786436
  43.9 10.7 %collective-permute-start.12 = (bf16[4,128,256]{2,1,0:T(8,128)(2,1)S(1)}, bf16[4,128,256]{2,1,0:T(8,128)(2,1)S(1)}, u32[]{:S(2)}, u32[]{:S(2)}) collective-permute-start(bf16[4,128,256]{2,1,0:T(8,128)(2,1)S(1)} %copy-done.7), channel_id=1, source_target_pairs={{0,5},{1,4},{2,7},{3,6},{4,1},{5,0},{6,3},{7,2},{8,13},{9,12},{10,... | collective-permute-start | bytes 786440 | tf_op jit(solution)/shard_map/ppermute | solution.py:242
  44.6 11.6 %collective-permute-start.13 = (bf16[4,128,256]{2,1,0:T(8,128)(2,1)S(1)}, bf16[4,128,256]{2,1,0:T(8,128)(2,1)S(1)}, u32[]{:S(2)}, u32[]{:S(2)}) collective-permute-start(bf16[4,128,256]{2,1,0:T(8,128)(2,1)S(1)} %copy-done.6), channel_id=1, source_target_pairs={{0,1},{1,0},{2,3},{3,2},{4,5},{5,4},{6,7},{7,6},{8,9},{9,8},{10,11... | collective-permute-start | bytes 786440 | tf_op jit(solution)/shard_map/ppermute | solution.py:242
  49.3 17.1 %collective-permute-start.21 = (bf16[4,128,256]{2,1,0:T(8,128)(2,1)S(1)}, bf16[4,128,256]{2,1,0:T(8,128)(2,1)S(1)}, u32[]{:S(2)}, u32[]{:S(2)}) collective-permute-start(bf16[4,128,256]{2,1,0:T(8,128)(2,1)S(1)} %get-tuple-element.105), channel_id=1, source_target_pairs={{0,6},{1,7},{2,4},{3,5},{4,2},{5,3},{6,0},{7,1},{8,14},{9,15},{10,... | collective-permute-start | bytes 786440 | tf_op jit(solution)/shard_map/ppermute | solution.py:242
  50.7 16.6 %collective-permute-start.22 = (bf16[4,128,256]{2,1,0:T(8,128)(2,1)S(1)}, bf16[4,128,256]{2,1,0:T(8,128)(2,1)S(1)}, u32[]{:S(2)}, u32[]{:S(2)}) collective-permute-start(bf16[4,128,256]{2,1,0:T(8,128)(2,1)S(1)} %get-tuple-element.106), channel_id=1, source_target_pairs={{0,7},{1,6},{2,5},{3,4},{4,3},{5,2},{6,1},{7,0},{8,15},{9,14},{10,... | collective-permute-start | bytes 786440 | tf_op jit(solution)/shard_map/ppermute | solution.py:242
  53.9 17.9 %collective-permute-start.23 = (bf16[4,128,256]{2,1,0:T(8,128)(2,1)S(1)}, bf16[4,128,256]{2,1,0:T(8,128)(2,1)S(1)}, u32[]{:S(2)}, u32[]{:S(2)}) collective-permute-start(bf16[4,128,256]{2,1,0:T(8,128)(2,1)S(1)} %get-tuple-element.107), channel_id=1, source_target_pairs={{0,2},{1,3},{2,0},{3,1},{4,6},{5,7},{6,4},{7,5},{8,10},{9,11},{10,... | collective-permute-start | bytes 786440 | tf_op jit(solution)/shard_map/ppermute | solution.py:242
  54.5 18.7 %collective-permute-start.24 = (bf16[4,128,256]{2,1,0:T(8,128)(2,1)S(1)}, bf16[4,128,256]{2,1,0:T(8,128)(2,1)S(1)}, u32[]{:S(2)}, u32[]{:S(2)}) collective-permute-start(bf16[4,128,256]{2,1,0:T(8,128)(2,1)S(1)} %get-tuple-element.108), channel_id=1, source_target_pairs={{0,4},{1,5},{2,6},{3,7},{4,0},{5,1},{6,2},{7,3},{8,12},{9,13},{10,... | collective-permute-start | bytes 786440 | tf_op jit(solution)/shard_map/ppermute | solution.py:242
  56.2 20.2 %collective-permute-start.25 = (bf16[4,128,256]{2,1,0:T(8,128)(2,1)S(1)}, bf16[4,128,256]{2,1,0:T(8,128)(2,1)S(1)}, u32[]{:S(2)}, u32[]{:S(2)}) collective-permute-start(bf16[4,128,256]{2,1,0:T(8,128)(2,1)S(1)} %get-tuple-element.109), channel_id=1, source_target_pairs={{0,3},{1,2},{2,1},{3,0},{4,7},{5,6},{6,5},{7,4},{8,11},{9,10},{10,... | collective-permute-start | bytes 786440 | tf_op jit(solution)/shard_map/ppermute | solution.py:242
  66.4 10.7 %collective-permute-start.26 = (bf16[4,128,256]{2,1,0:T(8,128)(2,1)S(1)}, bf16[4,128,256]{2,1,0:T(8,128)(2,1)S(1)}, u32[]{:S(2)}, u32[]{:S(2)}) collective-permute-start(bf16[4,128,256]{2,1,0:T(8,128)(2,1)S(1)} %get-tuple-element.110), channel_id=1, source_target_pairs={{0,5},{1,4},{2,7},{3,6},{4,1},{5,0},{6,3},{7,2},{8,13},{9,12},{10,... | collective-permute-start | bytes 786440 | tf_op jit(solution)/shard_map/ppermute | solution.py:242
  67.4 11.4 %collective-permute-start.27 = (bf16[4,128,256]{2,1,0:T(8,128)(2,1)S(1)}, bf16[4,128,256]{2,1,0:T(8,128)(2,1)S(1)}, u32[]{:S(2)}, u32[]{:S(2)}) collective-permute-start(bf16[4,128,256]{2,1,0:T(8,128)(2,1)S(1)} %get-tuple-element.111), channel_id=1, source_target_pairs={{0,1},{1,0},{2,3},{3,2},{4,5},{5,4},{6,7},{7,6},{8,9},{9,8},{10,11... | collective-permute-start | bytes 786440 | tf_op jit(solution)/shard_map/ppermute | solution.py:242
  71.8 11.0 %collective-permute-start.14 = (bf16[4,128,256]{2,1,0:T(8,128)(2,1)S(1)}, bf16[4,128,256]{2,1,0:T(8,128)(2,1)S(1)}, u32[]{:S(2)}, u32[]{:S(2)}) collective-permute-start(bf16[4,128,256]{2,1,0:T(8,128)(2,1)S(1)} %get-tuple-element.97), channel_id=1, source_target_pairs={{0,6},{1,7},{2,4},{3,5},{4,2},{5,3},{6,0},{7,1},{8,14},{9,15},{10,... | collective-permute-start | bytes 786440 | tf_op jit(solution)/shard_map/ppermute | solution.py:242
  73.3 14.5 %collective-permute-start.15 = (bf16[4,128,256]{2,1,0:T(8,128)(2,1)S(1)}, bf16[4,128,256]{2,1,0:T(8,128)(2,1)S(1)}, u32[]{:S(2)}, u32[]{:S(2)}) collective-permute-start(bf16[4,128,256]{2,1,0:T(8,128)(2,1)S(1)} %get-tuple-element.98), channel_id=1, source_target_pairs={{0,7},{1,6},{2,5},{3,4},{4,3},{5,2},{6,1},{7,0},{8,15},{9,14},{10,... | collective-permute-start | bytes 786440 | tf_op jit(solution)/shard_map/ppermute | solution.py:242
  76.4 17.9 %collective-permute-start.16 = (bf16[4,128,256]{2,1,0:T(8,128)(2,1)S(1)}, bf16[4,128,256]{2,1,0:T(8,128)(2,1)S(1)}, u32[]{:S(2)}, u32[]{:S(2)}) collective-permute-start(bf16[4,128,256]{2,1,0:T(8,128)(2,1)S(1)} %get-tuple-element.99), channel_id=1, source_target_pairs={{0,2},{1,3},{2,0},{3,1},{4,6},{5,7},{6,4},{7,5},{8,10},{9,11},{10,... | collective-permute-start | bytes 786440 | tf_op jit(solution)/shard_map/ppermute | solution.py:242
  77.0 17.3 %collective-permute-start.17 = (bf16[4,128,256]{2,1,0:T(8,128)(2,1)S(1)}, bf16[4,128,256]{2,1,0:T(8,128)(2,1)S(1)}, u32[]{:S(2)}, u32[]{:S(2)}) collective-permute-start(bf16[4,128,256]{2,1,0:T(8,128)(2,1)S(1)} %get-tuple-element.100), channel_id=1, source_target_pairs={{0,4},{1,5},{2,6},{3,7},{4,0},{5,1},{6,2},{7,3},{8,12},{9,13},{10,... | collective-permute-start | bytes 786440 | tf_op jit(solution)/shard_map/ppermute | solution.py:242
  78.7 19.3 %collective-permute-start.18 = (bf16[4,128,256]{2,1,0:T(8,128)(2,1)S(1)}, bf16[4,128,256]{2,1,0:T(8,128)(2,1)S(1)}, u32[]{:S(2)}, u32[]{:S(2)}) collective-permute-start(bf16[4,128,256]{2,1,0:T(8,128)(2,1)S(1)} %get-tuple-element.101), channel_id=1, source_target_pairs={{0,3},{1,2},{2,1},{3,0},{4,7},{5,6},{6,5},{7,4},{8,11},{9,10},{10,... | collective-permute-start | bytes 786440 | tf_op jit(solution)/shard_map/ppermute | solution.py:242
  82.8 15.9 %collective-permute-start.19 = (bf16[4,128,256]{2,1,0:T(8,128)(2,1)S(1)}, bf16[4,128,256]{2,1,0:T(8,128)(2,1)S(1)}, u32[]{:S(2)}, u32[]{:S(2)}) collective-permute-start(bf16[4,128,256]{2,1,0:T(8,128)(2,1)S(1)} %get-tuple-element.102), channel_id=1, source_target_pairs={{0,5},{1,4},{2,7},{3,6},{4,1},{5,0},{6,3},{7,2},{8,13},{9,12},{10,... | collective-permute-start | bytes 786440 | tf_op jit(solution)/shard_map/ppermute | solution.py:242
  87.7 11.0 %collective-permute-start.20 = (bf16[4,128,256]{2,1,0:T(8,128)(2,1)S(1)}, bf16[4,128,256]{2,1,0:T(8,128)(2,1)S(1)}, u32[]{:S(2)}, u32[]{:S(2)}) collective-permute-start(bf16[4,128,256]{2,1,0:T(8,128)(2,1)S(1)} %get-tuple-element.103), channel_id=1, source_target_pairs={{0,1},{1,0},{2,3},{3,2},{4,5},{5,4},{6,7},{7,6},{8,9},{9,8},{10,11... | collective-permute-start | bytes 786440 | tf_op jit(solution)/shard_map/ppermute | solution.py:242

commit v3 on v2

--- a/solution.py
+++ b/solution.py
@@ -15,8 +15,8 @@
 CHUNKS = 2
 AHEAD = 5
 SMALL = 8 * 1024 * 1024
-FIRST_CUTS = (0,)
-LAST_CUTS = (0,)
+EARLY = 2
+LAST = (3,)
 LIMIT = 40 * 1024 * 1024
 
 F32 = jnp.float32
@@ -245,62 +245,57 @@
 
     def pack(c, slots):
         return pl.pallas_call(
-            functools.partial(pack_kernel, hops[slots], heads, c * count, count),
-            out_shape=[piece] * len(hops[slots]),
+            functools.partial(pack_kernel, [hops[s] for s in slots], heads, c * count, count),
+            out_shape=[piece] * len(slots),
             in_specs=[SMEM] + [ANY] * 4,
-            out_specs=[VMEM] * len(hops[slots]),
-            scratch_shapes=[pltpu.SemaphoreType.DMA((len(hops[slots]), 4))],
-            name=f"pack_{c}_{slots.start}",
+            out_specs=[VMEM] * len(slots),
+            scratch_shapes=[pltpu.SemaphoreType.DMA((len(slots), 4))],
+            name=f"pack_{c}_{slots[0]}",
         )(me, *arrays)
 
+    def prepare(c):
+        order = [*range(1, groups), 0]
+        parts = (order[:EARLY], order[EARLY:]) if c == 0 else (order,)
+        made = {s: p for slots in parts for s, p in zip(slots, pack(c, slots))}
+        return [made[s] for s in range(groups)]
+
     def unpack(c, slots, pieces, before):
-        kept, own = len(before), len(hops[slots])
+        kept, own = len(before), len(slots)
         return pl.pallas_call(
-            functools.partial(unpack_kernel, hops[slots], heads, c * count, count, kept),
+            functools.partial(unpack_kernel, [hops[s] for s in slots], heads, c * count, count, kept),
             out_shape=[jax.ShapeDtypeStruct((rows, channels), BF16)] * 4,
             in_specs=[SMEM] + [VMEM] * own + [ANY] * kept,
             out_specs=[ANY] * 4,
             input_output_aliases={1 + own + a: a for a in range(kept)},
             scratch_shapes=[pltpu.SemaphoreType.DMA((own, 4))],
             compiler_params=pltpu.CompilerParams(vmem_limit_bytes=SMALL),
-            name=f"unpack_{c}_{slots.start}",
-        )(me, *pieces[slots], *before)
+            name=f"unpack_{c}_{slots[0]}",
+        )(me, *[pieces[s] for s in slots], *before)
 
     def after(pieces, others):
         both = lax.optimization_barrier((*pieces, *others))
         return list(both[: len(pieces)]), list(both[len(pieces) :])
 
+    near = AHEAD + 1
     tables = rope_tables(positions)
-    packed = [
-        [p for lo, hi in zip(cuts, cuts[1:]) for p in pack(c, slice(lo, hi))]
-        for c, cuts in enumerate([FIRST_CUTS + (groups,)] + [(0, groups)] * (chunks - 1))
-    ]
-    near = AHEAD + 1
+    packed = [prepare(c) for c in range(chunks)]
     if chunks > 1:
         packed[1], tables = after(packed[1], tables)
     arrived = [exchange(packed[0])]
     turned = []
     for c in range(chunks):
-        pending = packed[c + 1] if c + 1 < chunks else turned[-1] if turned else []
-        head = exchange(pending[:near])
+        if c + 1 < chunks:
+            head = exchange(packed[c + 1][:near])
         new = attention_call(hops, count, me, block_flags, band_ids, tables, arrived[c])
-        tail, new = pending[near:], list(new)
         if c + 1 < chunks:
-            tail, new = after(tail, new)
-        moved = head + exchange(tail, near)
-        if c + 1 < chunks:
-            arrived.append(moved)
-            if c:
-                turned[-1] = exchange(turned[-1])
-        elif turned:
-            turned[-1] = moved
-        turned.append(new)
-    turned[-1] = exchange(turned[-1])
+            tail, new = after(packed[c + 1][near:], new)
+            arrived.append(head + exchange(tail, near))
+        turned.append(exchange(new))
     results = ()
     for c in range(chunks):
-        cuts = LAST_CUTS if c + 1 == chunks else (0,)
-        for lo, hi in zip(cuts, cuts[1:] + (groups,)):
-            results = unpack(c, slice(lo, hi), turned[c], results)
+        ends = [*LAST, groups] if c + 1 == chunks else [groups]
+        for lo, hi in zip([0] + ends, ends):
+            results = unpack(c, range(lo, hi), turned[c], results)
     return tuple(results)
 
 

time: 101 us -> 99.2 us (0.982)
  waiting for transfers between devices: 43.6 us -> 39.8 us
  Pallas kernels: 28 us -> 30.1 us
    ppermute x28, waiting for transfers between devices: 43.6 us -> 39.8 us  [exchange(): lax.ppermute(piece, 'seq', [(i, i ^ d) for i in range(groups)])]
    pallas_call x4 -> x6, Pallas kernels: 9.53 us -> 11.7 us  [the longest x3 7.92 us: pack(): pl.pallas_call(functools.partial(pack_kernel, [hops[s] for s in slots], h...]
  transfers between devices with their start and end apart: 28 -> 28, of which waited for: 13 -> 13; matrix products, arithmetic and copies ran while one was open for 3% -> 3% of each run, Pallas kernels for 23% -> 27%
where the time goes in v3:
time: 99.2 us; the launch traced here: 98.8 us
  waiting for transfers between devices  39.8 us (40%)
  Pallas kernels  30.1 us (30%)
  starting transfers between devices  24.8 us (25%)
  other arithmetic  2.92 us (3%)
  between operations  1.04 us (1%)
    ppermute x28, waiting for transfers between devices, exchange(): lax.ppermute(piece, 'seq', [(i, i ^ d) for i in range(groups)])  39.8 us
    ppermute x28, starting transfers between devices, exchange(): lax.ppermute(piece, 'seq', [(i, i ^ d) for i in range(groups)])  24.8 us
    pallas_call x2, Pallas kernels, attention_call(): pl.pallas_call(functools.partial(attention_kernel, hops, rows, count, wid...  18.5 us
    pallas_call x3, Pallas kernels, pack(): pl.pallas_call(functools.partial(pack_kernel, [hops[s] for s in slots], h...  7.92 us
    pallas_call x3, Pallas kernels, unpack(): pl.pallas_call(functools.partial(unpack_kernel, [hops[s] for s in slots],...  3.75 us
    mul x1, other arithmetic, rope_tables(): return (jnp.cos(angle), jnp.sin(angle) * sign[None, :])  2.35 us
  transfers between devices with their start and end apart: 28, of which 13 were waited for; matrix products, arithmetic and copies ran while one was open for 3% of the time, Pallas kernels for 27%

profile of v3, /device:TPU:0, one launch (start us, length us, event | category | flops | bytes accessed | tf_op | source)
XLA Modules:
  0.0 98.8 jit_solution(14699290956509186835)
XLA Ops:
  0.6 1.9 %pack_0_1.1 = (bf16[4,128,256]{2,1,0:T(8,128)(2,1)}, bf16[4,128,256]{2,1,0:T(8,128)(2,1)}) custom-call(s32[1]{0:T(128)} %bitcast.me_ref, bf16[128,4096]{1,0:T(8,128)(2,1)} %q_ref.5, bf16[128,4096]{1,0:T(8,128)(2,1)} %k_ref.5, bf16[128,4096]{1,0:T(8,128)(2,1)} %v_ref.5, bf16[128,4096]{1,0:T(8,128)(2,1)} %g_ref.5), custom_call_target="tpu_custom_call" | custom-call | tf_op jit(solution)/shard_map/pack_0_1/pallas_call | solution.py:247
  2.6 4.0 %collective-permute-start.5 = (bf16[4,128,256]{2,1,0:T(8,128)(2,1)}, bf16[4,128,256]{2,1,0:T(8,128)(2,1)S(1)}, u32[]{:S(2)}, u32[]{:S(2)}) collective-permute-start(bf16[4,128,256]{2,1,0:T(8,128)(2,1)} %get-tuple-element.83), channel_id=1, source_target_pairs={{0,6},{1,7},{2,4},{3,5},{4,2},{5,3},{6,0},{7,1},{8,14},{9,15},{10,... | collective-permute-start | bytes 786440 | tf_op jit(solution)/shard_map/ppermute | solution.py:242
  6.5 0.0 collective-permute-start.6
  6.5 2.8 %pack_0_3.1 = (bf16[4,128,256]{2,1,0:T(8,128)(2,1)}, bf16[4,128,256]{2,1,0:T(8,128)(2,1)}, bf16[4,128,256]{2,1,0:T(8,128)(2,1)}, bf16[4,128,256]{2,1,0:T(8,128)(...) custom-call(s32[1]{0:T(128)} %bitcast.me_ref, bf16[128,4096]{1,0:T(8,128)(2,1)} %q_ref.5, ...), custom_call_target="tpu_custom_call" | custom-call | tf_op jit(solution)/shard_map/pack_0_3/pallas_call | solution.py:247
  9.4 1.2 %collective-permute-start.7 = (bf16[4,128,256]{2,1,0:T(8,128)(2,1)}, bf16[4,128,256]{2,1,0:T(8,128)(2,1)S(1)}, u32[]{:S(2)}, u32[]{:S(2)}) collective-permute-start(bf16[4,128,256]{2,1,0:T(8,128)(2,1)} %get-tuple-element.85), channel_id=1, source_target_pairs={{0,2},{1,3},{2,0},{3,1},{4,6},{5,7},{6,4},{7,5},{8,10},{9,11},{10,... | collective-permute-start | bytes 786440 | tf_op jit(solution)/shard_map/ppermute | solution.py:242
  10.5 1.5 %collective-permute-start.8 = (bf16[4,128,256]{2,1,0:T(8,128)(2,1)}, bf16[4,128,256]{2,1,0:T(8,128)(2,1)S(1)}, u32[]{:S(2)}, u32[]{:S(2)}) collective-permute-start(bf16[4,128,256]{2,1,0:T(8,128)(2,1)} %get-tuple-element.86), channel_id=1, source_target_pairs={{0,4},{1,5},{2,6},{3,7},{4,0},{5,1},{6,2},{7,3},{8,12},{9,13},{10,... | collective-permute-start | bytes 786440 | tf_op jit(solution)/shard_map/ppermute | solution.py:242
  12.1 0.6 collective-permute-start.9
  12.7 0.2 broadcast_multiply_fusion.2
  12.9 0.3 broadcast_multiply_fusion.1
  13.2 0.7 collective-permute-done.5.rest_1_
  13.9 0.0 collective-permute-start.10
  13.9 5.3 %collective-permute-done.6.rest_2_ = bf16[4,128,256]{2,1,0:T(8,128)(2,1)S(1)} collective-permute-done((bf16[4,128,256]{2,1,0:T(8,128)(2,1)}, bf16[4,128,256]{2,1,0:T(8,128)(2,1)S(1)}, u32[]{:S(2)}, u32[]{:S(2)}) %collective-permute-start.6) | collective-permute-done | bytes 262176 | tf_op jit(solution)/shard_map/ppermute | solution.py:242
  19.2 0.1 collective-permute-start.11
  19.4 3.2 %pack_1_1.1 = (bf16[4,128,256]{2,1,0:T(8,128)(2,1)}, bf16[4,128,256]{2,1,0:T(8,128)(2,1)}, bf16[4,128,256]{2,1,0:T(8,128)(2,1)}, bf16[4,128,256]{2,1,0:T(8,128)(...) custom-call(s32[1]{0:T(128)} %bitcast.me_ref, ...), custom_call_target="tpu_custom_call" | custom-call | tf_op jit(solution)/shard_map/pack_1_1/pallas_call | solution.py:247
  22.6 0.0 copy-start.12
  22.6 0.0 copy-start.11
  22.6 0.0 copy-start.10
  22.6 0.0 copy-start.9
  22.6 2.4 %sine_multiply_fusion = (f32[1024,128]{1,0:T(8,128)S(1)}, f32[1024,128]{1,0:T(8,128)S(1)}) fusion(f32[128]{0:T(128)S(1)} %compare_select_fusion, f32[1024,42]{1,0:T(8,128)S(1)} %get-tuple-element.130, f32[1024,42]{1,0:T(8,128)S(1)} %get-tuple-element.129, f32[1024,44]{1,0:T(8,128)S(1)} %broadcast_multiply_fusion.2), kind=kLoop, calls=%fused_computation.1 | loop fusion | flops 393216 | bytes 1573376 | tf_op jit(solution)/shard_map/mul | solution.py:38
  25.0 0.0 copy-start.3
  25.0 0.0 copy-start.2
  25.0 0.0 copy-start.4
  25.0 0.7 collective-permute-done.7.rest_3_
  25.7 2.3 %collective-permute-start = (bf16[4,128,256]{2,1,0:T(8,128)(2,1)S(1)}, bf16[4,128,256]{2,1,0:T(8,128)(2,1)S(1)}, u32[]{:S(2)}, u32[]{:S(2)}) collective-permute-start(bf16[4,128,256]{2,1,0:T(8,128)(2,1)S(1)} %copy-done.12), channel_id=1, source_target_pairs={{0,6},{1,7},{2,4},{3,5},{4,2},{5,3},{6,0},{7,1},{8,14},{9,15},{10,... | collective-permute-start | bytes 786440 | tf_op jit(solution)/shard_map/ppermute | solution.py:242
  28.1 0.0 collective-permute-start.1
  28.1 2.2 %collective-permute-done.9.rest_5_ = bf16[4,128,256]{2,1,0:T(8,128)(2,1)S(1)} collective-permute-done((bf16[4,128,256]{2,1,0:T(8,128)(2,1)}, bf16[4,128,256]{2,1,0:T(8,128)(2,1)S(1)}, u32[]{:S(2)}, u32[]{:S(2)}) %collective-permute-start.9) | collective-permute-done | bytes 262176 | tf_op jit(solution)/shard_map/ppermute | solution.py:242
  30.3 0.5 collective-permute-start.2
  30.8 1.7 %collective-permute-start.3 = (bf16[4,128,256]{2,1,0:T(8,128)(2,1)S(1)}, bf16[4,128,256]{2,1,0:T(8,128)(2,1)S(1)}, u32[]{:S(2)}, u32[]{:S(2)}) collective-permute-start(bf16[4,128,256]{2,1,0:T(8,128)(2,1)S(1)} %copy-done.9), channel_id=1, source_target_pairs={{0,4},{1,5},{2,6},{3,7},{4,0},{5,1},{6,2},{7,3},{8,12},{9,13},{10,... | collective-permute-start | bytes 786440 | tf_op jit(solution)/shard_map/ppermute | solution.py:242
  32.5 0.0 collective-permute-done.11.rest_7_
  32.5 0.9 collective-permute-start.4
  33.5 9.2 %attention.2 = (bf16[4,128,256]{2,1,0:T(8,128)(2,1)S(1)}, bf16[4,128,256]{2,1,0:T(8,128)(2,1)S(1)}, bf16[4,128,256]{2,1,0:T(8,128)(2,1)S(1)}, bf16[4,128,256]{2,...) custom-call(s32[1]{0:T(128)} %bitcast.me_ref, ...), custom_call_target="tpu_custom_call" | custom-call | flops 2684354560 | bytes 4194304 | tf_op jit(solution)/shard_map/attention/pallas_call | solution.py:208
  42.6 0.0 collective-permute-done.rest_1_
  42.6 0.7 collective-permute-start.12
  43.4 0.0 collective-permute-done.1.rest_2_
  43.4 0.4 collective-permute-start.13
  43.8 4.2 %collective-permute-done.2.rest_3_ = bf16[4,128,256]{2,1,0:T(8,128)(2,1)S(1)} collective-permute-done((bf16[4,128,256]{2,1,0:T(8,128)(2,1)S(1)}, bf16[4,128,256]{2,1,0:T(8,128)(2,1)S(1)}, u32[]{:S(2)}, u32[]{:S(2)}) %collective-permute-start.2) | collective-permute-done | bytes 262176 | tf_op jit(solution)/shard_map/ppermute | solution.py:242
  48.0 1.4 %collective-permute-start.21 = (bf16[4,128,256]{2,1,0:T(8,128)(2,1)S(1)}, bf16[4,128,256]{2,1,0:T(8,128)(2,1)S(1)}, u32[]{:S(2)}, u32[]{:S(2)}) collective-permute-start(bf16[4,128,256]{2,1,0:T(8,128)(2,1)S(1)} %get-tuple-element.109), channel_id=1, source_target_pairs={{0,6},{1,7},{2,4},{3,5},{4,2},{5,3},{6,0},{7,1},{8,14},{9,15},{10,... | collective-permute-start | bytes 786440 | tf_op jit(solution)/shard_map/ppermute | solution.py:242
  49.5 3.2 %collective-permute-done.4.rest_5_ = bf16[4,128,256]{2,1,0:T(8,128)(2,1)S(1)} collective-permute-done((bf16[4,128,256]{2,1,0:T(8,128)(2,1)S(1)}, bf16[4,128,256]{2,1,0:T(8,128)(2,1)S(1)}, u32[]{:S(2)}, u32[]{:S(2)}) %collective-permute-start.4) | collective-permute-done | bytes 262176 | tf_op jit(solution)/shard_map/ppermute | solution.py:242
  52.7 0.6 collective-permute-start.23
  53.2 0.0 collective-permute-done.12.rest_6_
  53.2 1.7 %collective-permute-start.24 = (bf16[4,128,256]{2,1,0:T(8,128)(2,1)S(1)}, bf16[4,128,256]{2,1,0:T(8,128)(2,1)S(1)}, u32[]{:S(2)}, u32[]{:S(2)}) collective-permute-start(bf16[4,128,256]{2,1,0:T(8,128)(2,1)S(1)} %get-tuple-element.112), channel_id=1, source_target_pairs={{0,4},{1,5},{2,6},{3,7},{4,0},{5,1},{6,2},{7,3},{8,12},{9,13},{10,... | collective-permute-start | bytes 786440 | tf_op jit(solution)/shard_map/ppermute | solution.py:242
  54.9 0.0 collective-permute-done.13.rest_7_
  55.0 0.9 collective-permute-start.25
  55.8 9.3 %attention.3 = (bf16[4,128,256]{2,1,0:T(8,128)(2,1)S(1)}, bf16[4,128,256]{2,1,0:T(8,128)(2,1)S(1)}, bf16[4,128,256]{2,1,0:T(8,128)(2,1)S(1)}, bf16[4,128,256]{2,...) custom-call(s32[1]{0:T(128)} %bitcast.me_ref, ...), custom_call_target="tpu_custom_call" | custom-call | flops 2684354560 | bytes 4194304 | tf_op jit(solution)/shard_map/attention/pallas_call | solution.py:208
  65.1 0.0 collective-permute-done.21.rest_1_
  65.1 1.0 collective-permute-start.26
  66.1 0.3 collective-permute-start.27
  66.4 4.2 %collective-permute-done.23.rest_3_ = bf16[4,128,256]{2,1,0:T(8,128)(2,1)S(1)} collective-permute-done((bf16[4,128,256]{2,1,0:T(8,128)(2,1)S(1)}, bf16[4,128,256]{2,1,0:T(8,128)(2,1)S(1)}, u32[]{:S(2)}, u32[]{:S(2)}) %collective-permute-start.23) | collective-permute-done | bytes 262176 | tf_op jit(solution)/shard_map/ppermute | solution.py:242
  70.6 1.4 %collective-permute-start.19 = (bf16[4,128,256]{2,1,0:T(8,128)(2,1)S(1)}, bf16[4,128,256]{2,1,0:T(8,128)(2,1)S(1)}, u32[]{:S(2)}, u32[]{:S(2)}) collective-permute-start(bf16[4,128,256]{2,1,0:T(8,128)(2,1)S(1)} %get-tuple-element.106), channel_id=1, source_target_pairs={{0,6},{1,7},{2,4},{3,5},{4,2},{5,3},{6,0},{7,1},{8,14},{9,15},{10,... | collective-permute-start | bytes 786440 | tf_op jit(solution)/shard_map/ppermute | solution.py:242
  72.0 0.0 collective-permute-done.24.rest_4_
  72.0 0.0 collective-permute-start.20
  72.0 3.2 %collective-permute-done.25.rest_5_ = bf16[4,128,256]{2,1,0:T(8,128)(2,1)S(1)} collective-permute-done((bf16[4,128,256]{2,1,0:T(8,128)(2,1)S(1)}, bf16[4,128,256]{2,1,0:T(8,128)(2,1)S(1)}, u32[]{:S(2)}, u32[]{:S(2)}) %collective-permute-start.25) | collective-permute-done | bytes 262176 | tf_op jit(solution)/shard_map/ppermute | solution.py:242
  75.2 0.6 collective-permute-start.14
  75.8 1.7 %collective-permute-start.15 = (bf16[4,128,256]{2,1,0:T(8,128)(2,1)S(1)}, bf16[4,128,256]{2,1,0:T(8,128)(2,1)S(1)}, u32[]{:S(2)}, u32[]{:S(2)}) collective-permute-start(bf16[4,128,256]{2,1,0:T(8,128)(2,1)S(1)} %get-tuple-element.101), channel_id=1, source_target_pairs={{0,4},{1,5},{2,6},{3,7},{4,0},{5,1},{6,2},{7,3},{8,12},{9,13},{10,... | collective-permute-start | bytes 786440 | tf_op jit(solution)/shard_map/ppermute | solution.py:242
  77.5 0.8 collective-permute-start.16
  78.3 3.2 %collective-permute-done.19.rest_1_ = bf16[4,128,256]{2,1,0:T(8,128)(2,1)S(1)} collective-permute-done((bf16[4,128,256]{2,1,0:T(8,128)(2,1)S(1)}, bf16[4,128,256]{2,1,0:T(8,128)(2,1)S(1)}, u32[]{:S(2)}, u32[]{:S(2)}) %collective-permute-start.19) | collective-permute-done | bytes 262176 | tf_op jit(solution)/shard_map/ppermute | solution.py:242
  81.5 4.9 %collective-permute-done.20.rest_2_ = bf16[4,128,256]{2,1,0:T(8,128)(2,1)S(1)} collective-permute-done((bf16[4,128,256]{2,1,0:T(8,128)(2,1)S(1)}, bf16[4,128,256]{2,1,0:T(8,128)(2,1)S(1)}, u32[]{:S(2)}, u32[]{:S(2)}) %collective-permute-start.20) | collective-permute-done | bytes 262176 | tf_op jit(solution)/shard_map/ppermute | solution.py:242
  86.5 0.4 collective-permute-start.18
  86.9 1.6 %unpack_0_0.1 = (bf16[128,4096]{1,0:T(8,128)(2,1)}, bf16[128,4096]{1,0:T(8,128)(2,1)}, bf16[128,4096]{1,0:T(8,128)(2,1)}, bf16[128,4096]{1,0:T(8,128)(2,1)}) custom-call(s32[1]{0:T(128)} %bitcast.me_ref, bf16[4,128,256]{2,1,0:T(8,128)(2,1)S(1)} %get-tuple-element.108.rest_0_, bf16[4,128,256]{2,1,0:T(8,128)(2,1)S(1)} %collective-permute-done.21.rest_1_, ...), custom_call_target="tpu_custom_call" | custom-call | tf_op jit(solution)/shard_map/unpack_0_0/pallas_call | solution.py:264
  88.5 1.0 unpack_1_0.1
  89.5 3.6 %collective-permute-done.14.rest_0_ = bf16[4,128,256]{2,1,0:T(8,128)(2,1)S(1)} collective-permute-done((bf16[4,128,256]{2,1,0:T(8,128)(2,1)S(1)}, bf16[4,128,256]{2,1,0:T(8,128)(2,1)S(1)}, u32[]{:S(2)}, u32[]{:S(2)}) %collective-permute-start.14) | collective-permute-done | bytes 262176 | tf_op jit(solution)/shard_map/ppermute | solution.py:242
  93.1 3.7 %collective-permute-done.16.rest_2_ = bf16[4,128,256]{2,1,0:T(8,128)(2,1)S(1)} collective-permute-done((bf16[4,128,256]{2,1,0:T(8,128)(2,1)S(1)}, bf16[4,128,256]{2,1,0:T(8,128)(2,1)S(1)}, u32[]{:S(2)}, u32[]{:S(2)}) %collective-permute-start.16) | collective-permute-done | bytes 262176 | tf_op jit(solution)/shard_map/ppermute | solution.py:242
  96.8 0.7 collective-permute-done.17.rest_3_
  97.4 1.2 %unpack_1_3.1 = (bf16[128,4096]{1,0:T(8,128)(2,1)}, bf16[128,4096]{1,0:T(8,128)(2,1)}, bf16[128,4096]{1,0:T(8,128)(2,1)}, bf16[128,4096]{1,0:T(8,128)(2,1)}) custom-call(s32[1]{0:T(128)} %bitcast.me_ref, bf16[4,128,256]{2,1,0:T(8,128)(2,1)S(1)} %collective-permute-done.14.rest_0_, ...), custom_call_target="tpu_custom_call", output_to_operand_aliasing={{0}: (6, {}), {1}: (7, {}), {2}: (8, {}), {3}: (9, {})} | custom-call | tf_op jit(solution)/shard_map/unpack_1_3/pallas_call | solution.py:264
  (33 shorter events, 0.1 us)
Async XLA Ops:
  2.6 11.3 %collective-permute-start.5 = (bf16[4,128,256]{2,1,0:T(8,128)(2,1)}, bf16[4,128,256]{2,1,0:T(8,128)(2,1)S(1)}, u32[]{:S(2)}, u32[]{:S(2)}) collective-permute-start(bf16[4,128,256]{2,1,0:T(8,128)(2,1)} %get-tuple-element.83), channel_id=1, source_target_pairs={{0,6},{1,7},{2,4},{3,5},{4,2},{5,3},{6,0},{7,1},{8,14},{9,15},{10,... | collective-permute-start | bytes 786440 | tf_op jit(solution)/shard_map/ppermute | solution.py:242
  6.5 6.1 %copy-start.5 = (s32[3,1024]{1,0:T(4,128)S(1)}, s32[3,1024]{1,0:T(4,128)}, u32[]{:S(2)}) copy-start(s32[3,1024]{1,0:T(4,128)} %param.13) | copy-start | bytes 36868
  6.5 12.7 %collective-permute-start.6 = (bf16[4,128,256]{2,1,0:T(8,128)(2,1)}, bf16[4,128,256]{2,1,0:T(8,128)(2,1)S(1)}, u32[]{:S(2)}, u32[]{:S(2)}) collective-permute-start(bf16[4,128,256]{2,1,0:T(8,128)(2,1)} %get-tuple-element.84), channel_id=1, source_target_pairs={{0,7},{1,6},{2,5},{3,4},{4,3},{5,2},{6,1},{7,0},{8,15},{9,14},{10,... | collective-permute-start | bytes 786440 | tf_op jit(solution)/shard_map/ppermute | solution.py:242
  9.4 16.4 %collective-permute-start.7 = (bf16[4,128,256]{2,1,0:T(8,128)(2,1)}, bf16[4,128,256]{2,1,0:T(8,128)(2,1)S(1)}, u32[]{:S(2)}, u32[]{:S(2)}) collective-permute-start(bf16[4,128,256]{2,1,0:T(8,128)(2,1)} %get-tuple-element.85), channel_id=1, source_target_pairs={{0,2},{1,3},{2,0},{3,1},{4,6},{5,7},{6,4},{7,5},{8,10},{9,11},{10,... | collective-permute-start | bytes 786440 | tf_op jit(solution)/shard_map/ppermute | solution.py:242
  10.5 17.5 %collective-permute-start.8 = (bf16[4,128,256]{2,1,0:T(8,128)(2,1)}, bf16[4,128,256]{2,1,0:T(8,128)(2,1)S(1)}, u32[]{:S(2)}, u32[]{:S(2)}) collective-permute-start(bf16[4,128,256]{2,1,0:T(8,128)(2,1)} %get-tuple-element.86), channel_id=1, source_target_pairs={{0,4},{1,5},{2,6},{3,7},{4,0},{5,1},{6,2},{7,3},{8,12},{9,13},{10,... | collective-permute-start | bytes 786440 | tf_op jit(solution)/shard_map/ppermute | solution.py:242
  12.1 18.2 %collective-permute-start.9 = (bf16[4,128,256]{2,1,0:T(8,128)(2,1)}, bf16[4,128,256]{2,1,0:T(8,128)(2,1)S(1)}, u32[]{:S(2)}, u32[]{:S(2)}) collective-permute-start(bf16[4,128,256]{2,1,0:T(8,128)(2,1)} %get-tuple-element.87), channel_id=1, source_target_pairs={{0,3},{1,2},{2,1},{3,0},{4,7},{5,6},{6,5},{7,4},{8,11},{9,10},{10,... | collective-permute-start | bytes 786440 | tf_op jit(solution)/shard_map/ppermute | solution.py:242
  13.9 16.9 %collective-permute-start.10 = (bf16[4,128,256]{2,1,0:T(8,128)(2,1)}, bf16[4,128,256]{2,1,0:T(8,128)(2,1)S(1)}, u32[]{:S(2)}, u32[]{:S(2)}) collective-permute-start(bf16[4,128,256]{2,1,0:T(8,128)(2,1)} %get-tuple-element.88), channel_id=1, source_target_pairs={{0,5},{1,4},{2,7},{3,6},{4,1},{5,0},{6,3},{7,2},{8,13},{9,12},{10,... | collective-permute-start | bytes 786440 | tf_op jit(solution)/shard_map/ppermute | solution.py:242
  19.2 13.3 %collective-permute-start.11 = (bf16[4,128,256]{2,1,0:T(8,128)(2,1)}, bf16[4,128,256]{2,1,0:T(8,128)(2,1)S(1)}, u32[]{:S(2)}, u32[]{:S(2)}) collective-permute-start(bf16[4,128,256]{2,1,0:T(8,128)(2,1)} %get-tuple-element.89), channel_id=1, source_target_pairs={{0,1},{1,0},{2,3},{3,2},{4,5},{5,4},{6,7},{7,6},{8,9},{9,8},{10,11... | collective-permute-start | bytes 786440 | tf_op jit(solution)/shard_map/ppermute | solution.py:242
  22.6 3.2 %copy-start.12 = (bf16[4,128,256]{2,1,0:T(8,128)(2,1)S(1)}, bf16[4,128,256]{2,1,0:T(8,128)(2,1)}, u32[]{:S(2)}) copy-start(bf16[4,128,256]{2,1,0:T(8,128)(2,1)} %get-tuple-element.75) | copy-start | bytes 786436
  22.6 5.5 %copy-start.11 = (bf16[4,128,256]{2,1,0:T(8,128)(2,1)S(1)}, bf16[4,128,256]{2,1,0:T(8,128)(2,1)}, u32[]{:S(2)}) copy-start(bf16[4,128,256]{2,1,0:T(8,128)(2,1)} %get-tuple-element.76) | copy-start | bytes 786436
  22.6 7.7 %copy-start.10 = (bf16[4,128,256]{2,1,0:T(8,128)(2,1)S(1)}, bf16[4,128,256]{2,1,0:T(8,128)(2,1)}, u32[]{:S(2)}) copy-start(bf16[4,128,256]{2,1,0:T(8,128)(2,1)} %get-tuple-element.77) | copy-start | bytes 786436
  22.6 8.2 %copy-start.9 = (bf16[4,128,256]{2,1,0:T(8,128)(2,1)S(1)}, bf16[4,128,256]{2,1,0:T(8,128)(2,1)}, u32[]{:S(2)}) copy-start(bf16[4,128,256]{2,1,0:T(8,128)(2,1)} %get-tuple-element.78) | copy-start | bytes 786436
  22.6 9.9 %copy-start.8 = (bf16[4,128,256]{2,1,0:T(8,128)(2,1)S(1)}, bf16[4,128,256]{2,1,0:T(8,128)(2,1)}, u32[]{:S(2)}) copy-start(bf16[4,128,256]{2,1,0:T(8,128)(2,1)} %get-tuple-element.79) | copy-start | bytes 786436
  22.6 10.8 %copy-start.1 = (bf16[4,128,256]{2,1,0:T(8,128)(2,1)S(1)}, bf16[4,128,256]{2,1,0:T(8,128)(2,1)}, u32[]{:S(2)}) copy-start(bf16[4,128,256]{2,1,0:T(8,128)(2,1)} %get-tuple-element.82.rest_0_) | copy-start | bytes 786436
  25.0 8.4 %copy-start.3 = (s32[8,8]{1,0:T(8,128)S(1)}, s32[8,8]{1,0:T(8,128)}, u32[]{:S(2)}) copy-start(s32[8,8]{1,0:T(8,128)} %bands_ref.3) | copy-start | bytes 772
  25.0 8.4 %copy-start.2 = (s32[8,8]{1,0:T(8,128)S(1)}, s32[8,8]{1,0:T(8,128)}, u32[]{:S(2)}) copy-start(s32[8,8]{1,0:T(8,128)} %flags_ref.3) | copy-start | bytes 772
  25.0 8.4 %copy-start.4 = (s32[8]{0:T(128)S(1)}, s32[8]{0:T(128)}, u32[]{:S(2)}) copy-start(s32[8]{0:T(128)} %constant.57.clone.hops_ref) | copy-start | bytes 100
  25.7 16.9 %collective-permute-start = (bf16[4,128,256]{2,1,0:T(8,128)(2,1)S(1)}, bf16[4,128,256]{2,1,0:T(8,128)(2,1)S(1)}, u32[]{:S(2)}, u32[]{:S(2)}) collective-permute-start(bf16[4,128,256]{2,1,0:T(8,128)(2,1)S(1)} %copy-done.12), channel_id=1, source_target_pairs={{0,6},{1,7},{2,4},{3,5},{4,2},{5,3},{6,0},{7,1},{8,14},{9,15},{10,... | collective-permute-start | bytes 786440 | tf_op jit(solution)/shard_map/ppermute | solution.py:242
  28.1 15.3 %collective-permute-start.1 = (bf16[4,128,256]{2,1,0:T(8,128)(2,1)S(1)}, bf16[4,128,256]{2,1,0:T(8,128)(2,1)S(1)}, u32[]{:S(2)}, u32[]{:S(2)}) collective-permute-start(bf16[4,128,256]{2,1,0:T(8,128)(2,1)S(1)} %copy-done.11), channel_id=1, source_target_pairs={{0,7},{1,6},{2,5},{3,4},{4,3},{5,2},{6,1},{7,0},{8,15},{9,14},{10,... | collective-permute-start | bytes 786440 | tf_op jit(solution)/shard_map/ppermute | solution.py:242
  30.3 17.8 %collective-permute-start.2 = (bf16[4,128,256]{2,1,0:T(8,128)(2,1)S(1)}, bf16[4,128,256]{2,1,0:T(8,128)(2,1)S(1)}, u32[]{:S(2)}, u32[]{:S(2)}) collective-permute-start(bf16[4,128,256]{2,1,0:T(8,128)(2,1)S(1)} %copy-done.10), channel_id=1, source_target_pairs={{0,2},{1,3},{2,0},{3,1},{4,6},{5,7},{6,4},{7,5},{8,10},{9,11},{10,... | collective-permute-start | bytes 786440 | tf_op jit(solution)/shard_map/ppermute | solution.py:242
  30.8 18.7 %collective-permute-start.3 = (bf16[4,128,256]{2,1,0:T(8,128)(2,1)S(1)}, bf16[4,128,256]{2,1,0:T(8,128)(2,1)S(1)}, u32[]{:S(2)}, u32[]{:S(2)}) collective-permute-start(bf16[4,128,256]{2,1,0:T(8,128)(2,1)S(1)} %copy-done.9), channel_id=1, source_target_pairs={{0,4},{1,5},{2,6},{3,7},{4,0},{5,1},{6,2},{7,3},{8,12},{9,13},{10,... | collective-permute-start | bytes 786440 | tf_op jit(solution)/shard_map/ppermute | solution.py:242
  32.5 20.2 %collective-permute-start.4 = (bf16[4,128,256]{2,1,0:T(8,128)(2,1)S(1)}, bf16[4,128,256]{2,1,0:T(8,128)(2,1)S(1)}, u32[]{:S(2)}, u32[]{:S(2)}) collective-permute-start(bf16[4,128,256]{2,1,0:T(8,128)(2,1)S(1)} %copy-done.8), channel_id=1, source_target_pairs={{0,3},{1,2},{2,1},{3,0},{4,7},{5,6},{6,5},{7,4},{8,11},{9,10},{10,... | collective-permute-start | bytes 786440 | tf_op jit(solution)/shard_map/ppermute | solution.py:242
  33.4 9.2 %copy-start.7 = (bf16[4,128,256]{2,1,0:T(8,128)(2,1)S(1)}, bf16[4,128,256]{2,1,0:T(8,128)(2,1)}, u32[]{:S(2)}) copy-start(bf16[4,128,256]{2,1,0:T(8,128)(2,1)} %get-tuple-element.98) | copy-start | bytes 786436
  33.4 9.9 %copy-start.6 = (bf16[4,128,256]{2,1,0:T(8,128)(2,1)S(1)}, bf16[4,128,256]{2,1,0:T(8,128)(2,1)}, u32[]{:S(2)}) copy-start(bf16[4,128,256]{2,1,0:T(8,128)(2,1)} %get-tuple-element.99) | copy-start | bytes 786436
  33.4 22.4 %copy-start = (bf16[4,128,256]{2,1,0:T(8,128)(2,1)S(1)}, bf16[4,128,256]{2,1,0:T(8,128)(2,1)}, u32[]{:S(2)}) copy-start(bf16[4,128,256]{2,1,0:T(8,128)(2,1)} %get-tuple-element.74.rest_0_) | copy-start | bytes 786436
  42.6 10.6 %collective-permute-start.12 = (bf16[4,128,256]{2,1,0:T(8,128)(2,1)S(1)}, bf16[4,128,256]{2,1,0:T(8,128)(2,1)S(1)}, u32[]{:S(2)}, u32[]{:S(2)}) collective-permute-start(bf16[4,128,256]{2,1,0:T(8,128)(2,1)S(1)} %copy-done.7), channel_id=1, source_target_pairs={{0,5},{1,4},{2,7},{3,6},{4,1},{5,0},{6,3},{7,2},{8,13},{9,12},{10,... | collective-permute-start | bytes 786440 | tf_op jit(solution)/shard_map/ppermute | solution.py:242
  43.4 11.6 %collective-permute-start.13 = (bf16[4,128,256]{2,1,0:T(8,128)(2,1)S(1)}, bf16[4,128,256]{2,1,0:T(8,128)(2,1)S(1)}, u32[]{:S(2)}, u32[]{:S(2)}) collective-permute-start(bf16[4,128,256]{2,1,0:T(8,128)(2,1)S(1)} %copy-done.6), channel_id=1, source_target_pairs={{0,1},{1,0},{2,3},{3,2},{4,5},{5,4},{6,7},{7,6},{8,9},{9,8},{10,11... | collective-permute-start | bytes 786440 | tf_op jit(solution)/shard_map/ppermute | solution.py:242
  48.0 17.1 %collective-permute-start.21 = (bf16[4,128,256]{2,1,0:T(8,128)(2,1)S(1)}, bf16[4,128,256]{2,1,0:T(8,128)(2,1)S(1)}, u32[]{:S(2)}, u32[]{:S(2)}) collective-permute-start(bf16[4,128,256]{2,1,0:T(8,128)(2,1)S(1)} %get-tuple-element.109), channel_id=1, source_target_pairs={{0,6},{1,7},{2,4},{3,5},{4,2},{5,3},{6,0},{7,1},{8,14},{9,15},{10,... | collective-permute-start | bytes 786440 | tf_op jit(solution)/shard_map/ppermute | solution.py:242
  49.5 16.6 %collective-permute-start.22 = (bf16[4,128,256]{2,1,0:T(8,128)(2,1)S(1)}, bf16[4,128,256]{2,1,0:T(8,128)(2,1)S(1)}, u32[]{:S(2)}, u32[]{:S(2)}) collective-permute-start(bf16[4,128,256]{2,1,0:T(8,128)(2,1)S(1)} %get-tuple-element.110), channel_id=1, source_target_pairs={{0,7},{1,6},{2,5},{3,4},{4,3},{5,2},{6,1},{7,0},{8,15},{9,14},{10,... | collective-permute-start | bytes 786440 | tf_op jit(solution)/shard_map/ppermute | solution.py:242
  52.7 17.9 %collective-permute-start.23 = (bf16[4,128,256]{2,1,0:T(8,128)(2,1)S(1)}, bf16[4,128,256]{2,1,0:T(8,128)(2,1)S(1)}, u32[]{:S(2)}, u32[]{:S(2)}) collective-permute-start(bf16[4,128,256]{2,1,0:T(8,128)(2,1)S(1)} %get-tuple-element.111), channel_id=1, source_target_pairs={{0,2},{1,3},{2,0},{3,1},{4,6},{5,7},{6,4},{7,5},{8,10},{9,11},{10,... | collective-permute-start | bytes 786440 | tf_op jit(solution)/shard_map/ppermute | solution.py:242
  53.2 18.8 %collective-permute-start.24 = (bf16[4,128,256]{2,1,0:T(8,128)(2,1)S(1)}, bf16[4,128,256]{2,1,0:T(8,128)(2,1)S(1)}, u32[]{:S(2)}, u32[]{:S(2)}) collective-permute-start(bf16[4,128,256]{2,1,0:T(8,128)(2,1)S(1)} %get-tuple-element.112), channel_id=1, source_target_pairs={{0,4},{1,5},{2,6},{3,7},{4,0},{5,1},{6,2},{7,3},{8,12},{9,13},{10,... | collective-permute-start | bytes 786440 | tf_op jit(solution)/shard_map/ppermute | solution.py:242
  55.0 20.2 %collective-permute-start.25 = (bf16[4,128,256]{2,1,0:T(8,128)(2,1)S(1)}, bf16[4,128,256]{2,1,0:T(8,128)(2,1)S(1)}, u32[]{:S(2)}, u32[]{:S(2)}) collective-permute-start(bf16[4,128,256]{2,1,0:T(8,128)(2,1)S(1)} %get-tuple-element.113), channel_id=1, source_target_pairs={{0,3},{1,2},{2,1},{3,0},{4,7},{5,6},{6,5},{7,4},{8,11},{9,10},{10,... | collective-permute-start | bytes 786440 | tf_op jit(solution)/shard_map/ppermute | solution.py:242
  65.1 10.6 %collective-permute-start.26 = (bf16[4,128,256]{2,1,0:T(8,128)(2,1)S(1)}, bf16[4,128,256]{2,1,0:T(8,128)(2,1)S(1)}, u32[]{:S(2)}, u32[]{:S(2)}) collective-permute-start(bf16[4,128,256]{2,1,0:T(8,128)(2,1)S(1)} %get-tuple-element.114), channel_id=1, source_target_pairs={{0,5},{1,4},{2,7},{3,6},{4,1},{5,0},{6,3},{7,2},{8,13},{9,12},{10,... | collective-permute-start | bytes 786440 | tf_op jit(solution)/shard_map/ppermute | solution.py:242
  66.1 11.4 %collective-permute-start.27 = (bf16[4,128,256]{2,1,0:T(8,128)(2,1)S(1)}, bf16[4,128,256]{2,1,0:T(8,128)(2,1)S(1)}, u32[]{:S(2)}, u32[]{:S(2)}) collective-permute-start(bf16[4,128,256]{2,1,0:T(8,128)(2,1)S(1)} %get-tuple-element.115), channel_id=1, source_target_pairs={{0,1},{1,0},{2,3},{3,2},{4,5},{5,4},{6,7},{7,6},{8,9},{9,8},{10,11... | collective-permute-start | bytes 786440 | tf_op jit(solution)/shard_map/ppermute | solution.py:242
  70.6 11.0 %collective-permute-start.19 = (bf16[4,128,256]{2,1,0:T(8,128)(2,1)S(1)}, bf16[4,128,256]{2,1,0:T(8,128)(2,1)S(1)}, u32[]{:S(2)}, u32[]{:S(2)}) collective-permute-start(bf16[4,128,256]{2,1,0:T(8,128)(2,1)S(1)} %get-tuple-element.106), channel_id=1, source_target_pairs={{0,6},{1,7},{2,4},{3,5},{4,2},{5,3},{6,0},{7,1},{8,14},{9,15},{10,... | collective-permute-start | bytes 786440 | tf_op jit(solution)/shard_map/ppermute | solution.py:242
  72.0 14.5 %collective-permute-start.20 = (bf16[4,128,256]{2,1,0:T(8,128)(2,1)S(1)}, bf16[4,128,256]{2,1,0:T(8,128)(2,1)S(1)}, u32[]{:S(2)}, u32[]{:S(2)}) collective-permute-start(bf16[4,128,256]{2,1,0:T(8,128)(2,1)S(1)} %get-tuple-element.107), channel_id=1, source_target_pairs={{0,7},{1,6},{2,5},{3,4},{4,3},{5,2},{6,1},{7,0},{8,15},{9,14},{10,... | collective-permute-start | bytes 786440 | tf_op jit(solution)/shard_map/ppermute | solution.py:242
  75.2 17.9 %collective-permute-start.14 = (bf16[4,128,256]{2,1,0:T(8,128)(2,1)S(1)}, bf16[4,128,256]{2,1,0:T(8,128)(2,1)S(1)}, u32[]{:S(2)}, u32[]{:S(2)}) collective-permute-start(bf16[4,128,256]{2,1,0:T(8,128)(2,1)S(1)} %get-tuple-element.100), channel_id=1, source_target_pairs={{0,2},{1,3},{2,0},{3,1},{4,6},{5,7},{6,4},{7,5},{8,10},{9,11},{10,... | collective-permute-start | bytes 786440 | tf_op jit(solution)/shard_map/ppermute | solution.py:242
  75.8 17.3 %collective-permute-start.15 = (bf16[4,128,256]{2,1,0:T(8,128)(2,1)S(1)}, bf16[4,128,256]{2,1,0:T(8,128)(2,1)S(1)}, u32[]{:S(2)}, u32[]{:S(2)}) collective-permute-start(bf16[4,128,256]{2,1,0:T(8,128)(2,1)S(1)} %get-tuple-element.101), channel_id=1, source_target_pairs={{0,4},{1,5},{2,6},{3,7},{4,0},{5,1},{6,2},{7,3},{8,12},{9,13},{10,... | collective-permute-start | bytes 786440 | tf_op jit(solution)/shard_map/ppermute | solution.py:242
  77.5 19.3 %collective-permute-start.16 = (bf16[4,128,256]{2,1,0:T(8,128)(2,1)S(1)}, bf16[4,128,256]{2,1,0:T(8,128)(2,1)S(1)}, u32[]{:S(2)}, u32[]{:S(2)}) collective-permute-start(bf16[4,128,256]{2,1,0:T(8,128)(2,1)S(1)} %get-tuple-element.102), channel_id=1, source_target_pairs={{0,3},{1,2},{2,1},{3,0},{4,7},{5,6},{6,5},{7,4},{8,11},{9,10},{10,... | collective-permute-start | bytes 786440 | tf_op jit(solution)/shard_map/ppermute | solution.py:242
  81.5 15.9 %collective-permute-start.17 = (bf16[4,128,256]{2,1,0:T(8,128)(2,1)S(1)}, bf16[4,128,256]{2,1,0:T(8,128)(2,1)S(1)}, u32[]{:S(2)}, u32[]{:S(2)}) collective-permute-start(bf16[4,128,256]{2,1,0:T(8,128)(2,1)S(1)} %get-tuple-element.103), channel_id=1, source_target_pairs={{0,5},{1,4},{2,7},{3,6},{4,1},{5,0},{6,3},{7,2},{8,13},{9,12},{10,... | collective-permute-start | bytes 786440 | tf_op jit(solution)/shard_map/ppermute | solution.py:242
  86.5 11.0 %collective-permute-start.18 = (bf16[4,128,256]{2,1,0:T(8,128)(2,1)S(1)}, bf16[4,128,256]{2,1,0:T(8,128)(2,1)S(1)}, u32[]{:S(2)}, u32[]{:S(2)}) collective-permute-start(bf16[4,128,256]{2,1,0:T(8,128)(2,1)S(1)} %get-tuple-element.104), channel_id=1, source_target_pairs={{0,1},{1,0},{2,3},{3,2},{4,5},{5,4},{6,7},{7,6},{8,9},{9,8},{10,11... | collective-permute-start | bytes 786440 | tf_op jit(solution)/shard_map/ppermute | solution.py:242

commit v4 on v3

--- a/solution.py
+++ b/solution.py
@@ -246,12 +246,12 @@
     def pack(c, slots):
         return pl.pallas_call(
             functools.partial(pack_kernel, [hops[s] for s in slots], heads, c * count, count),
-            out_shape=[piece] * len(slots),
+            out_shape=[pltpu.VMEM(piece.shape, BF16) if c == 0 and len(slots) == EARLY else piece] * len(slots),
             in_specs=[SMEM] + [ANY] * 4,
             out_specs=[VMEM] * len(slots),
             scratch_shapes=[pltpu.SemaphoreType.DMA((len(slots), 4))],
             name=f"pack_{c}_{slots[0]}",
-        )(me, *arrays)
+        )(me, *[pltpu.with_memory_space_constraint(a, pltpu.HBM) for a in arrays])
 
     def prepare(c):
         order = [*range(1, groups), 0]

time: 99.2 us -> 98.2 us (0.990)
  transfers between devices with their start and end apart: 28 -> 28, of which waited for: 13 -> 13; matrix products, arithmetic and copies ran while one was open for 3% -> 3% of each run, Pallas kernels for 27% -> 28%
where the time goes in v4:
time: 98.2 us; the launch traced here: 97.8 us
  waiting for transfers between devices  39.3 us (40%)
  Pallas kernels  29.3 us (30%)
  starting transfers between devices  25.1 us (26%)
  other arithmetic  2.92 us (3%)
  between operations  1.04 us (1%)
    ppermute x28, waiting for transfers between devices, exchange(): lax.ppermute(piece, 'seq', [(i, i ^ d) for i in range(groups)])  39.3 us
    ppermute x28, starting transfers between devices, exchange(): lax.ppermute(piece, 'seq', [(i, i ^ d) for i in range(groups)])  25.1 us
    pallas_call x2, Pallas kernels, attention_call(): pl.pallas_call(functools.partial(attention_kernel, hops, rows, count, wid...  18.5 us
    pallas_call x3, Pallas kernels, pack(): pl.pallas_call(functools.partial(pack_kernel, [hops[s] for s in slots], h...  7.13 us
    pallas_call x3, Pallas kernels, unpack(): pl.pallas_call(functools.partial(unpack_kernel, [hops[s] for s in slots],...  3.75 us
    mul x1, other arithmetic, rope_tables(): return (jnp.cos(angle), jnp.sin(angle) * sign[None, :])  2.35 us
  transfers between devices with their start and end apart: 28, of which 13 were waited for; matrix products, arithmetic and copies ran while one was open for 3% of the time, Pallas kernels for 28%

profile of v4, /device:TPU:0, one launch (start us, length us, event | category | flops | bytes accessed | tf_op | source)
XLA Modules:
  0.0 97.8 jit_solution(4613735553436803107)
XLA Ops:
  0.6 1.1 %pack_0_1.1 = (bf16[4,128,256]{2,1,0:T(8,128)(2,1)S(1)}, bf16[4,128,256]{2,1,0:T(8,128)(2,1)S(1)}) custom-call(s32[1]{0:T(128)} %bitcast.me_ref, bf16[128,4096]{1,0:T(8,128)(2,1)} %q_ref.5, bf16[128,4096]{1,0:T(8,128)(2,1)} %k_ref.5, bf16[128,4096]{1,0:T(8,128)(2,1)} %v_ref.5, bf16[128,4096]{1,0:T(8,128)(2,1)} %g_ref.5), custom_call_target="tpu_custom_call" | custom-call | tf_op jit(solution)/shard_map/pack_0_1/pallas_call | solution.py:247
  1.8 4.0 %collective-permute-start.5 = (bf16[4,128,256]{2,1,0:T(8,128)(2,1)S(1)}, bf16[4,128,256]{2,1,0:T(8,128)(2,1)S(1)}, u32[]{:S(2)}, u32[]{:S(2)}) collective-permute-start(bf16[4,128,256]{2,1,0:T(8,128)(2,1)S(1)} %get-tuple-element.83), channel_id=1, source_target_pairs={{0,6},{1,7},{2,4},{3,5},{4,2},{5,3},{6,0},{7,1},{8,14},{9,15},{10,... | collective-permute-start | bytes 786440 | tf_op jit(solution)/shard_map/ppermute | solution.py:242
  5.7 2.8 %pack_0_3.1 = (bf16[4,128,256]{2,1,0:T(8,128)(2,1)}, bf16[4,128,256]{2,1,0:T(8,128)(2,1)}, bf16[4,128,256]{2,1,0:T(8,128)(2,1)}, bf16[4,128,256]{2,1,0:T(8,128)(...) custom-call(s32[1]{0:T(128)} %bitcast.me_ref, bf16[128,4096]{1,0:T(8,128)(2,1)} %q_ref.5, ...), custom_call_target="tpu_custom_call" | custom-call | tf_op jit(solution)/shard_map/pack_0_3/pallas_call | solution.py:247
  8.6 1.2 %collective-permute-start.7 = (bf16[4,128,256]{2,1,0:T(8,128)(2,1)}, bf16[4,128,256]{2,1,0:T(8,128)(2,1)S(1)}, u32[]{:S(2)}, u32[]{:S(2)}) collective-permute-start(bf16[4,128,256]{2,1,0:T(8,128)(2,1)} %get-tuple-element.85), channel_id=1, source_target_pairs={{0,2},{1,3},{2,0},{3,1},{4,6},{5,7},{6,4},{7,5},{8,10},{9,11},{10,... | collective-permute-start | bytes 786440 | tf_op jit(solution)/shard_map/ppermute | solution.py:242
  9.7 1.5 %collective-permute-start.8 = (bf16[4,128,256]{2,1,0:T(8,128)(2,1)}, bf16[4,128,256]{2,1,0:T(8,128)(2,1)S(1)}, u32[]{:S(2)}, u32[]{:S(2)}) collective-permute-start(bf16[4,128,256]{2,1,0:T(8,128)(2,1)} %get-tuple-element.86), channel_id=1, source_target_pairs={{0,4},{1,5},{2,6},{3,7},{4,0},{5,1},{6,2},{7,3},{8,12},{9,13},{10,... | collective-permute-start | bytes 786440 | tf_op jit(solution)/shard_map/ppermute | solution.py:242
  11.3 0.6 collective-permute-start.9
  11.9 0.2 broadcast_multiply_fusion.2
  12.1 0.3 broadcast_multiply_fusion.1
  12.4 0.5 collective-permute-done.5.rest_1_
  12.9 0.2 collective-permute-start.10
  13.1 5.0 %collective-permute-done.6.rest_2_ = bf16[4,128,256]{2,1,0:T(8,128)(2,1)S(1)} collective-permute-done((bf16[4,128,256]{2,1,0:T(8,128)(2,1)S(1)}, bf16[4,128,256]{2,1,0:T(8,128)(2,1)S(1)}, u32[]{:S(2)}, u32[]{:S(2)}) %collective-permute-start.6) | collective-permute-done | bytes 262176 | tf_op jit(solution)/shard_map/ppermute | solution.py:242
  18.1 0.2 collective-permute-start.11
  18.4 3.2 %pack_1_1.1 = (bf16[4,128,256]{2,1,0:T(8,128)(2,1)}, bf16[4,128,256]{2,1,0:T(8,128)(2,1)}, bf16[4,128,256]{2,1,0:T(8,128)(2,1)}, bf16[4,128,256]{2,1,0:T(8,128)(...) custom-call(s32[1]{0:T(128)} %bitcast.me_ref, ...), custom_call_target="tpu_custom_call" | custom-call | tf_op jit(solution)/shard_map/pack_1_1/pallas_call | solution.py:247
  21.6 0.0 copy-start.12
  21.6 0.0 copy-start.11
  21.6 0.0 copy-start.10
  21.6 0.0 copy-start.9
  21.6 2.4 %sine_multiply_fusion = (f32[1024,128]{1,0:T(8,128)S(1)}, f32[1024,128]{1,0:T(8,128)S(1)}) fusion(f32[128]{0:T(128)S(1)} %compare_select_fusion, f32[1024,42]{1,0:T(8,128)S(1)} %get-tuple-element.130, f32[1024,42]{1,0:T(8,128)S(1)} %get-tuple-element.129, f32[1024,44]{1,0:T(8,128)S(1)} %broadcast_multiply_fusion.2), kind=kLoop, calls=%fused_computation.1 | loop fusion | flops 393216 | bytes 1573376 | tf_op jit(solution)/shard_map/mul | solution.py:38
  24.0 0.0 copy-start.3
  24.0 0.0 copy-start.2
  24.0 0.0 copy-start.4
  24.0 0.7 collective-permute-done.7.rest_3_
  24.7 2.3 %collective-permute-start = (bf16[4,128,256]{2,1,0:T(8,128)(2,1)S(1)}, bf16[4,128,256]{2,1,0:T(8,128)(2,1)S(1)}, u32[]{:S(2)}, u32[]{:S(2)}) collective-permute-start(bf16[4,128,256]{2,1,0:T(8,128)(2,1)S(1)} %copy-done.12), channel_id=1, source_target_pairs={{0,6},{1,7},{2,4},{3,5},{4,2},{5,3},{6,0},{7,1},{8,14},{9,15},{10,... | collective-permute-start | bytes 786440 | tf_op jit(solution)/shard_map/ppermute | solution.py:242
  27.1 0.0 collective-permute-start.1
  27.1 2.2 %collective-permute-done.9.rest_5_ = bf16[4,128,256]{2,1,0:T(8,128)(2,1)S(1)} collective-permute-done((bf16[4,128,256]{2,1,0:T(8,128)(2,1)}, bf16[4,128,256]{2,1,0:T(8,128)(2,1)S(1)}, u32[]{:S(2)}, u32[]{:S(2)}) %collective-permute-start.9) | collective-permute-done | bytes 262176 | tf_op jit(solution)/shard_map/ppermute | solution.py:242
  29.3 0.5 collective-permute-start.2
  29.8 0.0 collective-permute-done.10.rest_6_
  29.8 1.7 %collective-permute-start.3 = (bf16[4,128,256]{2,1,0:T(8,128)(2,1)S(1)}, bf16[4,128,256]{2,1,0:T(8,128)(2,1)S(1)}, u32[]{:S(2)}, u32[]{:S(2)}) collective-permute-start(bf16[4,128,256]{2,1,0:T(8,128)(2,1)S(1)} %copy-done.9), channel_id=1, source_target_pairs={{0,4},{1,5},{2,6},{3,7},{4,0},{5,1},{6,2},{7,3},{8,12},{9,13},{10,... | collective-permute-start | bytes 786440 | tf_op jit(solution)/shard_map/ppermute | solution.py:242
  31.5 0.0 collective-permute-done.11.rest_7_
  31.5 0.9 collective-permute-start.4
  32.5 9.1 %attention.2 = (bf16[4,128,256]{2,1,0:T(8,128)(2,1)S(1)}, bf16[4,128,256]{2,1,0:T(8,128)(2,1)S(1)}, bf16[4,128,256]{2,1,0:T(8,128)(2,1)S(1)}, bf16[4,128,256]{2,...) custom-call(s32[1]{0:T(128)} %bitcast.me_ref, ...), custom_call_target="tpu_custom_call" | custom-call | flops 2684354560 | bytes 4194304 | tf_op jit(solution)/shard_map/attention/pallas_call | solution.py:208
  41.6 0.7 collective-permute-start.12
  42.4 0.4 collective-permute-start.13
  42.8 4.2 %collective-permute-done.2.rest_3_ = bf16[4,128,256]{2,1,0:T(8,128)(2,1)S(1)} collective-permute-done((bf16[4,128,256]{2,1,0:T(8,128)(2,1)S(1)}, bf16[4,128,256]{2,1,0:T(8,128)(2,1)S(1)}, u32[]{:S(2)}, u32[]{:S(2)}) %collective-permute-start.2) | collective-permute-done | bytes 262176 | tf_op jit(solution)/shard_map/ppermute | solution.py:242
  47.0 1.4 %collective-permute-start.21 = (bf16[4,128,256]{2,1,0:T(8,128)(2,1)S(1)}, bf16[4,128,256]{2,1,0:T(8,128)(2,1)S(1)}, u32[]{:S(2)}, u32[]{:S(2)}) collective-permute-start(bf16[4,128,256]{2,1,0:T(8,128)(2,1)S(1)} %get-tuple-element.109), channel_id=1, source_target_pairs={{0,6},{1,7},{2,4},{3,5},{4,2},{5,3},{6,0},{7,1},{8,14},{9,15},{10,... | collective-permute-start | bytes 786440 | tf_op jit(solution)/shard_map/ppermute | solution.py:242
  48.5 0.0 collective-permute-done.3.rest_4_
  48.5 3.2 %collective-permute-done.4.rest_5_ = bf16[4,128,256]{2,1,0:T(8,128)(2,1)S(1)} collective-permute-done((bf16[4,128,256]{2,1,0:T(8,128)(2,1)S(1)}, bf16[4,128,256]{2,1,0:T(8,128)(2,1)S(1)}, u32[]{:S(2)}, u32[]{:S(2)}) %collective-permute-start.4) | collective-permute-done | bytes 262176 | tf_op jit(solution)/shard_map/ppermute | solution.py:242
  51.7 0.6 collective-permute-start.23
  52.2 0.0 collective-permute-done.12.rest_6_
  52.2 1.7 %collective-permute-start.24 = (bf16[4,128,256]{2,1,0:T(8,128)(2,1)S(1)}, bf16[4,128,256]{2,1,0:T(8,128)(2,1)S(1)}, u32[]{:S(2)}, u32[]{:S(2)}) collective-permute-start(bf16[4,128,256]{2,1,0:T(8,128)(2,1)S(1)} %get-tuple-element.112), channel_id=1, source_target_pairs={{0,4},{1,5},{2,6},{3,7},{4,0},{5,1},{6,2},{7,3},{8,12},{9,13},{10,... | collective-permute-start | bytes 786440 | tf_op jit(solution)/shard_map/ppermute | solution.py:242
  54.0 0.0 collective-permute-done.13.rest_7_
  54.0 0.9 collective-permute-start.25
  54.8 9.3 %attention.3 = (bf16[4,128,256]{2,1,0:T(8,128)(2,1)S(1)}, bf16[4,128,256]{2,1,0:T(8,128)(2,1)S(1)}, bf16[4,128,256]{2,1,0:T(8,128)(2,1)S(1)}, bf16[4,128,256]{2,...) custom-call(s32[1]{0:T(128)} %bitcast.me_ref, ...), custom_call_target="tpu_custom_call" | custom-call | flops 2684354560 | bytes 4194304 | tf_op jit(solution)/shard_map/attention/pallas_call | solution.py:208
  64.1 0.0 collective-permute-done.21.rest_1_
  64.1 1.0 collective-permute-start.26
  65.1 0.3 collective-permute-start.27
  65.4 4.2 %collective-permute-done.23.rest_3_ = bf16[4,128,256]{2,1,0:T(8,128)(2,1)S(1)} collective-permute-done((bf16[4,128,256]{2,1,0:T(8,128)(2,1)S(1)}, bf16[4,128,256]{2,1,0:T(8,128)(2,1)S(1)}, u32[]{:S(2)}, u32[]{:S(2)}) %collective-permute-start.23) | collective-permute-done | bytes 262176 | tf_op jit(solution)/shard_map/ppermute | solution.py:242
  69.6 1.4 %collective-permute-start.19 = (bf16[4,128,256]{2,1,0:T(8,128)(2,1)S(1)}, bf16[4,128,256]{2,1,0:T(8,128)(2,1)S(1)}, u32[]{:S(2)}, u32[]{:S(2)}) collective-permute-start(bf16[4,128,256]{2,1,0:T(8,128)(2,1)S(1)} %get-tuple-element.106), channel_id=1, source_target_pairs={{0,6},{1,7},{2,4},{3,5},{4,2},{5,3},{6,0},{7,1},{8,14},{9,15},{10,... | collective-permute-start | bytes 786440 | tf_op jit(solution)/shard_map/ppermute | solution.py:242
  71.0 0.0 collective-permute-done.24.rest_4_
  71.0 0.0 collective-permute-start.20
  71.0 3.2 %collective-permute-done.25.rest_5_ = bf16[4,128,256]{2,1,0:T(8,128)(2,1)S(1)} collective-permute-done((bf16[4,128,256]{2,1,0:T(8,128)(2,1)S(1)}, bf16[4,128,256]{2,1,0:T(8,128)(2,1)S(1)}, u32[]{:S(2)}, u32[]{:S(2)}) %collective-permute-start.25) | collective-permute-done | bytes 262176 | tf_op jit(solution)/shard_map/ppermute | solution.py:242
  74.2 0.6 collective-permute-start.14
  74.8 1.7 %collective-permute-start.15 = (bf16[4,128,256]{2,1,0:T(8,128)(2,1)S(1)}, bf16[4,128,256]{2,1,0:T(8,128)(2,1)S(1)}, u32[]{:S(2)}, u32[]{:S(2)}) collective-permute-start(bf16[4,128,256]{2,1,0:T(8,128)(2,1)S(1)} %get-tuple-element.101), channel_id=1, source_target_pairs={{0,4},{1,5},{2,6},{3,7},{4,0},{5,1},{6,2},{7,3},{8,12},{9,13},{10,... | collective-permute-start | bytes 786440 | tf_op jit(solution)/shard_map/ppermute | solution.py:242
  76.5 0.0 collective-permute-done.27.rest_7_
  76.5 0.8 collective-permute-start.16
  77.3 3.2 %collective-permute-done.19.rest_1_ = bf16[4,128,256]{2,1,0:T(8,128)(2,1)S(1)} collective-permute-done((bf16[4,128,256]{2,1,0:T(8,128)(2,1)S(1)}, bf16[4,128,256]{2,1,0:T(8,128)(2,1)S(1)}, u32[]{:S(2)}, u32[]{:S(2)}) %collective-permute-start.19) | collective-permute-done | bytes 262176 | tf_op jit(solution)/shard_map/ppermute | solution.py:242
  80.5 4.9 %collective-permute-done.20.rest_2_ = bf16[4,128,256]{2,1,0:T(8,128)(2,1)S(1)} collective-permute-done((bf16[4,128,256]{2,1,0:T(8,128)(2,1)S(1)}, bf16[4,128,256]{2,1,0:T(8,128)(2,1)S(1)}, u32[]{:S(2)}, u32[]{:S(2)}) %collective-permute-start.20) | collective-permute-done | bytes 262176 | tf_op jit(solution)/shard_map/ppermute | solution.py:242
  85.5 0.4 collective-permute-start.18
  85.9 1.6 %unpack_0_0.1 = (bf16[128,4096]{1,0:T(8,128)(2,1)}, bf16[128,4096]{1,0:T(8,128)(2,1)}, bf16[128,4096]{1,0:T(8,128)(2,1)}, bf16[128,4096]{1,0:T(8,128)(2,1)}) custom-call(s32[1]{0:T(128)} %bitcast.me_ref, bf16[4,128,256]{2,1,0:T(8,128)(2,1)S(1)} %get-tuple-element.108.rest_0_, bf16[4,128,256]{2,1,0:T(8,128)(2,1)S(1)} %collective-permute-done.21.rest_1_, ...), custom_call_target="tpu_custom_call" | custom-call | tf_op jit(solution)/shard_map/unpack_0_0/pallas_call | solution.py:264
  87.5 1.0 unpack_1_0.1
  88.5 3.6 %collective-permute-done.14.rest_0_ = bf16[4,128,256]{2,1,0:T(8,128)(2,1)S(1)} collective-permute-done((bf16[4,128,256]{2,1,0:T(8,128)(2,1)S(1)}, bf16[4,128,256]{2,1,0:T(8,128)(2,1)S(1)}, u32[]{:S(2)}, u32[]{:S(2)}) %collective-permute-start.14) | collective-permute-done | bytes 262176 | tf_op jit(solution)/shard_map/ppermute | solution.py:242
  92.1 3.7 %collective-permute-done.16.rest_2_ = bf16[4,128,256]{2,1,0:T(8,128)(2,1)S(1)} collective-permute-done((bf16[4,128,256]{2,1,0:T(8,128)(2,1)S(1)}, bf16[4,128,256]{2,1,0:T(8,128)(2,1)S(1)}, u32[]{:S(2)}, u32[]{:S(2)}) %collective-permute-start.16) | collective-permute-done | bytes 262176 | tf_op jit(solution)/shard_map/ppermute | solution.py:242
  95.8 0.7 collective-permute-done.17.rest_3_
  96.4 1.2 %unpack_1_3.1 = (bf16[128,4096]{1,0:T(8,128)(2,1)}, bf16[128,4096]{1,0:T(8,128)(2,1)}, bf16[128,4096]{1,0:T(8,128)(2,1)}, bf16[128,4096]{1,0:T(8,128)(2,1)}) custom-call(s32[1]{0:T(128)} %bitcast.me_ref, bf16[4,128,256]{2,1,0:T(8,128)(2,1)S(1)} %collective-permute-done.14.rest_0_, ...), custom_call_target="tpu_custom_call", output_to_operand_aliasing={{0}: (6, {}), {1}: (7, {}), {2}: (8, {}), {3}: (9, {})} | custom-call | tf_op jit(solution)/shard_map/unpack_1_3/pallas_call | solution.py:264
  (33 shorter events, 0.1 us)
Async XLA Ops:
  1.8 11.1 %collective-permute-start.5 = (bf16[4,128,256]{2,1,0:T(8,128)(2,1)S(1)}, bf16[4,128,256]{2,1,0:T(8,128)(2,1)S(1)}, u32[]{:S(2)}, u32[]{:S(2)}) collective-permute-start(bf16[4,128,256]{2,1,0:T(8,128)(2,1)S(1)} %get-tuple-element.83), channel_id=1, source_target_pairs={{0,6},{1,7},{2,4},{3,5},{4,2},{5,3},{6,0},{7,1},{8,14},{9,15},{10,... | collective-permute-start | bytes 786440 | tf_op jit(solution)/shard_map/ppermute | solution.py:242
  5.7 6.1 %copy-start.5 = (s32[3,1024]{1,0:T(4,128)S(1)}, s32[3,1024]{1,0:T(4,128)}, u32[]{:S(2)}) copy-start(s32[3,1024]{1,0:T(4,128)} %param.13) | copy-start | bytes 36868
  5.7 12.4 %collective-permute-start.6 = (bf16[4,128,256]{2,1,0:T(8,128)(2,1)S(1)}, bf16[4,128,256]{2,1,0:T(8,128)(2,1)S(1)}, u32[]{:S(2)}, u32[]{:S(2)}) collective-permute-start(bf16[4,128,256]{2,1,0:T(8,128)(2,1)S(1)} %get-tuple-element.84), channel_id=1, source_target_pairs={{0,7},{1,6},{2,5},{3,4},{4,3},{5,2},{6,1},{7,0},{8,15},{9,14},{10,... | collective-permute-start | bytes 786440 | tf_op jit(solution)/shard_map/ppermute | solution.py:242
  8.6 16.2 %collective-permute-start.7 = (bf16[4,128,256]{2,1,0:T(8,128)(2,1)}, bf16[4,128,256]{2,1,0:T(8,128)(2,1)S(1)}, u32[]{:S(2)}, u32[]{:S(2)}) collective-permute-start(bf16[4,128,256]{2,1,0:T(8,128)(2,1)} %get-tuple-element.85), channel_id=1, source_target_pairs={{0,2},{1,3},{2,0},{3,1},{4,6},{5,7},{6,4},{7,5},{8,10},{9,11},{10,... | collective-permute-start | bytes 786440 | tf_op jit(solution)/shard_map/ppermute | solution.py:242
  9.7 17.3 %collective-permute-start.8 = (bf16[4,128,256]{2,1,0:T(8,128)(2,1)}, bf16[4,128,256]{2,1,0:T(8,128)(2,1)S(1)}, u32[]{:S(2)}, u32[]{:S(2)}) collective-permute-start(bf16[4,128,256]{2,1,0:T(8,128)(2,1)} %get-tuple-element.86), channel_id=1, source_target_pairs={{0,4},{1,5},{2,6},{3,7},{4,0},{5,1},{6,2},{7,3},{8,12},{9,13},{10,... | collective-permute-start | bytes 786440 | tf_op jit(solution)/shard_map/ppermute | solution.py:242
  11.3 18.0 %collective-permute-start.9 = (bf16[4,128,256]{2,1,0:T(8,128)(2,1)}, bf16[4,128,256]{2,1,0:T(8,128)(2,1)S(1)}, u32[]{:S(2)}, u32[]{:S(2)}) collective-permute-start(bf16[4,128,256]{2,1,0:T(8,128)(2,1)} %get-tuple-element.87), channel_id=1, source_target_pairs={{0,3},{1,2},{2,1},{3,0},{4,7},{5,6},{6,5},{7,4},{8,11},{9,10},{10,... | collective-permute-start | bytes 786440 | tf_op jit(solution)/shard_map/ppermute | solution.py:242
  12.9 16.9 %collective-permute-start.10 = (bf16[4,128,256]{2,1,0:T(8,128)(2,1)}, bf16[4,128,256]{2,1,0:T(8,128)(2,1)S(1)}, u32[]{:S(2)}, u32[]{:S(2)}) collective-permute-start(bf16[4,128,256]{2,1,0:T(8,128)(2,1)} %get-tuple-element.88), channel_id=1, source_target_pairs={{0,5},{1,4},{2,7},{3,6},{4,1},{5,0},{6,3},{7,2},{8,13},{9,12},{10,... | collective-permute-start | bytes 786440 | tf_op jit(solution)/shard_map/ppermute | solution.py:242
  18.1 13.4 %collective-permute-start.11 = (bf16[4,128,256]{2,1,0:T(8,128)(2,1)}, bf16[4,128,256]{2,1,0:T(8,128)(2,1)S(1)}, u32[]{:S(2)}, u32[]{:S(2)}) collective-permute-start(bf16[4,128,256]{2,1,0:T(8,128)(2,1)} %get-tuple-element.89), channel_id=1, source_target_pairs={{0,1},{1,0},{2,3},{3,2},{4,5},{5,4},{6,7},{7,6},{8,9},{9,8},{10,11... | collective-permute-start | bytes 786440 | tf_op jit(solution)/shard_map/ppermute | solution.py:242
  21.6 3.2 %copy-start.12 = (bf16[4,128,256]{2,1,0:T(8,128)(2,1)S(1)}, bf16[4,128,256]{2,1,0:T(8,128)(2,1)}, u32[]{:S(2)}) copy-start(bf16[4,128,256]{2,1,0:T(8,128)(2,1)} %get-tuple-element.75) | copy-start | bytes 786436
  21.6 5.5 %copy-start.11 = (bf16[4,128,256]{2,1,0:T(8,128)(2,1)S(1)}, bf16[4,128,256]{2,1,0:T(8,128)(2,1)}, u32[]{:S(2)}) copy-start(bf16[4,128,256]{2,1,0:T(8,128)(2,1)} %get-tuple-element.76) | copy-start | bytes 786436
  21.6 7.7 %copy-start.10 = (bf16[4,128,256]{2,1,0:T(8,128)(2,1)S(1)}, bf16[4,128,256]{2,1,0:T(8,128)(2,1)}, u32[]{:S(2)}) copy-start(bf16[4,128,256]{2,1,0:T(8,128)(2,1)} %get-tuple-element.77) | copy-start | bytes 786436
  21.6 8.2 %copy-start.9 = (bf16[4,128,256]{2,1,0:T(8,128)(2,1)S(1)}, bf16[4,128,256]{2,1,0:T(8,128)(2,1)}, u32[]{:S(2)}) copy-start(bf16[4,128,256]{2,1,0:T(8,128)(2,1)} %get-tuple-element.78) | copy-start | bytes 786436
  21.6 9.9 %copy-start.8 = (bf16[4,128,256]{2,1,0:T(8,128)(2,1)S(1)}, bf16[4,128,256]{2,1,0:T(8,128)(2,1)}, u32[]{:S(2)}) copy-start(bf16[4,128,256]{2,1,0:T(8,128)(2,1)} %get-tuple-element.79) | copy-start | bytes 786436
  21.6 10.8 %copy-start.1 = (bf16[4,128,256]{2,1,0:T(8,128)(2,1)S(1)}, bf16[4,128,256]{2,1,0:T(8,128)(2,1)}, u32[]{:S(2)}) copy-start(bf16[4,128,256]{2,1,0:T(8,128)(2,1)} %get-tuple-element.82.rest_0_) | copy-start | bytes 786436
  24.0 8.4 %copy-start.3 = (s32[8,8]{1,0:T(8,128)S(1)}, s32[8,8]{1,0:T(8,128)}, u32[]{:S(2)}) copy-start(s32[8,8]{1,0:T(8,128)} %bands_ref.3) | copy-start | bytes 772
  24.0 8.4 %copy-start.2 = (s32[8,8]{1,0:T(8,128)S(1)}, s32[8,8]{1,0:T(8,128)}, u32[]{:S(2)}) copy-start(s32[8,8]{1,0:T(8,128)} %flags_ref.3) | copy-start | bytes 772
  24.0 8.4 %copy-start.4 = (s32[8]{0:T(128)S(1)}, s32[8]{0:T(128)}, u32[]{:S(2)}) copy-start(s32[8]{0:T(128)} %constant.57.clone.hops_ref) | copy-start | bytes 100
  24.7 16.9 %collective-permute-start = (bf16[4,128,256]{2,1,0:T(8,128)(2,1)S(1)}, bf16[4,128,256]{2,1,0:T(8,128)(2,1)S(1)}, u32[]{:S(2)}, u32[]{:S(2)}) collective-permute-start(bf16[4,128,256]{2,1,0:T(8,128)(2,1)S(1)} %copy-done.12), channel_id=1, source_target_pairs={{0,6},{1,7},{2,4},{3,5},{4,2},{5,3},{6,0},{7,1},{8,14},{9,15},{10,... | collective-permute-start | bytes 786440 | tf_op jit(solution)/shard_map/ppermute | solution.py:242
  27.1 15.3 %collective-permute-start.1 = (bf16[4,128,256]{2,1,0:T(8,128)(2,1)S(1)}, bf16[4,128,256]{2,1,0:T(8,128)(2,1)S(1)}, u32[]{:S(2)}, u32[]{:S(2)}) collective-permute-start(bf16[4,128,256]{2,1,0:T(8,128)(2,1)S(1)} %copy-done.11), channel_id=1, source_target_pairs={{0,7},{1,6},{2,5},{3,4},{4,3},{5,2},{6,1},{7,0},{8,15},{9,14},{10,... | collective-permute-start | bytes 786440 | tf_op jit(solution)/shard_map/ppermute | solution.py:242
  29.3 17.8 %collective-permute-start.2 = (bf16[4,128,256]{2,1,0:T(8,128)(2,1)S(1)}, bf16[4,128,256]{2,1,0:T(8,128)(2,1)S(1)}, u32[]{:S(2)}, u32[]{:S(2)}) collective-permute-start(bf16[4,128,256]{2,1,0:T(8,128)(2,1)S(1)} %copy-done.10), channel_id=1, source_target_pairs={{0,2},{1,3},{2,0},{3,1},{4,6},{5,7},{6,4},{7,5},{8,10},{9,11},{10,... | collective-permute-start | bytes 786440 | tf_op jit(solution)/shard_map/ppermute | solution.py:242
  29.8 18.7 %collective-permute-start.3 = (bf16[4,128,256]{2,1,0:T(8,128)(2,1)S(1)}, bf16[4,128,256]{2,1,0:T(8,128)(2,1)S(1)}, u32[]{:S(2)}, u32[]{:S(2)}) collective-permute-start(bf16[4,128,256]{2,1,0:T(8,128)(2,1)S(1)} %copy-done.9), channel_id=1, source_target_pairs={{0,4},{1,5},{2,6},{3,7},{4,0},{5,1},{6,2},{7,3},{8,12},{9,13},{10,... | collective-permute-start | bytes 786440 | tf_op jit(solution)/shard_map/ppermute | solution.py:242
  31.5 20.2 %collective-permute-start.4 = (bf16[4,128,256]{2,1,0:T(8,128)(2,1)S(1)}, bf16[4,128,256]{2,1,0:T(8,128)(2,1)S(1)}, u32[]{:S(2)}, u32[]{:S(2)}) collective-permute-start(bf16[4,128,256]{2,1,0:T(8,128)(2,1)S(1)} %copy-done.8), channel_id=1, source_target_pairs={{0,3},{1,2},{2,1},{3,0},{4,7},{5,6},{6,5},{7,4},{8,11},{9,10},{10,... | collective-permute-start | bytes 786440 | tf_op jit(solution)/shard_map/ppermute | solution.py:242
  32.4 9.2 %copy-start.7 = (bf16[4,128,256]{2,1,0:T(8,128)(2,1)S(1)}, bf16[4,128,256]{2,1,0:T(8,128)(2,1)}, u32[]{:S(2)}) copy-start(bf16[4,128,256]{2,1,0:T(8,128)(2,1)} %get-tuple-element.98) | copy-start | bytes 786436
  32.4 9.9 %copy-start.6 = (bf16[4,128,256]{2,1,0:T(8,128)(2,1)S(1)}, bf16[4,128,256]{2,1,0:T(8,128)(2,1)}, u32[]{:S(2)}) copy-start(bf16[4,128,256]{2,1,0:T(8,128)(2,1)} %get-tuple-element.99) | copy-start | bytes 786436
  32.4 22.4 %copy-start = (bf16[4,128,256]{2,1,0:T(8,128)(2,1)S(1)}, bf16[4,128,256]{2,1,0:T(8,128)(2,1)}, u32[]{:S(2)}) copy-start(bf16[4,128,256]{2,1,0:T(8,128)(2,1)} %get-tuple-element.74.rest_0_) | copy-start | bytes 786436
  41.6 10.6 %collective-permute-start.12 = (bf16[4,128,256]{2,1,0:T(8,128)(2,1)S(1)}, bf16[4,128,256]{2,1,0:T(8,128)(2,1)S(1)}, u32[]{:S(2)}, u32[]{:S(2)}) collective-permute-start(bf16[4,128,256]{2,1,0:T(8,128)(2,1)S(1)} %copy-done.7), channel_id=1, source_target_pairs={{0,5},{1,4},{2,7},{3,6},{4,1},{5,0},{6,3},{7,2},{8,13},{9,12},{10,... | collective-permute-start | bytes 786440 | tf_op jit(solution)/shard_map/ppermute | solution.py:242
  42.4 11.6 %collective-permute-start.13 = (bf16[4,128,256]{2,1,0:T(8,128)(2,1)S(1)}, bf16[4,128,256]{2,1,0:T(8,128)(2,1)S(1)}, u32[]{:S(2)}, u32[]{:S(2)}) collective-permute-start(bf16[4,128,256]{2,1,0:T(8,128)(2,1)S(1)} %copy-done.6), channel_id=1, source_target_pairs={{0,1},{1,0},{2,3},{3,2},{4,5},{5,4},{6,7},{7,6},{8,9},{9,8},{10,11... | collective-permute-start | bytes 786440 | tf_op jit(solution)/shard_map/ppermute | solution.py:242
  47.0 17.1 %collective-permute-start.21 = (bf16[4,128,256]{2,1,0:T(8,128)(2,1)S(1)}, bf16[4,128,256]{2,1,0:T(8,128)(2,1)S(1)}, u32[]{:S(2)}, u32[]{:S(2)}) collective-permute-start(bf16[4,128,256]{2,1,0:T(8,128)(2,1)S(1)} %get-tuple-element.109), channel_id=1, source_target_pairs={{0,6},{1,7},{2,4},{3,5},{4,2},{5,3},{6,0},{7,1},{8,14},{9,15},{10,... | collective-permute-start | bytes 786440 | tf_op jit(solution)/shard_map/ppermute | solution.py:242
  48.5 16.6 %collective-permute-start.22 = (bf16[4,128,256]{2,1,0:T(8,128)(2,1)S(1)}, bf16[4,128,256]{2,1,0:T(8,128)(2,1)S(1)}, u32[]{:S(2)}, u32[]{:S(2)}) collective-permute-start(bf16[4,128,256]{2,1,0:T(8,128)(2,1)S(1)} %get-tuple-element.110), channel_id=1, source_target_pairs={{0,7},{1,6},{2,5},{3,4},{4,3},{5,2},{6,1},{7,0},{8,15},{9,14},{10,... | collective-permute-start | bytes 786440 | tf_op jit(solution)/shard_map/ppermute | solution.py:242
  51.7 17.9 %collective-permute-start.23 = (bf16[4,128,256]{2,1,0:T(8,128)(2,1)S(1)}, bf16[4,128,256]{2,1,0:T(8,128)(2,1)S(1)}, u32[]{:S(2)}, u32[]{:S(2)}) collective-permute-start(bf16[4,128,256]{2,1,0:T(8,128)(2,1)S(1)} %get-tuple-element.111), channel_id=1, source_target_pairs={{0,2},{1,3},{2,0},{3,1},{4,6},{5,7},{6,4},{7,5},{8,10},{9,11},{10,... | collective-permute-start | bytes 786440 | tf_op jit(solution)/shard_map/ppermute | solution.py:242
  52.2 18.8 %collective-permute-start.24 = (bf16[4,128,256]{2,1,0:T(8,128)(2,1)S(1)}, bf16[4,128,256]{2,1,0:T(8,128)(2,1)S(1)}, u32[]{:S(2)}, u32[]{:S(2)}) collective-permute-start(bf16[4,128,256]{2,1,0:T(8,128)(2,1)S(1)} %get-tuple-element.112), channel_id=1, source_target_pairs={{0,4},{1,5},{2,6},{3,7},{4,0},{5,1},{6,2},{7,3},{8,12},{9,13},{10,... | collective-permute-start | bytes 786440 | tf_op jit(solution)/shard_map/ppermute | solution.py:242
  54.0 20.2 %collective-permute-start.25 = (bf16[4,128,256]{2,1,0:T(8,128)(2,1)S(1)}, bf16[4,128,256]{2,1,0:T(8,128)(2,1)S(1)}, u32[]{:S(2)}, u32[]{:S(2)}) collective-permute-start(bf16[4,128,256]{2,1,0:T(8,128)(2,1)S(1)} %get-tuple-element.113), channel_id=1, source_target_pairs={{0,3},{1,2},{2,1},{3,0},{4,7},{5,6},{6,5},{7,4},{8,11},{9,10},{10,... | collective-permute-start | bytes 786440 | tf_op jit(solution)/shard_map/ppermute | solution.py:242
  64.1 10.6 %collective-permute-start.26 = (bf16[4,128,256]{2,1,0:T(8,128)(2,1)S(1)}, bf16[4,128,256]{2,1,0:T(8,128)(2,1)S(1)}, u32[]{:S(2)}, u32[]{:S(2)}) collective-permute-start(bf16[4,128,256]{2,1,0:T(8,128)(2,1)S(1)} %get-tuple-element.114), channel_id=1, source_target_pairs={{0,5},{1,4},{2,7},{3,6},{4,1},{5,0},{6,3},{7,2},{8,13},{9,12},{10,... | collective-permute-start | bytes 786440 | tf_op jit(solution)/shard_map/ppermute | solution.py:242
  65.1 11.4 %collective-permute-start.27 = (bf16[4,128,256]{2,1,0:T(8,128)(2,1)S(1)}, bf16[4,128,256]{2,1,0:T(8,128)(2,1)S(1)}, u32[]{:S(2)}, u32[]{:S(2)}) collective-permute-start(bf16[4,128,256]{2,1,0:T(8,128)(2,1)S(1)} %get-tuple-element.115), channel_id=1, source_target_pairs={{0,1},{1,0},{2,3},{3,2},{4,5},{5,4},{6,7},{7,6},{8,9},{9,8},{10,11... | collective-permute-start | bytes 786440 | tf_op jit(solution)/shard_map/ppermute | solution.py:242
  69.6 11.0 %collective-permute-start.19 = (bf16[4,128,256]{2,1,0:T(8,128)(2,1)S(1)}, bf16[4,128,256]{2,1,0:T(8,128)(2,1)S(1)}, u32[]{:S(2)}, u32[]{:S(2)}) collective-permute-start(bf16[4,128,256]{2,1,0:T(8,128)(2,1)S(1)} %get-tuple-element.106), channel_id=1, source_target_pairs={{0,6},{1,7},{2,4},{3,5},{4,2},{5,3},{6,0},{7,1},{8,14},{9,15},{10,... | collective-permute-start | bytes 786440 | tf_op jit(solution)/shard_map/ppermute | solution.py:242
  71.0 14.5 %collective-permute-start.20 = (bf16[4,128,256]{2,1,0:T(8,128)(2,1)S(1)}, bf16[4,128,256]{2,1,0:T(8,128)(2,1)S(1)}, u32[]{:S(2)}, u32[]{:S(2)}) collective-permute-start(bf16[4,128,256]{2,1,0:T(8,128)(2,1)S(1)} %get-tuple-element.107), channel_id=1, source_target_pairs={{0,7},{1,6},{2,5},{3,4},{4,3},{5,2},{6,1},{7,0},{8,15},{9,14},{10,... | collective-permute-start | bytes 786440 | tf_op jit(solution)/shard_map/ppermute | solution.py:242
  74.2 17.9 %collective-permute-start.14 = (bf16[4,128,256]{2,1,0:T(8,128)(2,1)S(1)}, bf16[4,128,256]{2,1,0:T(8,128)(2,1)S(1)}, u32[]{:S(2)}, u32[]{:S(2)}) collective-permute-start(bf16[4,128,256]{2,1,0:T(8,128)(2,1)S(1)} %get-tuple-element.100), channel_id=1, source_target_pairs={{0,2},{1,3},{2,0},{3,1},{4,6},{5,7},{6,4},{7,5},{8,10},{9,11},{10,... | collective-permute-start | bytes 786440 | tf_op jit(solution)/shard_map/ppermute | solution.py:242
  74.8 17.3 %collective-permute-start.15 = (bf16[4,128,256]{2,1,0:T(8,128)(2,1)S(1)}, bf16[4,128,256]{2,1,0:T(8,128)(2,1)S(1)}, u32[]{:S(2)}, u32[]{:S(2)}) collective-permute-start(bf16[4,128,256]{2,1,0:T(8,128)(2,1)S(1)} %get-tuple-element.101), channel_id=1, source_target_pairs={{0,4},{1,5},{2,6},{3,7},{4,0},{5,1},{6,2},{7,3},{8,12},{9,13},{10,... | collective-permute-start | bytes 786440 | tf_op jit(solution)/shard_map/ppermute | solution.py:242
  76.5 19.3 %collective-permute-start.16 = (bf16[4,128,256]{2,1,0:T(8,128)(2,1)S(1)}, bf16[4,128,256]{2,1,0:T(8,128)(2,1)S(1)}, u32[]{:S(2)}, u32[]{:S(2)}) collective-permute-start(bf16[4,128,256]{2,1,0:T(8,128)(2,1)S(1)} %get-tuple-element.102), channel_id=1, source_target_pairs={{0,3},{1,2},{2,1},{3,0},{4,7},{5,6},{6,5},{7,4},{8,11},{9,10},{10,... | collective-permute-start | bytes 786440 | tf_op jit(solution)/shard_map/ppermute | solution.py:242
  80.5 15.9 %collective-permute-start.17 = (bf16[4,128,256]{2,1,0:T(8,128)(2,1)S(1)}, bf16[4,128,256]{2,1,0:T(8,128)(2,1)S(1)}, u32[]{:S(2)}, u32[]{:S(2)}) collective-permute-start(bf16[4,128,256]{2,1,0:T(8,128)(2,1)S(1)} %get-tuple-element.103), channel_id=1, source_target_pairs={{0,5},{1,4},{2,7},{3,6},{4,1},{5,0},{6,3},{7,2},{8,13},{9,12},{10,... | collective-permute-start | bytes 786440 | tf_op jit(solution)/shard_map/ppermute | solution.py:242
  85.5 11.0 %collective-permute-start.18 = (bf16[4,128,256]{2,1,0:T(8,128)(2,1)S(1)}, bf16[4,128,256]{2,1,0:T(8,128)(2,1)S(1)}, u32[]{:S(2)}, u32[]{:S(2)}) collective-permute-start(bf16[4,128,256]{2,1,0:T(8,128)(2,1)S(1)} %get-tuple-element.104), channel_id=1, source_target_pairs={{0,1},{1,0},{2,3},{3,2},{4,5},{5,4},{6,7},{7,6},{8,9},{9,8},{10,11... | collective-permute-start | bytes 786440 | tf_op jit(solution)/shard_map/ppermute | solution.py:242

commit v5 on v4

--- a/solution.py
+++ b/solution.py
@@ -163,21 +163,25 @@
                 at = slice(j * BLK, (j + 1) * BLK)
                 weights = jnp.exp2(scores[h, at, :] - largest[h])
                 scores[h, at, :] = weights
-                low[h, at, :] = weights.astype(BF16)
                 norm = norm + jnp.sum(weights.reshape(BLK // 8, 8, width), axis=0)
             inverse[h] = 1.0 / jnp.sum(norm, axis=0, keepdims=True)
         for h in heads:
-            out_t = (dot(vt[h], low[h]) * inverse[h]).astype(BF16).astype(F32)
+            for j in range(blocks):
+                at = slice(j * BLK, (j + 1) * BLK)
+                low[h, at, :] = (scores[h, at, :] * inverse[h]).astype(BF16)
+        for h in heads:
+            out_t = dot(vt[h], low[h]).astype(BF16).astype(F32)
             grad_t = gt[h, :, mine].astype(F32)
             delta[h] = jnp.sum(out_t * grad_t, axis=0, keepdims=True)
             os[h, mine, :] = out_t.T.astype(BF16)
-            dv[h] += dot_t(low[h], (grad_t * inverse[h]).astype(BF16))
+            dv[h] += dot(low[h], gs[h, mine, :])
         for h in heads:
             grad = gs[h, mine, :]
+            factor = inverse[h] * scale
             for j in range(blocks):
                 at = slice(j * BLK, (j + 1) * BLK)
                 grad_probs = dot_t(vs[h, at, :], grad)
-                ds[h, at, :] = (scores[h, at, :] * ((grad_probs - delta[h]) * inverse[h])).astype(BF16)
+                ds[h, at, :] = (scores[h, at, :] * ((grad_probs - delta[h]) * factor)).astype(BF16)
         for h in heads:
             dqs[h, mine, :] = dot(kt[h], ds[h]).T
             dk[h] += dot(ds[h], qr[h, mine, :])
@@ -186,7 +190,7 @@
     lax.fori_loop(0, total // width, one_step, 0, unroll=True)
     for d in range(groups):
         at = slice(d * rows, (d + 1) * rows)
-        cos, sin = cos_ref[table_rows(d), :] * scale, sin_ref[table_rows(d), :] * -scale
+        cos, sin = cos_ref[table_rows(d), :], -sin_ref[table_rows(d), :]
         for h in heads:
             cols = slice(h * DH, (h + 1) * DH)
             outs[d][0, :, cols] = os[h, at, :]

time: 98.2 us -> 98.2 us (level)
  transfers between devices with their start and end apart: 28 -> 28, of which waited for: 13 -> 13; matrix products, arithmetic and copies ran while one was open for 3% -> 3% of each run, Pallas kernels for 28% -> 27%
where the time goes in v5:
time: 98.2 us; the launch traced here: 97.8 us
  waiting for transfers between devices  39.4 us (40%)
  Pallas kernels  29.2 us (30%)
  starting transfers between devices  25.1 us (26%)
  other arithmetic  2.92 us (3%)
  between operations  1.04 us (1%)
    ppermute x28, waiting for transfers between devices, exchange(): lax.ppermute(piece, 'seq', [(i, i ^ d) for i in range(groups)])  39.4 us
    ppermute x28, starting transfers between devices, exchange(): lax.ppermute(piece, 'seq', [(i, i ^ d) for i in range(groups)])  25.1 us
    pallas_call x2, Pallas kernels, attention_call(): pl.pallas_call(functools.partial(attention_kernel, hops, rows, count, wid...  18.3 us
    pallas_call x3, Pallas kernels, pack(): pl.pallas_call(functools.partial(pack_kernel, [hops[s] for s in slots], h...  7.13 us
    pallas_call x3, Pallas kernels, unpack(): pl.pallas_call(functools.partial(unpack_kernel, [hops[s] for s in slots],...  3.75 us
    mul x1, other arithmetic, rope_tables(): return (jnp.cos(angle), jnp.sin(angle) * sign[None, :])  2.35 us
  transfers between devices with their start and end apart: 28, of which 13 were waited for; matrix products, arithmetic and copies ran while one was open for 3% of the time, Pallas kernels for 27%

profile of v5, /device:TPU:0, one launch (start us, length us, event | category | flops | bytes accessed | tf_op | source)
XLA Modules:
  0.0 97.8 jit_solution(3477251940435171674)
XLA Ops:
  0.6 1.1 %pack_0_1.1 = (bf16[4,128,256]{2,1,0:T(8,128)(2,1)S(1)}, bf16[4,128,256]{2,1,0:T(8,128)(2,1)S(1)}) custom-call(s32[1]{0:T(128)} %bitcast.me_ref, bf16[128,4096]{1,0:T(8,128)(2,1)} %q_ref.5, bf16[128,4096]{1,0:T(8,128)(2,1)} %k_ref.5, bf16[128,4096]{1,0:T(8,128)(2,1)} %v_ref.5, bf16[128,4096]{1,0:T(8,128)(2,1)} %g_ref.5), custom_call_target="tpu_custom_call" | custom-call | tf_op jit(solution)/shard_map/pack_0_1/pallas_call | solution.py:251
  1.8 4.0 %collective-permute-start.5 = (bf16[4,128,256]{2,1,0:T(8,128)(2,1)S(1)}, bf16[4,128,256]{2,1,0:T(8,128)(2,1)S(1)}, u32[]{:S(2)}, u32[]{:S(2)}) collective-permute-start(bf16[4,128,256]{2,1,0:T(8,128)(2,1)S(1)} %get-tuple-element.83), channel_id=1, source_target_pairs={{0,6},{1,7},{2,4},{3,5},{4,2},{5,3},{6,0},{7,1},{8,14},{9,15},{10,... | collective-permute-start | bytes 786440 | tf_op jit(solution)/shard_map/ppermute | solution.py:246
  5.7 2.8 %pack_0_3.1 = (bf16[4,128,256]{2,1,0:T(8,128)(2,1)}, bf16[4,128,256]{2,1,0:T(8,128)(2,1)}, bf16[4,128,256]{2,1,0:T(8,128)(2,1)}, bf16[4,128,256]{2,1,0:T(8,128)(...) custom-call(s32[1]{0:T(128)} %bitcast.me_ref, bf16[128,4096]{1,0:T(8,128)(2,1)} %q_ref.5, ...), custom_call_target="tpu_custom_call" | custom-call | tf_op jit(solution)/shard_map/pack_0_3/pallas_call | solution.py:251
  8.6 1.2 %collective-permute-start.7 = (bf16[4,128,256]{2,1,0:T(8,128)(2,1)}, bf16[4,128,256]{2,1,0:T(8,128)(2,1)S(1)}, u32[]{:S(2)}, u32[]{:S(2)}) collective-permute-start(bf16[4,128,256]{2,1,0:T(8,128)(2,1)} %get-tuple-element.85), channel_id=1, source_target_pairs={{0,2},{1,3},{2,0},{3,1},{4,6},{5,7},{6,4},{7,5},{8,10},{9,11},{10,... | collective-permute-start | bytes 786440 | tf_op jit(solution)/shard_map/ppermute | solution.py:246
  9.7 1.5 %collective-permute-start.8 = (bf16[4,128,256]{2,1,0:T(8,128)(2,1)}, bf16[4,128,256]{2,1,0:T(8,128)(2,1)S(1)}, u32[]{:S(2)}, u32[]{:S(2)}) collective-permute-start(bf16[4,128,256]{2,1,0:T(8,128)(2,1)} %get-tuple-element.86), channel_id=1, source_target_pairs={{0,4},{1,5},{2,6},{3,7},{4,0},{5,1},{6,2},{7,3},{8,12},{9,13},{10,... | collective-permute-start | bytes 786440 | tf_op jit(solution)/shard_map/ppermute | solution.py:246
  11.3 0.6 collective-permute-start.9
  11.9 0.2 broadcast_multiply_fusion.2
  12.1 0.3 broadcast_multiply_fusion.1
  12.4 0.5 collective-permute-done.5.rest_1_
  12.9 0.2 collective-permute-start.10
  13.1 5.0 %collective-permute-done.6.rest_2_ = bf16[4,128,256]{2,1,0:T(8,128)(2,1)S(1)} collective-permute-done((bf16[4,128,256]{2,1,0:T(8,128)(2,1)S(1)}, bf16[4,128,256]{2,1,0:T(8,128)(2,1)S(1)}, u32[]{:S(2)}, u32[]{:S(2)}) %collective-permute-start.6) | collective-permute-done | bytes 262176 | tf_op jit(solution)/shard_map/ppermute | solution.py:246
  18.1 0.2 collective-permute-start.11
  18.4 3.2 %pack_1_1.1 = (bf16[4,128,256]{2,1,0:T(8,128)(2,1)}, bf16[4,128,256]{2,1,0:T(8,128)(2,1)}, bf16[4,128,256]{2,1,0:T(8,128)(2,1)}, bf16[4,128,256]{2,1,0:T(8,128)(...) custom-call(s32[1]{0:T(128)} %bitcast.me_ref, ...), custom_call_target="tpu_custom_call" | custom-call | tf_op jit(solution)/shard_map/pack_1_1/pallas_call | solution.py:251
  21.6 0.0 copy-start.12
  21.6 0.0 copy-start.11
  21.6 0.0 copy-start.10
  21.6 0.0 copy-start.9
  21.6 2.4 %sine_multiply_fusion = (f32[1024,128]{1,0:T(8,128)S(1)}, f32[1024,128]{1,0:T(8,128)S(1)}) fusion(f32[128]{0:T(128)S(1)} %compare_select_fusion, f32[1024,42]{1,0:T(8,128)S(1)} %get-tuple-element.130, f32[1024,42]{1,0:T(8,128)S(1)} %get-tuple-element.129, f32[1024,44]{1,0:T(8,128)S(1)} %broadcast_multiply_fusion.2), kind=kLoop, calls=%fused_computation.1 | loop fusion | flops 393216 | bytes 1573376 | tf_op jit(solution)/shard_map/mul | solution.py:38
  24.0 0.0 copy-start.3
  24.0 0.0 copy-start.2
  24.0 0.0 copy-start.4
  24.0 0.7 collective-permute-done.7.rest_3_
  24.7 2.3 %collective-permute-start = (bf16[4,128,256]{2,1,0:T(8,128)(2,1)S(1)}, bf16[4,128,256]{2,1,0:T(8,128)(2,1)S(1)}, u32[]{:S(2)}, u32[]{:S(2)}) collective-permute-start(bf16[4,128,256]{2,1,0:T(8,128)(2,1)S(1)} %copy-done.12), channel_id=1, source_target_pairs={{0,6},{1,7},{2,4},{3,5},{4,2},{5,3},{6,0},{7,1},{8,14},{9,15},{10,... | collective-permute-start | bytes 786440 | tf_op jit(solution)/shard_map/ppermute | solution.py:246
  27.1 0.0 collective-permute-start.1
  27.1 2.2 %collective-permute-done.9.rest_5_ = bf16[4,128,256]{2,1,0:T(8,128)(2,1)S(1)} collective-permute-done((bf16[4,128,256]{2,1,0:T(8,128)(2,1)}, bf16[4,128,256]{2,1,0:T(8,128)(2,1)S(1)}, u32[]{:S(2)}, u32[]{:S(2)}) %collective-permute-start.9) | collective-permute-done | bytes 262176 | tf_op jit(solution)/shard_map/ppermute | solution.py:246
  29.3 0.5 collective-permute-start.2
  29.8 0.0 collective-permute-done.10.rest_6_
  29.8 1.7 %collective-permute-start.3 = (bf16[4,128,256]{2,1,0:T(8,128)(2,1)S(1)}, bf16[4,128,256]{2,1,0:T(8,128)(2,1)S(1)}, u32[]{:S(2)}, u32[]{:S(2)}) collective-permute-start(bf16[4,128,256]{2,1,0:T(8,128)(2,1)S(1)} %copy-done.9), channel_id=1, source_target_pairs={{0,4},{1,5},{2,6},{3,7},{4,0},{5,1},{6,2},{7,3},{8,12},{9,13},{10,... | collective-permute-start | bytes 786440 | tf_op jit(solution)/shard_map/ppermute | solution.py:246
  31.5 0.0 collective-permute-done.11.rest_7_
  31.5 0.9 collective-permute-start.4
  32.5 9.1 %attention.2 = (bf16[4,128,256]{2,1,0:T(8,128)(2,1)S(1)}, bf16[4,128,256]{2,1,0:T(8,128)(2,1)S(1)}, bf16[4,128,256]{2,1,0:T(8,128)(2,1)S(1)}, bf16[4,128,256]{2,...) custom-call(s32[1]{0:T(128)} %bitcast.me_ref, ...), custom_call_target="tpu_custom_call" | custom-call | flops 2684354560 | bytes 4194304 | tf_op jit(solution)/shard_map/attention/pallas_call | solution.py:212
  41.5 0.0 collective-permute-done.rest_1_
  41.6 0.7 collective-permute-start.12
  42.3 0.0 collective-permute-done.1.rest_2_
  42.3 0.4 collective-permute-start.13
  42.7 4.3 %collective-permute-done.2.rest_3_ = bf16[4,128,256]{2,1,0:T(8,128)(2,1)S(1)} collective-permute-done((bf16[4,128,256]{2,1,0:T(8,128)(2,1)S(1)}, bf16[4,128,256]{2,1,0:T(8,128)(2,1)S(1)}, u32[]{:S(2)}, u32[]{:S(2)}) %collective-permute-start.2) | collective-permute-done | bytes 262176 | tf_op jit(solution)/shard_map/ppermute | solution.py:246
  47.0 1.4 %collective-permute-start.21 = (bf16[4,128,256]{2,1,0:T(8,128)(2,1)S(1)}, bf16[4,128,256]{2,1,0:T(8,128)(2,1)S(1)}, u32[]{:S(2)}, u32[]{:S(2)}) collective-permute-start(bf16[4,128,256]{2,1,0:T(8,128)(2,1)S(1)} %get-tuple-element.109), channel_id=1, source_target_pairs={{0,6},{1,7},{2,4},{3,5},{4,2},{5,3},{6,0},{7,1},{8,14},{9,15},{10,... | collective-permute-start | bytes 786440 | tf_op jit(solution)/shard_map/ppermute | solution.py:246
  48.5 0.0 collective-permute-done.3.rest_4_
  48.5 3.2 %collective-permute-done.4.rest_5_ = bf16[4,128,256]{2,1,0:T(8,128)(2,1)S(1)} collective-permute-done((bf16[4,128,256]{2,1,0:T(8,128)(2,1)S(1)}, bf16[4,128,256]{2,1,0:T(8,128)(2,1)S(1)}, u32[]{:S(2)}, u32[]{:S(2)}) %collective-permute-start.4) | collective-permute-done | bytes 262176 | tf_op jit(solution)/shard_map/ppermute | solution.py:246
  51.7 0.6 collective-permute-start.23
  52.2 0.0 collective-permute-done.12.rest_6_
  52.2 1.7 %collective-permute-start.24 = (bf16[4,128,256]{2,1,0:T(8,128)(2,1)S(1)}, bf16[4,128,256]{2,1,0:T(8,128)(2,1)S(1)}, u32[]{:S(2)}, u32[]{:S(2)}) collective-permute-start(bf16[4,128,256]{2,1,0:T(8,128)(2,1)S(1)} %get-tuple-element.112), channel_id=1, source_target_pairs={{0,4},{1,5},{2,6},{3,7},{4,0},{5,1},{6,2},{7,3},{8,12},{9,13},{10,... | collective-permute-start | bytes 786440 | tf_op jit(solution)/shard_map/ppermute | solution.py:246
  54.0 0.0 collective-permute-done.13.rest_7_
  54.0 0.9 collective-permute-start.25
  54.8 9.3 %attention.3 = (bf16[4,128,256]{2,1,0:T(8,128)(2,1)S(1)}, bf16[4,128,256]{2,1,0:T(8,128)(2,1)S(1)}, bf16[4,128,256]{2,1,0:T(8,128)(2,1)S(1)}, bf16[4,128,256]{2,...) custom-call(s32[1]{0:T(128)} %bitcast.me_ref, ...), custom_call_target="tpu_custom_call" | custom-call | flops 2684354560 | bytes 4194304 | tf_op jit(solution)/shard_map/attention/pallas_call | solution.py:212
  64.1 1.0 collective-permute-start.26
  65.1 0.3 collective-permute-start.27
  65.3 4.2 %collective-permute-done.23.rest_3_ = bf16[4,128,256]{2,1,0:T(8,128)(2,1)S(1)} collective-permute-done((bf16[4,128,256]{2,1,0:T(8,128)(2,1)S(1)}, bf16[4,128,256]{2,1,0:T(8,128)(2,1)S(1)}, u32[]{:S(2)}, u32[]{:S(2)}) %collective-permute-start.23) | collective-permute-done | bytes 262176 | tf_op jit(solution)/shard_map/ppermute | solution.py:246
  69.6 1.4 %collective-permute-start.19 = (bf16[4,128,256]{2,1,0:T(8,128)(2,1)S(1)}, bf16[4,128,256]{2,1,0:T(8,128)(2,1)S(1)}, u32[]{:S(2)}, u32[]{:S(2)}) collective-permute-start(bf16[4,128,256]{2,1,0:T(8,128)(2,1)S(1)} %get-tuple-element.106), channel_id=1, source_target_pairs={{0,6},{1,7},{2,4},{3,5},{4,2},{5,3},{6,0},{7,1},{8,14},{9,15},{10,... | collective-permute-start | bytes 786440 | tf_op jit(solution)/shard_map/ppermute | solution.py:246
  71.0 0.0 collective-permute-done.24.rest_4_
  71.0 0.0 collective-permute-start.20
  71.0 3.2 %collective-permute-done.25.rest_5_ = bf16[4,128,256]{2,1,0:T(8,128)(2,1)S(1)} collective-permute-done((bf16[4,128,256]{2,1,0:T(8,128)(2,1)S(1)}, bf16[4,128,256]{2,1,0:T(8,128)(2,1)S(1)}, u32[]{:S(2)}, u32[]{:S(2)}) %collective-permute-start.25) | collective-permute-done | bytes 262176 | tf_op jit(solution)/shard_map/ppermute | solution.py:246
  74.2 0.6 collective-permute-start.14
  74.8 1.7 %collective-permute-start.15 = (bf16[4,128,256]{2,1,0:T(8,128)(2,1)S(1)}, bf16[4,128,256]{2,1,0:T(8,128)(2,1)S(1)}, u32[]{:S(2)}, u32[]{:S(2)}) collective-permute-start(bf16[4,128,256]{2,1,0:T(8,128)(2,1)S(1)} %get-tuple-element.101), channel_id=1, source_target_pairs={{0,4},{1,5},{2,6},{3,7},{4,0},{5,1},{6,2},{7,3},{8,12},{9,13},{10,... | collective-permute-start | bytes 786440 | tf_op jit(solution)/shard_map/ppermute | solution.py:246
  76.5 0.8 collective-permute-start.16
  77.3 3.2 %collective-permute-done.19.rest_1_ = bf16[4,128,256]{2,1,0:T(8,128)(2,1)S(1)} collective-permute-done((bf16[4,128,256]{2,1,0:T(8,128)(2,1)S(1)}, bf16[4,128,256]{2,1,0:T(8,128)(2,1)S(1)}, u32[]{:S(2)}, u32[]{:S(2)}) %collective-permute-start.19) | collective-permute-done | bytes 262176 | tf_op jit(solution)/shard_map/ppermute | solution.py:246
  80.5 4.9 %collective-permute-done.20.rest_2_ = bf16[4,128,256]{2,1,0:T(8,128)(2,1)S(1)} collective-permute-done((bf16[4,128,256]{2,1,0:T(8,128)(2,1)S(1)}, bf16[4,128,256]{2,1,0:T(8,128)(2,1)S(1)}, u32[]{:S(2)}, u32[]{:S(2)}) %collective-permute-start.20) | collective-permute-done | bytes 262176 | tf_op jit(solution)/shard_map/ppermute | solution.py:246
  85.5 0.4 collective-permute-start.18
  85.9 1.6 %unpack_0_0.1 = (bf16[128,4096]{1,0:T(8,128)(2,1)}, bf16[128,4096]{1,0:T(8,128)(2,1)}, bf16[128,4096]{1,0:T(8,128)(2,1)}, bf16[128,4096]{1,0:T(8,128)(2,1)}) custom-call(s32[1]{0:T(128)} %bitcast.me_ref, bf16[4,128,256]{2,1,0:T(8,128)(2,1)S(1)} %get-tuple-element.108.rest_0_, bf16[4,128,256]{2,1,0:T(8,128)(2,1)S(1)} %collective-permute-done.21.rest_1_, ...), custom_call_target="tpu_custom_call" | custom-call | tf_op jit(solution)/shard_map/unpack_0_0/pallas_call | solution.py:268
  87.5 1.0 unpack_1_0.1
  88.5 3.6 %collective-permute-done.14.rest_0_ = bf16[4,128,256]{2,1,0:T(8,128)(2,1)S(1)} collective-permute-done((bf16[4,128,256]{2,1,0:T(8,128)(2,1)S(1)}, bf16[4,128,256]{2,1,0:T(8,128)(2,1)S(1)}, u32[]{:S(2)}, u32[]{:S(2)}) %collective-permute-start.14) | collective-permute-done | bytes 262176 | tf_op jit(solution)/shard_map/ppermute | solution.py:246
  92.1 3.7 %collective-permute-done.16.rest_2_ = bf16[4,128,256]{2,1,0:T(8,128)(2,1)S(1)} collective-permute-done((bf16[4,128,256]{2,1,0:T(8,128)(2,1)S(1)}, bf16[4,128,256]{2,1,0:T(8,128)(2,1)S(1)}, u32[]{:S(2)}, u32[]{:S(2)}) %collective-permute-start.16) | collective-permute-done | bytes 262176 | tf_op jit(solution)/shard_map/ppermute | solution.py:246
  95.8 0.7 collective-permute-done.17.rest_3_
  96.4 1.2 %unpack_1_3.1 = (bf16[128,4096]{1,0:T(8,128)(2,1)}, bf16[128,4096]{1,0:T(8,128)(2,1)}, bf16[128,4096]{1,0:T(8,128)(2,1)}, bf16[128,4096]{1,0:T(8,128)(2,1)}) custom-call(s32[1]{0:T(128)} %bitcast.me_ref, bf16[4,128,256]{2,1,0:T(8,128)(2,1)S(1)} %collective-permute-done.14.rest_0_, ...), custom_call_target="tpu_custom_call", output_to_operand_aliasing={{0}: (6, {}), {1}: (7, {}), {2}: (8, {}), {3}: (9, {})} | custom-call | tf_op jit(solution)/shard_map/unpack_1_3/pallas_call | solution.py:268
  (33 shorter events, 0.1 us)
Async XLA Ops:
  1.8 11.1 %collective-permute-start.5 = (bf16[4,128,256]{2,1,0:T(8,128)(2,1)S(1)}, bf16[4,128,256]{2,1,0:T(8,128)(2,1)S(1)}, u32[]{:S(2)}, u32[]{:S(2)}) collective-permute-start(bf16[4,128,256]{2,1,0:T(8,128)(2,1)S(1)} %get-tuple-element.83), channel_id=1, source_target_pairs={{0,6},{1,7},{2,4},{3,5},{4,2},{5,3},{6,0},{7,1},{8,14},{9,15},{10,... | collective-permute-start | bytes 786440 | tf_op jit(solution)/shard_map/ppermute | solution.py:246
  5.7 6.1 %copy-start.5 = (s32[3,1024]{1,0:T(4,128)S(1)}, s32[3,1024]{1,0:T(4,128)}, u32[]{:S(2)}) copy-start(s32[3,1024]{1,0:T(4,128)} %param.13) | copy-start | bytes 36868
  5.7 12.4 %collective-permute-start.6 = (bf16[4,128,256]{2,1,0:T(8,128)(2,1)S(1)}, bf16[4,128,256]{2,1,0:T(8,128)(2,1)S(1)}, u32[]{:S(2)}, u32[]{:S(2)}) collective-permute-start(bf16[4,128,256]{2,1,0:T(8,128)(2,1)S(1)} %get-tuple-element.84), channel_id=1, source_target_pairs={{0,7},{1,6},{2,5},{3,4},{4,3},{5,2},{6,1},{7,0},{8,15},{9,14},{10,... | collective-permute-start | bytes 786440 | tf_op jit(solution)/shard_map/ppermute | solution.py:246
  8.6 16.2 %collective-permute-start.7 = (bf16[4,128,256]{2,1,0:T(8,128)(2,1)}, bf16[4,128,256]{2,1,0:T(8,128)(2,1)S(1)}, u32[]{:S(2)}, u32[]{:S(2)}) collective-permute-start(bf16[4,128,256]{2,1,0:T(8,128)(2,1)} %get-tuple-element.85), channel_id=1, source_target_pairs={{0,2},{1,3},{2,0},{3,1},{4,6},{5,7},{6,4},{7,5},{8,10},{9,11},{10,... | collective-permute-start | bytes 786440 | tf_op jit(solution)/shard_map/ppermute | solution.py:246
  9.7 17.3 %collective-permute-start.8 = (bf16[4,128,256]{2,1,0:T(8,128)(2,1)}, bf16[4,128,256]{2,1,0:T(8,128)(2,1)S(1)}, u32[]{:S(2)}, u32[]{:S(2)}) collective-permute-start(bf16[4,128,256]{2,1,0:T(8,128)(2,1)} %get-tuple-element.86), channel_id=1, source_target_pairs={{0,4},{1,5},{2,6},{3,7},{4,0},{5,1},{6,2},{7,3},{8,12},{9,13},{10,... | collective-permute-start | bytes 786440 | tf_op jit(solution)/shard_map/ppermute | solution.py:246
  11.3 18.0 %collective-permute-start.9 = (bf16[4,128,256]{2,1,0:T(8,128)(2,1)}, bf16[4,128,256]{2,1,0:T(8,128)(2,1)S(1)}, u32[]{:S(2)}, u32[]{:S(2)}) collective-permute-start(bf16[4,128,256]{2,1,0:T(8,128)(2,1)} %get-tuple-element.87), channel_id=1, source_target_pairs={{0,3},{1,2},{2,1},{3,0},{4,7},{5,6},{6,5},{7,4},{8,11},{9,10},{10,... | collective-permute-start | bytes 786440 | tf_op jit(solution)/shard_map/ppermute | solution.py:246
  12.9 16.9 %collective-permute-start.10 = (bf16[4,128,256]{2,1,0:T(8,128)(2,1)}, bf16[4,128,256]{2,1,0:T(8,128)(2,1)S(1)}, u32[]{:S(2)}, u32[]{:S(2)}) collective-permute-start(bf16[4,128,256]{2,1,0:T(8,128)(2,1)} %get-tuple-element.88), channel_id=1, source_target_pairs={{0,5},{1,4},{2,7},{3,6},{4,1},{5,0},{6,3},{7,2},{8,13},{9,12},{10,... | collective-permute-start | bytes 786440 | tf_op jit(solution)/shard_map/ppermute | solution.py:246
  18.1 13.4 %collective-permute-start.11 = (bf16[4,128,256]{2,1,0:T(8,128)(2,1)}, bf16[4,128,256]{2,1,0:T(8,128)(2,1)S(1)}, u32[]{:S(2)}, u32[]{:S(2)}) collective-permute-start(bf16[4,128,256]{2,1,0:T(8,128)(2,1)} %get-tuple-element.89), channel_id=1, source_target_pairs={{0,1},{1,0},{2,3},{3,2},{4,5},{5,4},{6,7},{7,6},{8,9},{9,8},{10,11... | collective-permute-start | bytes 786440 | tf_op jit(solution)/shard_map/ppermute | solution.py:246
  21.6 3.2 %copy-start.12 = (bf16[4,128,256]{2,1,0:T(8,128)(2,1)S(1)}, bf16[4,128,256]{2,1,0:T(8,128)(2,1)}, u32[]{:S(2)}) copy-start(bf16[4,128,256]{2,1,0:T(8,128)(2,1)} %get-tuple-element.75) | copy-start | bytes 786436
  21.6 5.5 %copy-start.11 = (bf16[4,128,256]{2,1,0:T(8,128)(2,1)S(1)}, bf16[4,128,256]{2,1,0:T(8,128)(2,1)}, u32[]{:S(2)}) copy-start(bf16[4,128,256]{2,1,0:T(8,128)(2,1)} %get-tuple-element.76) | copy-start | bytes 786436
  21.6 7.7 %copy-start.10 = (bf16[4,128,256]{2,1,0:T(8,128)(2,1)S(1)}, bf16[4,128,256]{2,1,0:T(8,128)(2,1)}, u32[]{:S(2)}) copy-start(bf16[4,128,256]{2,1,0:T(8,128)(2,1)} %get-tuple-element.77) | copy-start | bytes 786436
  21.6 8.2 %copy-start.9 = (bf16[4,128,256]{2,1,0:T(8,128)(2,1)S(1)}, bf16[4,128,256]{2,1,0:T(8,128)(2,1)}, u32[]{:S(2)}) copy-start(bf16[4,128,256]{2,1,0:T(8,128)(2,1)} %get-tuple-element.78) | copy-start | bytes 786436
  21.6 9.9 %copy-start.8 = (bf16[4,128,256]{2,1,0:T(8,128)(2,1)S(1)}, bf16[4,128,256]{2,1,0:T(8,128)(2,1)}, u32[]{:S(2)}) copy-start(bf16[4,128,256]{2,1,0:T(8,128)(2,1)} %get-tuple-element.79) | copy-start | bytes 786436
  21.6 10.8 %copy-start.1 = (bf16[4,128,256]{2,1,0:T(8,128)(2,1)S(1)}, bf16[4,128,256]{2,1,0:T(8,128)(2,1)}, u32[]{:S(2)}) copy-start(bf16[4,128,256]{2,1,0:T(8,128)(2,1)} %get-tuple-element.82.rest_0_) | copy-start | bytes 786436
  24.0 8.4 %copy-start.3 = (s32[8,8]{1,0:T(8,128)S(1)}, s32[8,8]{1,0:T(8,128)}, u32[]{:S(2)}) copy-start(s32[8,8]{1,0:T(8,128)} %bands_ref.3) | copy-start | bytes 772
  24.0 8.4 %copy-start.2 = (s32[8,8]{1,0:T(8,128)S(1)}, s32[8,8]{1,0:T(8,128)}, u32[]{:S(2)}) copy-start(s32[8,8]{1,0:T(8,128)} %flags_ref.3) | copy-start | bytes 772
  24.0 8.4 %copy-start.4 = (s32[8]{0:T(128)S(1)}, s32[8]{0:T(128)}, u32[]{:S(2)}) copy-start(s32[8]{0:T(128)} %constant.57.clone.hops_ref) | copy-start | bytes 100
  24.7 16.8 %collective-permute-start = (bf16[4,128,256]{2,1,0:T(8,128)(2,1)S(1)}, bf16[4,128,256]{2,1,0:T(8,128)(2,1)S(1)}, u32[]{:S(2)}, u32[]{:S(2)}) collective-permute-start(bf16[4,128,256]{2,1,0:T(8,128)(2,1)S(1)} %copy-done.12), channel_id=1, source_target_pairs={{0,6},{1,7},{2,4},{3,5},{4,2},{5,3},{6,0},{7,1},{8,14},{9,15},{10,... | collective-permute-start | bytes 786440 | tf_op jit(solution)/shard_map/ppermute | solution.py:246
  27.1 15.2 %collective-permute-start.1 = (bf16[4,128,256]{2,1,0:T(8,128)(2,1)S(1)}, bf16[4,128,256]{2,1,0:T(8,128)(2,1)S(1)}, u32[]{:S(2)}, u32[]{:S(2)}) collective-permute-start(bf16[4,128,256]{2,1,0:T(8,128)(2,1)S(1)} %copy-done.11), channel_id=1, source_target_pairs={{0,7},{1,6},{2,5},{3,4},{4,3},{5,2},{6,1},{7,0},{8,15},{9,14},{10,... | collective-permute-start | bytes 786440 | tf_op jit(solution)/shard_map/ppermute | solution.py:246
  29.3 17.8 %collective-permute-start.2 = (bf16[4,128,256]{2,1,0:T(8,128)(2,1)S(1)}, bf16[4,128,256]{2,1,0:T(8,128)(2,1)S(1)}, u32[]{:S(2)}, u32[]{:S(2)}) collective-permute-start(bf16[4,128,256]{2,1,0:T(8,128)(2,1)S(1)} %copy-done.10), channel_id=1, source_target_pairs={{0,2},{1,3},{2,0},{3,1},{4,6},{5,7},{6,4},{7,5},{8,10},{9,11},{10,... | collective-permute-start | bytes 786440 | tf_op jit(solution)/shard_map/ppermute | solution.py:246
  29.8 18.7 %collective-permute-start.3 = (bf16[4,128,256]{2,1,0:T(8,128)(2,1)S(1)}, bf16[4,128,256]{2,1,0:T(8,128)(2,1)S(1)}, u32[]{:S(2)}, u32[]{:S(2)}) collective-permute-start(bf16[4,128,256]{2,1,0:T(8,128)(2,1)S(1)} %copy-done.9), channel_id=1, source_target_pairs={{0,4},{1,5},{2,6},{3,7},{4,0},{5,1},{6,2},{7,3},{8,12},{9,13},{10,... | collective-permute-start | bytes 786440 | tf_op jit(solution)/shard_map/ppermute | solution.py:246
  31.5 20.2 %collective-permute-start.4 = (bf16[4,128,256]{2,1,0:T(8,128)(2,1)S(1)}, bf16[4,128,256]{2,1,0:T(8,128)(2,1)S(1)}, u32[]{:S(2)}, u32[]{:S(2)}) collective-permute-start(bf16[4,128,256]{2,1,0:T(8,128)(2,1)S(1)} %copy-done.8), channel_id=1, source_target_pairs={{0,3},{1,2},{2,1},{3,0},{4,7},{5,6},{6,5},{7,4},{8,11},{9,10},{10,... | collective-permute-start | bytes 786440 | tf_op jit(solution)/shard_map/ppermute | solution.py:246
  32.4 9.1 %copy-start.7 = (bf16[4,128,256]{2,1,0:T(8,128)(2,1)S(1)}, bf16[4,128,256]{2,1,0:T(8,128)(2,1)}, u32[]{:S(2)}) copy-start(bf16[4,128,256]{2,1,0:T(8,128)(2,1)} %get-tuple-element.98) | copy-start | bytes 786436
  32.4 9.9 %copy-start.6 = (bf16[4,128,256]{2,1,0:T(8,128)(2,1)S(1)}, bf16[4,128,256]{2,1,0:T(8,128)(2,1)}, u32[]{:S(2)}) copy-start(bf16[4,128,256]{2,1,0:T(8,128)(2,1)} %get-tuple-element.99) | copy-start | bytes 786436
  32.4 22.4 %copy-start = (bf16[4,128,256]{2,1,0:T(8,128)(2,1)S(1)}, bf16[4,128,256]{2,1,0:T(8,128)(2,1)}, u32[]{:S(2)}) copy-start(bf16[4,128,256]{2,1,0:T(8,128)(2,1)} %get-tuple-element.74.rest_0_) | copy-start | bytes 786436
  41.6 10.7 %collective-permute-start.12 = (bf16[4,128,256]{2,1,0:T(8,128)(2,1)S(1)}, bf16[4,128,256]{2,1,0:T(8,128)(2,1)S(1)}, u32[]{:S(2)}, u32[]{:S(2)}) collective-permute-start(bf16[4,128,256]{2,1,0:T(8,128)(2,1)S(1)} %copy-done.7), channel_id=1, source_target_pairs={{0,5},{1,4},{2,7},{3,6},{4,1},{5,0},{6,3},{7,2},{8,13},{9,12},{10,... | collective-permute-start | bytes 786440 | tf_op jit(solution)/shard_map/ppermute | solution.py:246
  42.3 11.7 %collective-permute-start.13 = (bf16[4,128,256]{2,1,0:T(8,128)(2,1)S(1)}, bf16[4,128,256]{2,1,0:T(8,128)(2,1)S(1)}, u32[]{:S(2)}, u32[]{:S(2)}) collective-permute-start(bf16[4,128,256]{2,1,0:T(8,128)(2,1)S(1)} %copy-done.6), channel_id=1, source_target_pairs={{0,1},{1,0},{2,3},{3,2},{4,5},{5,4},{6,7},{7,6},{8,9},{9,8},{10,11... | collective-permute-start | bytes 786440 | tf_op jit(solution)/shard_map/ppermute | solution.py:246
  47.0 17.0 %collective-permute-start.21 = (bf16[4,128,256]{2,1,0:T(8,128)(2,1)S(1)}, bf16[4,128,256]{2,1,0:T(8,128)(2,1)S(1)}, u32[]{:S(2)}, u32[]{:S(2)}) collective-permute-start(bf16[4,128,256]{2,1,0:T(8,128)(2,1)S(1)} %get-tuple-element.109), channel_id=1, source_target_pairs={{0,6},{1,7},{2,4},{3,5},{4,2},{5,3},{6,0},{7,1},{8,14},{9,15},{10,... | collective-permute-start | bytes 786440 | tf_op jit(solution)/shard_map/ppermute | solution.py:246
  48.5 16.6 %collective-permute-start.22 = (bf16[4,128,256]{2,1,0:T(8,128)(2,1)S(1)}, bf16[4,128,256]{2,1,0:T(8,128)(2,1)S(1)}, u32[]{:S(2)}, u32[]{:S(2)}) collective-permute-start(bf16[4,128,256]{2,1,0:T(8,128)(2,1)S(1)} %get-tuple-element.110), channel_id=1, source_target_pairs={{0,7},{1,6},{2,5},{3,4},{4,3},{5,2},{6,1},{7,0},{8,15},{9,14},{10,... | collective-permute-start | bytes 786440 | tf_op jit(solution)/shard_map/ppermute | solution.py:246
  51.7 17.9 %collective-permute-start.23 = (bf16[4,128,256]{2,1,0:T(8,128)(2,1)S(1)}, bf16[4,128,256]{2,1,0:T(8,128)(2,1)S(1)}, u32[]{:S(2)}, u32[]{:S(2)}) collective-permute-start(bf16[4,128,256]{2,1,0:T(8,128)(2,1)S(1)} %get-tuple-element.111), channel_id=1, source_target_pairs={{0,2},{1,3},{2,0},{3,1},{4,6},{5,7},{6,4},{7,5},{8,10},{9,11},{10,... | collective-permute-start | bytes 786440 | tf_op jit(solution)/shard_map/ppermute | solution.py:246
  52.2 18.8 %collective-permute-start.24 = (bf16[4,128,256]{2,1,0:T(8,128)(2,1)S(1)}, bf16[4,128,256]{2,1,0:T(8,128)(2,1)S(1)}, u32[]{:S(2)}, u32[]{:S(2)}) collective-permute-start(bf16[4,128,256]{2,1,0:T(8,128)(2,1)S(1)} %get-tuple-element.112), channel_id=1, source_target_pairs={{0,4},{1,5},{2,6},{3,7},{4,0},{5,1},{6,2},{7,3},{8,12},{9,13},{10,... | collective-permute-start | bytes 786440 | tf_op jit(solution)/shard_map/ppermute | solution.py:246
  54.0 20.2 %collective-permute-start.25 = (bf16[4,128,256]{2,1,0:T(8,128)(2,1)S(1)}, bf16[4,128,256]{2,1,0:T(8,128)(2,1)S(1)}, u32[]{:S(2)}, u32[]{:S(2)}) collective-permute-start(bf16[4,128,256]{2,1,0:T(8,128)(2,1)S(1)} %get-tuple-element.113), channel_id=1, source_target_pairs={{0,3},{1,2},{2,1},{3,0},{4,7},{5,6},{6,5},{7,4},{8,11},{9,10},{10,... | collective-permute-start | bytes 786440 | tf_op jit(solution)/shard_map/ppermute | solution.py:246
  64.1 10.7 %collective-permute-start.26 = (bf16[4,128,256]{2,1,0:T(8,128)(2,1)S(1)}, bf16[4,128,256]{2,1,0:T(8,128)(2,1)S(1)}, u32[]{:S(2)}, u32[]{:S(2)}) collective-permute-start(bf16[4,128,256]{2,1,0:T(8,128)(2,1)S(1)} %get-tuple-element.114), channel_id=1, source_target_pairs={{0,5},{1,4},{2,7},{3,6},{4,1},{5,0},{6,3},{7,2},{8,13},{9,12},{10,... | collective-permute-start | bytes 786440 | tf_op jit(solution)/shard_map/ppermute | solution.py:246
  65.1 11.4 %collective-permute-start.27 = (bf16[4,128,256]{2,1,0:T(8,128)(2,1)S(1)}, bf16[4,128,256]{2,1,0:T(8,128)(2,1)S(1)}, u32[]{:S(2)}, u32[]{:S(2)}) collective-permute-start(bf16[4,128,256]{2,1,0:T(8,128)(2,1)S(1)} %get-tuple-element.115), channel_id=1, source_target_pairs={{0,1},{1,0},{2,3},{3,2},{4,5},{5,4},{6,7},{7,6},{8,9},{9,8},{10,11... | collective-permute-start | bytes 786440 | tf_op jit(solution)/shard_map/ppermute | solution.py:246
  69.6 11.0 %collective-permute-start.19 = (bf16[4,128,256]{2,1,0:T(8,128)(2,1)S(1)}, bf16[4,128,256]{2,1,0:T(8,128)(2,1)S(1)}, u32[]{:S(2)}, u32[]{:S(2)}) collective-permute-start(bf16[4,128,256]{2,1,0:T(8,128)(2,1)S(1)} %get-tuple-element.106), channel_id=1, source_target_pairs={{0,6},{1,7},{2,4},{3,5},{4,2},{5,3},{6,0},{7,1},{8,14},{9,15},{10,... | collective-permute-start | bytes 786440 | tf_op jit(solution)/shard_map/ppermute | solution.py:246
  71.0 14.5 %collective-permute-start.20 = (bf16[4,128,256]{2,1,0:T(8,128)(2,1)S(1)}, bf16[4,128,256]{2,1,0:T(8,128)(2,1)S(1)}, u32[]{:S(2)}, u32[]{:S(2)}) collective-permute-start(bf16[4,128,256]{2,1,0:T(8,128)(2,1)S(1)} %get-tuple-element.107), channel_id=1, source_target_pairs={{0,7},{1,6},{2,5},{3,4},{4,3},{5,2},{6,1},{7,0},{8,15},{9,14},{10,... | collective-permute-start | bytes 786440 | tf_op jit(solution)/shard_map/ppermute | solution.py:246
  74.2 17.9 %collective-permute-start.14 = (bf16[4,128,256]{2,1,0:T(8,128)(2,1)S(1)}, bf16[4,128,256]{2,1,0:T(8,128)(2,1)S(1)}, u32[]{:S(2)}, u32[]{:S(2)}) collective-permute-start(bf16[4,128,256]{2,1,0:T(8,128)(2,1)S(1)} %get-tuple-element.100), channel_id=1, source_target_pairs={{0,2},{1,3},{2,0},{3,1},{4,6},{5,7},{6,4},{7,5},{8,10},{9,11},{10,... | collective-permute-start | bytes 786440 | tf_op jit(solution)/shard_map/ppermute | solution.py:246
  74.8 17.3 %collective-permute-start.15 = (bf16[4,128,256]{2,1,0:T(8,128)(2,1)S(1)}, bf16[4,128,256]{2,1,0:T(8,128)(2,1)S(1)}, u32[]{:S(2)}, u32[]{:S(2)}) collective-permute-start(bf16[4,128,256]{2,1,0:T(8,128)(2,1)S(1)} %get-tuple-element.101), channel_id=1, source_target_pairs={{0,4},{1,5},{2,6},{3,7},{4,0},{5,1},{6,2},{7,3},{8,12},{9,13},{10,... | collective-permute-start | bytes 786440 | tf_op jit(solution)/shard_map/ppermute | solution.py:246
  76.5 19.3 %collective-permute-start.16 = (bf16[4,128,256]{2,1,0:T(8,128)(2,1)S(1)}, bf16[4,128,256]{2,1,0:T(8,128)(2,1)S(1)}, u32[]{:S(2)}, u32[]{:S(2)}) collective-permute-start(bf16[4,128,256]{2,1,0:T(8,128)(2,1)S(1)} %get-tuple-element.102), channel_id=1, source_target_pairs={{0,3},{1,2},{2,1},{3,0},{4,7},{5,6},{6,5},{7,4},{8,11},{9,10},{10,... | collective-permute-start | bytes 786440 | tf_op jit(solution)/shard_map/ppermute | solution.py:246
  80.5 15.9 %collective-permute-start.17 = (bf16[4,128,256]{2,1,0:T(8,128)(2,1)S(1)}, bf16[4,128,256]{2,1,0:T(8,128)(2,1)S(1)}, u32[]{:S(2)}, u32[]{:S(2)}) collective-permute-start(bf16[4,128,256]{2,1,0:T(8,128)(2,1)S(1)} %get-tuple-element.103), channel_id=1, source_target_pairs={{0,5},{1,4},{2,7},{3,6},{4,1},{5,0},{6,3},{7,2},{8,13},{9,12},{10,... | collective-permute-start | bytes 786440 | tf_op jit(solution)/shard_map/ppermute | solution.py:246
  85.5 11.0 %collective-permute-start.18 = (bf16[4,128,256]{2,1,0:T(8,128)(2,1)S(1)}, bf16[4,128,256]{2,1,0:T(8,128)(2,1)S(1)}, u32[]{:S(2)}, u32[]{:S(2)}) collective-permute-start(bf16[4,128,256]{2,1,0:T(8,128)(2,1)S(1)} %get-tuple-element.104), channel_id=1, source_target_pairs={{0,1},{1,0},{2,3},{3,2},{4,5},{5,4},{6,7},{7,6},{8,9},{9,8},{10,11... | collective-permute-start | bytes 786440 | tf_op jit(solution)/shard_map/ppermute | solution.py:246

commit v6 on v5

--- a/solution.py
+++ b/solution.py
@@ -13,7 +13,7 @@
 BLK = 128
 NTK = 2.0
 CHUNKS = 2
-AHEAD = 5
+AHEAD = 6
 SMALL = 8 * 1024 * 1024
 EARLY = 2
 LAST = (3,)

time: 98.2 us -> 98.1 us (level)
  transfers between devices with their start and end apart: 28 -> 28, of which waited for: 13 -> 12; matrix products, arithmetic and copies ran while one was open for 3% -> 3% of each run, Pallas kernels for 27% -> 28%
where the time goes in v6:
time: 98.1 us; the launch traced here: 97.8 us
  waiting for transfers between devices  38.7 us (39%)
  Pallas kernels  29.4 us (30%)
  starting transfers between devices  25.8 us (26%)
  other arithmetic  2.92 us (3%)
  between operations  1.03 us (1%)
    ppermute x28, waiting for transfers between devices, exchange(): lax.ppermute(piece, 'seq', [(i, i ^ d) for i in range(groups)])  38.7 us
    ppermute x28, starting transfers between devices, exchange(): lax.ppermute(piece, 'seq', [(i, i ^ d) for i in range(groups)])  25.8 us
    pallas_call x2, Pallas kernels, attention_call(): pl.pallas_call(functools.partial(attention_kernel, hops, rows, count, wid...  18.4 us
    pallas_call x3, Pallas kernels, pack(): pl.pallas_call(functools.partial(pack_kernel, [hops[s] for s in slots], h...  7.2 us
    pallas_call x3, Pallas kernels, unpack(): pl.pallas_call(functools.partial(unpack_kernel, [hops[s] for s in slots],...  3.75 us
    mul x1, other arithmetic, rope_tables(): return (jnp.cos(angle), jnp.sin(angle) * sign[None, :])  2.35 us
  transfers between devices with their start and end apart: 28, of which 12 were waited for; matrix products, arithmetic and copies ran while one was open for 3% of the time, Pallas kernels for 28%

profile of v6, /device:TPU:0, one launch (start us, length us, event | category | flops | bytes accessed | tf_op | source)
XLA Modules:
  0.0 97.8 jit_solution(988164644099629181)
XLA Ops:
  0.6 1.1 %pack_0_1.1 = (bf16[4,128,256]{2,1,0:T(8,128)(2,1)S(1)}, bf16[4,128,256]{2,1,0:T(8,128)(2,1)S(1)}) custom-call(s32[1]{0:T(128)} %bitcast.me_ref, bf16[128,4096]{1,0:T(8,128)(2,1)} %q_ref.5, bf16[128,4096]{1,0:T(8,128)(2,1)} %k_ref.5, bf16[128,4096]{1,0:T(8,128)(2,1)} %v_ref.5, bf16[128,4096]{1,0:T(8,128)(2,1)} %g_ref.5), custom_call_target="tpu_custom_call" | custom-call | tf_op jit(solution)/shard_map/pack_0_1/pallas_call | solution.py:251
  1.8 4.0 %collective-permute-start.6 = (bf16[4,128,256]{2,1,0:T(8,128)(2,1)S(1)}, bf16[4,128,256]{2,1,0:T(8,128)(2,1)S(1)}, u32[]{:S(2)}, u32[]{:S(2)}) collective-permute-start(bf16[4,128,256]{2,1,0:T(8,128)(2,1)S(1)} %get-tuple-element.82), channel_id=1, source_target_pairs={{0,6},{1,7},{2,4},{3,5},{4,2},{5,3},{6,0},{7,1},{8,14},{9,15},{10,... | collective-permute-start | bytes 786440 | tf_op jit(solution)/shard_map/ppermute | solution.py:246
  5.7 0.0 collective-permute-start.7
  5.7 2.8 %pack_0_3.1 = (bf16[4,128,256]{2,1,0:T(8,128)(2,1)}, bf16[4,128,256]{2,1,0:T(8,128)(2,1)}, bf16[4,128,256]{2,1,0:T(8,128)(2,1)}, bf16[4,128,256]{2,1,0:T(8,128)(...) custom-call(s32[1]{0:T(128)} %bitcast.me_ref, bf16[128,4096]{1,0:T(8,128)(2,1)} %q_ref.5, ...), custom_call_target="tpu_custom_call" | custom-call | tf_op jit(solution)/shard_map/pack_0_3/pallas_call | solution.py:251
  8.5 1.2 %collective-permute-start.8 = (bf16[4,128,256]{2,1,0:T(8,128)(2,1)}, bf16[4,128,256]{2,1,0:T(8,128)(2,1)S(1)}, u32[]{:S(2)}, u32[]{:S(2)}) collective-permute-start(bf16[4,128,256]{2,1,0:T(8,128)(2,1)} %get-tuple-element.84), channel_id=1, source_target_pairs={{0,2},{1,3},{2,0},{3,1},{4,6},{5,7},{6,4},{7,5},{8,10},{9,11},{10,... | collective-permute-start | bytes 786440 | tf_op jit(solution)/shard_map/ppermute | solution.py:246
  9.7 1.5 %collective-permute-start.9 = (bf16[4,128,256]{2,1,0:T(8,128)(2,1)}, bf16[4,128,256]{2,1,0:T(8,128)(2,1)S(1)}, u32[]{:S(2)}, u32[]{:S(2)}) collective-permute-start(bf16[4,128,256]{2,1,0:T(8,128)(2,1)} %get-tuple-element.85), channel_id=1, source_target_pairs={{0,4},{1,5},{2,6},{3,7},{4,0},{5,1},{6,2},{7,3},{8,12},{9,13},{10,... | collective-permute-start | bytes 786440 | tf_op jit(solution)/shard_map/ppermute | solution.py:246
  11.2 0.6 collective-permute-start.10
  11.9 0.2 broadcast_multiply_fusion.2
  12.1 0.3 broadcast_multiply_fusion.1
  12.4 2.4 %sine_multiply_fusion = (f32[1024,128]{1,0:T(8,128)S(1)}, f32[1024,128]{1,0:T(8,128)S(1)}) fusion(f32[128]{0:T(128)S(1)} %compare_select_fusion, f32[1024,42]{1,0:T(8,128)S(1)} %get-tuple-element.128, f32[1024,42]{1,0:T(8,128)S(1)} %get-tuple-element.127, f32[1024,44]{1,0:T(8,128)S(1)} %broadcast_multiply_fusion.2), kind=kLoop, calls=%fused_computation.1 | loop fusion | flops 393216 | bytes 1573376 | tf_op jit(solution)/shard_map/mul | solution.py:38
  14.8 3.3 %pack_1_1.1 = (bf16[4,128,256]{2,1,0:T(8,128)(2,1)}, bf16[4,128,256]{2,1,0:T(8,128)(2,1)}, bf16[4,128,256]{2,1,0:T(8,128)(2,1)}, bf16[4,128,256]{2,1,0:T(8,128)(...) custom-call(s32[1]{0:T(128)} %bitcast.me_ref, ...), custom_call_target="tpu_custom_call" | custom-call | tf_op jit(solution)/shard_map/pack_1_1/pallas_call | solution.py:251
  18.1 0.0 copy-start.3
  18.1 0.0 copy-start.2
  18.1 0.0 collective-permute-done.6.rest_1_
  18.1 0.6 collective-permute-start.11
  18.7 0.0 collective-permute-done.7.rest_2_
  18.8 0.1 collective-permute-start.12
  18.8 5.9 %collective-permute-done.8.rest_3_ = bf16[4,128,256]{2,1,0:T(8,128)(2,1)S(1)} collective-permute-done((bf16[4,128,256]{2,1,0:T(8,128)(2,1)}, bf16[4,128,256]{2,1,0:T(8,128)(2,1)S(1)}, u32[]{:S(2)}, u32[]{:S(2)}) %collective-permute-start.8) | collective-permute-done | bytes 262176 | tf_op jit(solution)/shard_map/ppermute | solution.py:246
  24.7 1.4 %collective-permute-start = (bf16[4,128,256]{2,1,0:T(8,128)(2,1)}, bf16[4,128,256]{2,1,0:T(8,128)(2,1)S(1)}, u32[]{:S(2)}, u32[]{:S(2)}) collective-permute-start(bf16[4,128,256]{2,1,0:T(8,128)(2,1)} %get-tuple-element.74), channel_id=1, source_target_pairs={{0,6},{1,7},{2,4},{3,5},{4,2},{5,3},{6,0},{7,1},{8,14},{9,15},{10,... | collective-permute-start | bytes 786440 | tf_op jit(solution)/shard_map/ppermute | solution.py:246
  26.2 0.0 collective-permute-done.9.rest_4_
  26.2 0.0 collective-permute-start.1
  26.2 3.3 %collective-permute-done.10.rest_5_ = bf16[4,128,256]{2,1,0:T(8,128)(2,1)S(1)} collective-permute-done((bf16[4,128,256]{2,1,0:T(8,128)(2,1)}, bf16[4,128,256]{2,1,0:T(8,128)(2,1)S(1)}, u32[]{:S(2)}, u32[]{:S(2)}) %collective-permute-start.10) | collective-permute-done | bytes 262176 | tf_op jit(solution)/shard_map/ppermute | solution.py:246
  29.5 0.5 collective-permute-start.2
  30.0 0.0 collective-permute-done.11.rest_6_
  30.0 1.7 %collective-permute-start.3 = (bf16[4,128,256]{2,1,0:T(8,128)(2,1)}, bf16[4,128,256]{2,1,0:T(8,128)(2,1)S(1)}, u32[]{:S(2)}, u32[]{:S(2)}) collective-permute-start(bf16[4,128,256]{2,1,0:T(8,128)(2,1)} %get-tuple-element.77), channel_id=1, source_target_pairs={{0,4},{1,5},{2,6},{3,7},{4,0},{5,1},{6,2},{7,3},{8,12},{9,13},{10,... | collective-permute-start | bytes 786440 | tf_op jit(solution)/shard_map/ppermute | solution.py:246
  31.7 0.0 collective-permute-done.12.rest_7_
  31.7 0.9 collective-permute-start.4
  32.6 2.9 %collective-permute-done.rest_1_ = bf16[4,128,256]{2,1,0:T(8,128)(2,1)S(1)} collective-permute-done((bf16[4,128,256]{2,1,0:T(8,128)(2,1)}, bf16[4,128,256]{2,1,0:T(8,128)(2,1)S(1)}, u32[]{:S(2)}, u32[]{:S(2)}) %collective-permute-start) | collective-permute-done | bytes 262176 | tf_op jit(solution)/shard_map/ppermute | solution.py:246
  35.5 0.0 collective-permute-start.5
  35.5 9.1 %attention.2 = (bf16[4,128,256]{2,1,0:T(8,128)(2,1)S(1)}, bf16[4,128,256]{2,1,0:T(8,128)(2,1)S(1)}, bf16[4,128,256]{2,1,0:T(8,128)(2,1)S(1)}, bf16[4,128,256]{2,...) custom-call(s32[1]{0:T(128)} %bitcast.me_ref, ...), custom_call_target="tpu_custom_call" | custom-call | flops 2684354560 | bytes 4194304 | tf_op jit(solution)/shard_map/attention/pallas_call | solution.py:212
  44.7 2.2 %collective-permute-start.13 = (bf16[4,128,256]{2,1,0:T(8,128)(2,1)S(1)}, bf16[4,128,256]{2,1,0:T(8,128)(2,1)S(1)}, u32[]{:S(2)}, u32[]{:S(2)}) collective-permute-start(bf16[4,128,256]{2,1,0:T(8,128)(2,1)S(1)} %copy-done.6), channel_id=1, source_target_pairs={{0,1},{1,0},{2,3},{3,2},{4,5},{5,4},{6,7},{7,6},{8,9},{9,8},{10,11... | collective-permute-start | bytes 786440 | tf_op jit(solution)/shard_map/ppermute | solution.py:246
  46.9 0.4 collective-permute-done.2.rest_3_
  47.2 1.4 %collective-permute-start.21 = (bf16[4,128,256]{2,1,0:T(8,128)(2,1)S(1)}, bf16[4,128,256]{2,1,0:T(8,128)(2,1)S(1)}, u32[]{:S(2)}, u32[]{:S(2)}) collective-permute-start(bf16[4,128,256]{2,1,0:T(8,128)(2,1)S(1)} %get-tuple-element.107), channel_id=1, source_target_pairs={{0,6},{1,7},{2,4},{3,5},{4,2},{5,3},{6,0},{7,1},{8,14},{9,15},{10,... | collective-permute-start | bytes 786440 | tf_op jit(solution)/shard_map/ppermute | solution.py:246
  48.7 0.0 collective-permute-done.3.rest_4_
  48.7 0.5 collective-permute-start.22
  49.2 2.8 %collective-permute-done.4.rest_5_ = bf16[4,128,256]{2,1,0:T(8,128)(2,1)S(1)} collective-permute-done((bf16[4,128,256]{2,1,0:T(8,128)(2,1)}, bf16[4,128,256]{2,1,0:T(8,128)(2,1)S(1)}, u32[]{:S(2)}, u32[]{:S(2)}) %collective-permute-start.4) | collective-permute-done | bytes 262176 | tf_op jit(solution)/shard_map/ppermute | solution.py:246
  52.0 0.5 collective-permute-start.23
  52.5 0.0 collective-permute-done.5.rest_6_
  52.5 1.6 %collective-permute-start.24 = (bf16[4,128,256]{2,1,0:T(8,128)(2,1)S(1)}, bf16[4,128,256]{2,1,0:T(8,128)(2,1)S(1)}, u32[]{:S(2)}, u32[]{:S(2)}) collective-permute-start(bf16[4,128,256]{2,1,0:T(8,128)(2,1)S(1)} %get-tuple-element.110), channel_id=1, source_target_pairs={{0,4},{1,5},{2,6},{3,7},{4,0},{5,1},{6,2},{7,3},{8,12},{9,13},{10,... | collective-permute-start | bytes 786440 | tf_op jit(solution)/shard_map/ppermute | solution.py:246
  54.1 0.0 collective-permute-done.13.rest_7_
  54.1 0.9 collective-permute-start.25
  55.0 9.3 %attention.3 = (bf16[4,128,256]{2,1,0:T(8,128)(2,1)S(1)}, bf16[4,128,256]{2,1,0:T(8,128)(2,1)S(1)}, bf16[4,128,256]{2,1,0:T(8,128)(2,1)S(1)}, bf16[4,128,256]{2,...) custom-call(s32[1]{0:T(128)} %bitcast.me_ref, ...), custom_call_target="tpu_custom_call" | custom-call | flops 2684354560 | bytes 4194304 | tf_op jit(solution)/shard_map/attention/pallas_call | solution.py:212
  64.3 0.0 collective-permute-done.21.rest_1_
  64.3 1.0 collective-permute-start.26
  65.3 0.0 collective-permute-done.22.rest_2_
  65.3 0.3 collective-permute-start.27
  65.6 4.2 %collective-permute-done.23.rest_3_ = bf16[4,128,256]{2,1,0:T(8,128)(2,1)S(1)} collective-permute-done((bf16[4,128,256]{2,1,0:T(8,128)(2,1)S(1)}, bf16[4,128,256]{2,1,0:T(8,128)(2,1)S(1)}, u32[]{:S(2)}, u32[]{:S(2)}) %collective-permute-start.23) | collective-permute-done | bytes 262176 | tf_op jit(solution)/shard_map/ppermute | solution.py:246
  69.8 1.4 %collective-permute-start.19 = (bf16[4,128,256]{2,1,0:T(8,128)(2,1)S(1)}, bf16[4,128,256]{2,1,0:T(8,128)(2,1)S(1)}, u32[]{:S(2)}, u32[]{:S(2)}) collective-permute-start(bf16[4,128,256]{2,1,0:T(8,128)(2,1)S(1)} %get-tuple-element.104), channel_id=1, source_target_pairs={{0,6},{1,7},{2,4},{3,5},{4,2},{5,3},{6,0},{7,1},{8,14},{9,15},{10,... | collective-permute-start | bytes 786440 | tf_op jit(solution)/shard_map/ppermute | solution.py:246
  71.2 3.2 %collective-permute-done.25.rest_5_ = bf16[4,128,256]{2,1,0:T(8,128)(2,1)S(1)} collective-permute-done((bf16[4,128,256]{2,1,0:T(8,128)(2,1)S(1)}, bf16[4,128,256]{2,1,0:T(8,128)(2,1)S(1)}, u32[]{:S(2)}, u32[]{:S(2)}) %collective-permute-start.25) | collective-permute-done | bytes 262176 | tf_op jit(solution)/shard_map/ppermute | solution.py:246
  74.4 0.5 collective-permute-start.14
  74.9 0.0 collective-permute-done.26.rest_6_
  74.9 1.8 %collective-permute-start.15 = (bf16[4,128,256]{2,1,0:T(8,128)(2,1)S(1)}, bf16[4,128,256]{2,1,0:T(8,128)(2,1)S(1)}, u32[]{:S(2)}, u32[]{:S(2)}) collective-permute-start(bf16[4,128,256]{2,1,0:T(8,128)(2,1)S(1)} %get-tuple-element.99), channel_id=1, source_target_pairs={{0,4},{1,5},{2,6},{3,7},{4,0},{5,1},{6,2},{7,3},{8,12},{9,13},{10,... | collective-permute-start | bytes 786440 | tf_op jit(solution)/shard_map/ppermute | solution.py:246
  76.7 0.0 collective-permute-done.27.rest_7_
  76.7 0.8 collective-permute-start.16
  77.5 3.0 %collective-permute-done.19.rest_1_ = bf16[4,128,256]{2,1,0:T(8,128)(2,1)S(1)} collective-permute-done((bf16[4,128,256]{2,1,0:T(8,128)(2,1)S(1)}, bf16[4,128,256]{2,1,0:T(8,128)(2,1)S(1)}, u32[]{:S(2)}, u32[]{:S(2)}) %collective-permute-start.19) | collective-permute-done | bytes 262176 | tf_op jit(solution)/shard_map/ppermute | solution.py:246
  80.5 0.0 collective-permute-start.17
  80.5 5.1 %collective-permute-done.20.rest_2_ = bf16[4,128,256]{2,1,0:T(8,128)(2,1)S(1)} collective-permute-done((bf16[4,128,256]{2,1,0:T(8,128)(2,1)S(1)}, bf16[4,128,256]{2,1,0:T(8,128)(2,1)S(1)}, u32[]{:S(2)}, u32[]{:S(2)}) %collective-permute-start.20) | collective-permute-done | bytes 262176 | tf_op jit(solution)/shard_map/ppermute | solution.py:246
  85.7 0.2 collective-permute-start.18
  85.9 1.6 %unpack_0_0.1 = (bf16[128,4096]{1,0:T(8,128)(2,1)}, bf16[128,4096]{1,0:T(8,128)(2,1)}, bf16[128,4096]{1,0:T(8,128)(2,1)}, bf16[128,4096]{1,0:T(8,128)(2,1)}) custom-call(s32[1]{0:T(128)} %bitcast.me_ref, bf16[4,128,256]{2,1,0:T(8,128)(2,1)S(1)} %get-tuple-element.106.rest_0_, bf16[4,128,256]{2,1,0:T(8,128)(2,1)S(1)} %collective-permute-done.21.rest_1_, ...), custom_call_target="tpu_custom_call" | custom-call | tf_op jit(solution)/shard_map/unpack_0_0/pallas_call | solution.py:268
  87.5 1.0 unpack_1_0.1
  88.5 3.8 %collective-permute-done.14.rest_0_ = bf16[4,128,256]{2,1,0:T(8,128)(2,1)S(1)} collective-permute-done((bf16[4,128,256]{2,1,0:T(8,128)(2,1)S(1)}, bf16[4,128,256]{2,1,0:T(8,128)(2,1)S(1)}, u32[]{:S(2)}, u32[]{:S(2)}) %collective-permute-start.14) | collective-permute-done | bytes 262176 | tf_op jit(solution)/shard_map/ppermute | solution.py:246
  92.3 3.5 %collective-permute-done.16.rest_2_ = bf16[4,128,256]{2,1,0:T(8,128)(2,1)S(1)} collective-permute-done((bf16[4,128,256]{2,1,0:T(8,128)(2,1)S(1)}, bf16[4,128,256]{2,1,0:T(8,128)(2,1)S(1)}, u32[]{:S(2)}, u32[]{:S(2)}) %collective-permute-start.16) | collective-permute-done | bytes 262176 | tf_op jit(solution)/shard_map/ppermute | solution.py:246
  95.7 0.7 collective-permute-done.17.rest_3_
  96.4 1.2 %unpack_1_3.1 = (bf16[128,4096]{1,0:T(8,128)(2,1)}, bf16[128,4096]{1,0:T(8,128)(2,1)}, bf16[128,4096]{1,0:T(8,128)(2,1)}, bf16[128,4096]{1,0:T(8,128)(2,1)}) custom-call(s32[1]{0:T(128)} %bitcast.me_ref, bf16[4,128,256]{2,1,0:T(8,128)(2,1)S(1)} %collective-permute-done.14.rest_0_, ...), custom_call_target="tpu_custom_call", output_to_operand_aliasing={{0}: (6, {}), {1}: (7, {}), {2}: (8, {}), {3}: (9, {})} | custom-call | tf_op jit(solution)/shard_map/unpack_1_3/pallas_call | solution.py:268
  (23 shorter events, 0.1 us)
Async XLA Ops:
  1.8 16.3 %collective-permute-start.6 = (bf16[4,128,256]{2,1,0:T(8,128)(2,1)S(1)}, bf16[4,128,256]{2,1,0:T(8,128)(2,1)S(1)}, u32[]{:S(2)}, u32[]{:S(2)}) collective-permute-start(bf16[4,128,256]{2,1,0:T(8,128)(2,1)S(1)} %get-tuple-element.82), channel_id=1, source_target_pairs={{0,6},{1,7},{2,4},{3,5},{4,2},{5,3},{6,0},{7,1},{8,14},{9,15},{10,... | collective-permute-start | bytes 786440 | tf_op jit(solution)/shard_map/ppermute | solution.py:246
  5.7 13.0 %collective-permute-start.7 = (bf16[4,128,256]{2,1,0:T(8,128)(2,1)S(1)}, bf16[4,128,256]{2,1,0:T(8,128)(2,1)S(1)}, u32[]{:S(2)}, u32[]{:S(2)}) collective-permute-start(bf16[4,128,256]{2,1,0:T(8,128)(2,1)S(1)} %get-tuple-element.83), channel_id=1, source_target_pairs={{0,7},{1,6},{2,5},{3,4},{4,3},{5,2},{6,1},{7,0},{8,15},{9,14},{10,... | collective-permute-start | bytes 786440 | tf_op jit(solution)/shard_map/ppermute | solution.py:246
  5.7 6.1 %copy-start.5 = (s32[3,1024]{1,0:T(4,128)S(1)}, s32[3,1024]{1,0:T(4,128)}, u32[]{:S(2)}) copy-start(s32[3,1024]{1,0:T(4,128)} %param.13) | copy-start | bytes 36868
  8.5 16.2 %collective-permute-start.8 = (bf16[4,128,256]{2,1,0:T(8,128)(2,1)}, bf16[4,128,256]{2,1,0:T(8,128)(2,1)S(1)}, u32[]{:S(2)}, u32[]{:S(2)}) collective-permute-start(bf16[4,128,256]{2,1,0:T(8,128)(2,1)} %get-tuple-element.84), channel_id=1, source_target_pairs={{0,2},{1,3},{2,0},{3,1},{4,6},{5,7},{6,4},{7,5},{8,10},{9,11},{10,... | collective-permute-start | bytes 786440 | tf_op jit(solution)/shard_map/ppermute | solution.py:246
  9.7 16.4 %collective-permute-start.9 = (bf16[4,128,256]{2,1,0:T(8,128)(2,1)}, bf16[4,128,256]{2,1,0:T(8,128)(2,1)S(1)}, u32[]{:S(2)}, u32[]{:S(2)}) collective-permute-start(bf16[4,128,256]{2,1,0:T(8,128)(2,1)} %get-tuple-element.85), channel_id=1, source_target_pairs={{0,4},{1,5},{2,6},{3,7},{4,0},{5,1},{6,2},{7,3},{8,12},{9,13},{10,... | collective-permute-start | bytes 786440 | tf_op jit(solution)/shard_map/ppermute | solution.py:246
  11.2 18.2 %collective-permute-start.10 = (bf16[4,128,256]{2,1,0:T(8,128)(2,1)}, bf16[4,128,256]{2,1,0:T(8,128)(2,1)S(1)}, u32[]{:S(2)}, u32[]{:S(2)}) collective-permute-start(bf16[4,128,256]{2,1,0:T(8,128)(2,1)} %get-tuple-element.86), channel_id=1, source_target_pairs={{0,3},{1,2},{2,1},{3,0},{4,7},{5,6},{6,5},{7,4},{8,11},{9,10},{10,... | collective-permute-start | bytes 786440 | tf_op jit(solution)/shard_map/ppermute | solution.py:246
  14.8 4.0 %copy-start.7 = (bf16[4,128,256]{2,1,0:T(8,128)(2,1)S(1)}, bf16[4,128,256]{2,1,0:T(8,128)(2,1)}, u32[]{:S(2)}) copy-start(bf16[4,128,256]{2,1,0:T(8,128)(2,1)} %get-tuple-element.88) | copy-start | bytes 786436
  14.8 20.7 %copy-start.1 = (bf16[4,128,256]{2,1,0:T(8,128)(2,1)S(1)}, bf16[4,128,256]{2,1,0:T(8,128)(2,1)}, u32[]{:S(2)}) copy-start(bf16[4,128,256]{2,1,0:T(8,128)(2,1)} %get-tuple-element.81.rest_0_) | copy-start | bytes 786436
  18.1 17.4 %copy-start.3 = (s32[8,8]{1,0:T(8,128)S(1)}, s32[8,8]{1,0:T(8,128)}, u32[]{:S(2)}) copy-start(s32[8,8]{1,0:T(8,128)} %bands_ref.3) | copy-start | bytes 772
  18.1 17.4 %copy-start.2 = (s32[8,8]{1,0:T(8,128)S(1)}, s32[8,8]{1,0:T(8,128)}, u32[]{:S(2)}) copy-start(s32[8,8]{1,0:T(8,128)} %flags_ref.3) | copy-start | bytes 772
  18.1 11.9 %collective-permute-start.11 = (bf16[4,128,256]{2,1,0:T(8,128)(2,1)}, bf16[4,128,256]{2,1,0:T(8,128)(2,1)S(1)}, u32[]{:S(2)}, u32[]{:S(2)}) collective-permute-start(bf16[4,128,256]{2,1,0:T(8,128)(2,1)} %get-tuple-element.87), channel_id=1, source_target_pairs={{0,5},{1,4},{2,7},{3,6},{4,1},{5,0},{6,3},{7,2},{8,13},{9,12},{10,... | collective-permute-start | bytes 786440 | tf_op jit(solution)/shard_map/ppermute | solution.py:246
  18.8 16.8 %copy-start.4 = (s32[8]{0:T(128)S(1)}, s32[8]{0:T(128)}, u32[]{:S(2)}) copy-start(s32[8]{0:T(128)} %constant.57.clone.hops_ref) | copy-start | bytes 100
  18.8 12.9 %collective-permute-start.12 = (bf16[4,128,256]{2,1,0:T(8,128)(2,1)S(1)}, bf16[4,128,256]{2,1,0:T(8,128)(2,1)S(1)}, u32[]{:S(2)}, u32[]{:S(2)}) collective-permute-start(bf16[4,128,256]{2,1,0:T(8,128)(2,1)S(1)} %copy-done.7), channel_id=1, source_target_pairs={{0,1},{1,0},{2,3},{3,2},{4,5},{5,4},{6,7},{7,6},{8,9},{9,8},{10,11... | collective-permute-start | bytes 786440 | tf_op jit(solution)/shard_map/ppermute | solution.py:246
  24.7 10.8 %collective-permute-start = (bf16[4,128,256]{2,1,0:T(8,128)(2,1)}, bf16[4,128,256]{2,1,0:T(8,128)(2,1)S(1)}, u32[]{:S(2)}, u32[]{:S(2)}) collective-permute-start(bf16[4,128,256]{2,1,0:T(8,128)(2,1)} %get-tuple-element.74), channel_id=1, source_target_pairs={{0,6},{1,7},{2,4},{3,5},{4,2},{5,3},{6,0},{7,1},{8,14},{9,15},{10,... | collective-permute-start | bytes 786440 | tf_op jit(solution)/shard_map/ppermute | solution.py:246
  26.2 18.5 %collective-permute-start.1 = (bf16[4,128,256]{2,1,0:T(8,128)(2,1)}, bf16[4,128,256]{2,1,0:T(8,128)(2,1)S(1)}, u32[]{:S(2)}, u32[]{:S(2)}) collective-permute-start(bf16[4,128,256]{2,1,0:T(8,128)(2,1)} %get-tuple-element.75), channel_id=1, source_target_pairs={{0,7},{1,6},{2,5},{3,4},{4,3},{5,2},{6,1},{7,0},{8,15},{9,14},{10,... | collective-permute-start | bytes 786440 | tf_op jit(solution)/shard_map/ppermute | solution.py:246
  29.5 17.8 %collective-permute-start.2 = (bf16[4,128,256]{2,1,0:T(8,128)(2,1)}, bf16[4,128,256]{2,1,0:T(8,128)(2,1)S(1)}, u32[]{:S(2)}, u32[]{:S(2)}) collective-permute-start(bf16[4,128,256]{2,1,0:T(8,128)(2,1)} %get-tuple-element.76), channel_id=1, source_target_pairs={{0,2},{1,3},{2,0},{3,1},{4,6},{5,7},{6,4},{7,5},{8,10},{9,11},{10,... | collective-permute-start | bytes 786440 | tf_op jit(solution)/shard_map/ppermute | solution.py:246
  30.0 18.7 %collective-permute-start.3 = (bf16[4,128,256]{2,1,0:T(8,128)(2,1)}, bf16[4,128,256]{2,1,0:T(8,128)(2,1)S(1)}, u32[]{:S(2)}, u32[]{:S(2)}) collective-permute-start(bf16[4,128,256]{2,1,0:T(8,128)(2,1)} %get-tuple-element.77), channel_id=1, source_target_pairs={{0,4},{1,5},{2,6},{3,7},{4,0},{5,1},{6,2},{7,3},{8,12},{9,13},{10,... | collective-permute-start | bytes 786440 | tf_op jit(solution)/shard_map/ppermute | solution.py:246
  31.7 20.3 %collective-permute-start.4 = (bf16[4,128,256]{2,1,0:T(8,128)(2,1)}, bf16[4,128,256]{2,1,0:T(8,128)(2,1)S(1)}, u32[]{:S(2)}, u32[]{:S(2)}) collective-permute-start(bf16[4,128,256]{2,1,0:T(8,128)(2,1)} %get-tuple-element.78), channel_id=1, source_target_pairs={{0,3},{1,2},{2,1},{3,0},{4,7},{5,6},{6,5},{7,4},{8,11},{9,10},{10,... | collective-permute-start | bytes 786440 | tf_op jit(solution)/shard_map/ppermute | solution.py:246
  35.5 17.0 %collective-permute-start.5 = (bf16[4,128,256]{2,1,0:T(8,128)(2,1)}, bf16[4,128,256]{2,1,0:T(8,128)(2,1)S(1)}, u32[]{:S(2)}, u32[]{:S(2)}) collective-permute-start(bf16[4,128,256]{2,1,0:T(8,128)(2,1)} %get-tuple-element.79), channel_id=1, source_target_pairs={{0,5},{1,4},{2,7},{3,6},{4,1},{5,0},{6,3},{7,2},{8,13},{9,12},{10,... | collective-permute-start | bytes 786440 | tf_op jit(solution)/shard_map/ppermute | solution.py:246
  35.5 9.1 %copy-start.6 = (bf16[4,128,256]{2,1,0:T(8,128)(2,1)S(1)}, bf16[4,128,256]{2,1,0:T(8,128)(2,1)}, u32[]{:S(2)}) copy-start(bf16[4,128,256]{2,1,0:T(8,128)(2,1)} %get-tuple-element.97) | copy-start | bytes 786436
  35.5 19.5 %copy-start = (bf16[4,128,256]{2,1,0:T(8,128)(2,1)S(1)}, bf16[4,128,256]{2,1,0:T(8,128)(2,1)}, u32[]{:S(2)}) copy-start(bf16[4,128,256]{2,1,0:T(8,128)(2,1)} %get-tuple-element.73.rest_0_) | copy-start | bytes 786436
  44.7 9.5 %collective-permute-start.13 = (bf16[4,128,256]{2,1,0:T(8,128)(2,1)S(1)}, bf16[4,128,256]{2,1,0:T(8,128)(2,1)S(1)}, u32[]{:S(2)}, u32[]{:S(2)}) collective-permute-start(bf16[4,128,256]{2,1,0:T(8,128)(2,1)S(1)} %copy-done.6), channel_id=1, source_target_pairs={{0,1},{1,0},{2,3},{3,2},{4,5},{5,4},{6,7},{7,6},{8,9},{9,8},{10,11... | collective-permute-start | bytes 786440 | tf_op jit(solution)/shard_map/ppermute | solution.py:246
  47.2 17.1 %collective-permute-start.21 = (bf16[4,128,256]{2,1,0:T(8,128)(2,1)S(1)}, bf16[4,128,256]{2,1,0:T(8,128)(2,1)S(1)}, u32[]{:S(2)}, u32[]{:S(2)}) collective-permute-start(bf16[4,128,256]{2,1,0:T(8,128)(2,1)S(1)} %get-tuple-element.107), channel_id=1, source_target_pairs={{0,6},{1,7},{2,4},{3,5},{4,2},{5,3},{6,0},{7,1},{8,14},{9,15},{10,... | collective-permute-start | bytes 786440 | tf_op jit(solution)/shard_map/ppermute | solution.py:246
  48.7 16.6 %collective-permute-start.22 = (bf16[4,128,256]{2,1,0:T(8,128)(2,1)S(1)}, bf16[4,128,256]{2,1,0:T(8,128)(2,1)S(1)}, u32[]{:S(2)}, u32[]{:S(2)}) collective-permute-start(bf16[4,128,256]{2,1,0:T(8,128)(2,1)S(1)} %get-tuple-element.108), channel_id=1, source_target_pairs={{0,7},{1,6},{2,5},{3,4},{4,3},{5,2},{6,1},{7,0},{8,15},{9,14},{10,... | collective-permute-start | bytes 786440 | tf_op jit(solution)/shard_map/ppermute | solution.py:246
  52.0 17.8 %collective-permute-start.23 = (bf16[4,128,256]{2,1,0:T(8,128)(2,1)S(1)}, bf16[4,128,256]{2,1,0:T(8,128)(2,1)S(1)}, u32[]{:S(2)}, u32[]{:S(2)}) collective-permute-start(bf16[4,128,256]{2,1,0:T(8,128)(2,1)S(1)} %get-tuple-element.109), channel_id=1, source_target_pairs={{0,2},{1,3},{2,0},{3,1},{4,6},{5,7},{6,4},{7,5},{8,10},{9,11},{10,... | collective-permute-start | bytes 786440 | tf_op jit(solution)/shard_map/ppermute | solution.py:246
  52.5 18.7 %collective-permute-start.24 = (bf16[4,128,256]{2,1,0:T(8,128)(2,1)S(1)}, bf16[4,128,256]{2,1,0:T(8,128)(2,1)S(1)}, u32[]{:S(2)}, u32[]{:S(2)}) collective-permute-start(bf16[4,128,256]{2,1,0:T(8,128)(2,1)S(1)} %get-tuple-element.110), channel_id=1, source_target_pairs={{0,4},{1,5},{2,6},{3,7},{4,0},{5,1},{6,2},{7,3},{8,12},{9,13},{10,... | collective-permute-start | bytes 786440 | tf_op jit(solution)/shard_map/ppermute | solution.py:246
  54.1 20.2 %collective-permute-start.25 = (bf16[4,128,256]{2,1,0:T(8,128)(2,1)S(1)}, bf16[4,128,256]{2,1,0:T(8,128)(2,1)S(1)}, u32[]{:S(2)}, u32[]{:S(2)}) collective-permute-start(bf16[4,128,256]{2,1,0:T(8,128)(2,1)S(1)} %get-tuple-element.111), channel_id=1, source_target_pairs={{0,3},{1,2},{2,1},{3,0},{4,7},{5,6},{6,5},{7,4},{8,11},{9,10},{10,... | collective-permute-start | bytes 786440 | tf_op jit(solution)/shard_map/ppermute | solution.py:246
  64.3 10.6 %collective-permute-start.26 = (bf16[4,128,256]{2,1,0:T(8,128)(2,1)S(1)}, bf16[4,128,256]{2,1,0:T(8,128)(2,1)S(1)}, u32[]{:S(2)}, u32[]{:S(2)}) collective-permute-start(bf16[4,128,256]{2,1,0:T(8,128)(2,1)S(1)} %get-tuple-element.112), channel_id=1, source_target_pairs={{0,5},{1,4},{2,7},{3,6},{4,1},{5,0},{6,3},{7,2},{8,13},{9,12},{10,... | collective-permute-start | bytes 786440 | tf_op jit(solution)/shard_map/ppermute | solution.py:246
  65.3 11.4 %collective-permute-start.27 = (bf16[4,128,256]{2,1,0:T(8,128)(2,1)S(1)}, bf16[4,128,256]{2,1,0:T(8,128)(2,1)S(1)}, u32[]{:S(2)}, u32[]{:S(2)}) collective-permute-start(bf16[4,128,256]{2,1,0:T(8,128)(2,1)S(1)} %get-tuple-element.113), channel_id=1, source_target_pairs={{0,1},{1,0},{2,3},{3,2},{4,5},{5,4},{6,7},{7,6},{8,9},{9,8},{10,11... | collective-permute-start | bytes 786440 | tf_op jit(solution)/shard_map/ppermute | solution.py:246
  69.8 10.8 %collective-permute-start.19 = (bf16[4,128,256]{2,1,0:T(8,128)(2,1)S(1)}, bf16[4,128,256]{2,1,0:T(8,128)(2,1)S(1)}, u32[]{:S(2)}, u32[]{:S(2)}) collective-permute-start(bf16[4,128,256]{2,1,0:T(8,128)(2,1)S(1)} %get-tuple-element.104), channel_id=1, source_target_pairs={{0,6},{1,7},{2,4},{3,5},{4,2},{5,3},{6,0},{7,1},{8,14},{9,15},{10,... | collective-permute-start | bytes 786440 | tf_op jit(solution)/shard_map/ppermute | solution.py:246
  71.2 14.5 %collective-permute-start.20 = (bf16[4,128,256]{2,1,0:T(8,128)(2,1)S(1)}, bf16[4,128,256]{2,1,0:T(8,128)(2,1)S(1)}, u32[]{:S(2)}, u32[]{:S(2)}) collective-permute-start(bf16[4,128,256]{2,1,0:T(8,128)(2,1)S(1)} %get-tuple-element.105), channel_id=1, source_target_pairs={{0,7},{1,6},{2,5},{3,4},{4,3},{5,2},{6,1},{7,0},{8,15},{9,14},{10,... | collective-permute-start | bytes 786440 | tf_op jit(solution)/shard_map/ppermute | solution.py:246
  74.4 17.9 %collective-permute-start.14 = (bf16[4,128,256]{2,1,0:T(8,128)(2,1)S(1)}, bf16[4,128,256]{2,1,0:T(8,128)(2,1)S(1)}, u32[]{:S(2)}, u32[]{:S(2)}) collective-permute-start(bf16[4,128,256]{2,1,0:T(8,128)(2,1)S(1)} %get-tuple-element.98), channel_id=1, source_target_pairs={{0,2},{1,3},{2,0},{3,1},{4,6},{5,7},{6,4},{7,5},{8,10},{9,11},{10,... | collective-permute-start | bytes 786440 | tf_op jit(solution)/shard_map/ppermute | solution.py:246
  74.9 17.4 %collective-permute-start.15 = (bf16[4,128,256]{2,1,0:T(8,128)(2,1)S(1)}, bf16[4,128,256]{2,1,0:T(8,128)(2,1)S(1)}, u32[]{:S(2)}, u32[]{:S(2)}) collective-permute-start(bf16[4,128,256]{2,1,0:T(8,128)(2,1)S(1)} %get-tuple-element.99), channel_id=1, source_target_pairs={{0,4},{1,5},{2,6},{3,7},{4,0},{5,1},{6,2},{7,3},{8,12},{9,13},{10,... | collective-permute-start | bytes 786440 | tf_op jit(solution)/shard_map/ppermute | solution.py:246
  76.7 19.1 %collective-permute-start.16 = (bf16[4,128,256]{2,1,0:T(8,128)(2,1)S(1)}, bf16[4,128,256]{2,1,0:T(8,128)(2,1)S(1)}, u32[]{:S(2)}, u32[]{:S(2)}) collective-permute-start(bf16[4,128,256]{2,1,0:T(8,128)(2,1)S(1)} %get-tuple-element.100), channel_id=1, source_target_pairs={{0,3},{1,2},{2,1},{3,0},{4,7},{5,6},{6,5},{7,4},{8,11},{9,10},{10,... | collective-permute-start | bytes 786440 | tf_op jit(solution)/shard_map/ppermute | solution.py:246
  80.5 15.9 %collective-permute-start.17 = (bf16[4,128,256]{2,1,0:T(8,128)(2,1)S(1)}, bf16[4,128,256]{2,1,0:T(8,128)(2,1)S(1)}, u32[]{:S(2)}, u32[]{:S(2)}) collective-permute-start(bf16[4,128,256]{2,1,0:T(8,128)(2,1)S(1)} %get-tuple-element.101), channel_id=1, source_target_pairs={{0,5},{1,4},{2,7},{3,6},{4,1},{5,0},{6,3},{7,2},{8,13},{9,12},{10,... | collective-permute-start | bytes 786440 | tf_op jit(solution)/shard_map/ppermute | solution.py:246
  85.7 10.8 %collective-permute-start.18 = (bf16[4,128,256]{2,1,0:T(8,128)(2,1)S(1)}, bf16[4,128,256]{2,1,0:T(8,128)(2,1)S(1)}, u32[]{:S(2)}, u32[]{:S(2)}) collective-permute-start(bf16[4,128,256]{2,1,0:T(8,128)(2,1)S(1)} %get-tuple-element.102), channel_id=1, source_target_pairs={{0,1},{1,0},{2,3},{3,2},{4,5},{5,4},{6,7},{7,6},{8,9},{9,8},{10,11... | collective-permute-start | bytes 786440 | tf_op jit(solution)/shard_map/ppermute | solution.py:246
